TPU v7x, 32 devices: a whole 2x2x4 slice. The times are simulated.
32 devices in a mesh: group: 4 (over y, x), fsdp: 8 (over z, core).
Axes of the slice: x: 2, y: 2, z: 4, core: 2. Of those that a mesh axis runs over, the one named last changes fastest.
Arguments:
- hidden_input_slots: bfloat16 [256, 8192], P('group'), may hold values from -6 to 6
- base_weight: bfloat16 [8192, 14784], P('group', 'fsdp'), may hold values from -0.0625 to 0.0625
- adapter_a: bfloat16 [8192, 64], P('group'), may hold values from -0.0625 to 0.0625
- adapter_up_matrix: bfloat16 [64, 14784], P(None, 'fsdp'), may hold values from -0.75 to 0.75
- upstream: bfloat16 [256, 14784], P('group', 'fsdp'), may hold values from -6 to 6
- logp_new: float32 [4, 4, 16], P('group'), may hold values from -2 to -0.5
- logp_old: float32 [4, 4, 16], P('group'), may hold values from -2 to -0.5
- rewards: float32 [4, 4], P('group'), may hold values from -1.35 to 2.35
- comp_lengths: int32 [4, 4], P('group'), may hold values from 1 to 16, 40 in all within a row
- assignment: int32 [4, 4], P('group'), may hold values from 0 to 3, each once within a row
Outputs:
- projection_output: bfloat16 [256, 14784], P('group', 'fsdp')
- gradient_down_adapter: float32 [8192, 64], P('group')
- gradient_up_adapter: float32 [64, 14784], P('group', 'fsdp')
- loss_parts: float32 [4], P('group')
Inputs may be any that keep to these rules, and one draw needn't show every extreme that they name: `comp_lengths`: every generator group has a completion of exactly 16 tokens. `assignment`: each generator group assigns exactly one completion to each trainer group.
All inputs are finite; a program needn't handle non-finite values.
Results may differ from a plain program's by a relative error of at most 0.0049.
Values may be sent and summed in bfloat16 or wider, within the bound.
No kernel may reach another device: no remote copies, remote signals or barrier semaphores. Data moves between devices by JAX's collectives and lax.ppermute only.
A program may use at most 128 MiB of HBM per device.

v0:
```python
import jax
import jax.numpy as jnp
from jax import lax
from jax.sharding import PartitionSpec as P

COMP = 16


ADAPTER_SCALING = 0.25
SPREAD_FLOOR = 0.16


def prompt_table(prompt_row, count):
    return (prompt_row[:, None] == jnp.arange(count, dtype=jnp.int32)[None, :]).astype(jnp.float32)


def advantages(reward_row, onehot, reward_sums, reward_squares):
    reward_mean = reward_sums / COMP
    reward_var = reward_squares / COMP - reward_mean * reward_mean
    spread = jnp.sqrt(jnp.maximum(reward_var, SPREAD_FLOOR))
    centre = jnp.dot(onehot, reward_mean, precision=lax.Precision.HIGHEST)
    scaled = jnp.dot(onehot, spread, precision=lax.Precision.HIGHEST)
    return (reward_row - centre) / scaled


def prompt_sums(reward_row, onehot):
    reward_sums = jnp.dot(reward_row, onehot, precision=lax.Precision.HIGHEST)
    reward_squares = jnp.dot(reward_row * reward_row, onehot, precision=lax.Precision.HIGHEST)
    return (reward_sums, reward_squares)


def add_rows(hidden_input_slots, weight_piece):
    return jnp.dot(hidden_input_slots, weight_piece, preferred_element_type=jnp.float32)


def on_device(
    hidden_input_slots,
    base_weight,
    adapter_a,
    adapter_up_matrix,
    upstream,
    logp_new,
    logp_old,
    rewards,
    comp_lengths,
    assignment,
):
    groups = lax.axis_size("group")
    prompts = groups * groups // COMP
    own_group = lax.axis_index("group")
    prompt_row = (own_group * groups + jnp.arange(groups, dtype=jnp.int32)) // COMP
    dest_order = (assignment[0][None, :] == jnp.arange(groups, dtype=jnp.int32)[:, None]).astype(
        jnp.float32
    )
    send_old = jnp.dot(dest_order, logp_old[0], precision=lax.Precision.HIGHEST)
    send_len = jnp.dot(
        dest_order, comp_lengths[0].astype(jnp.float32), precision=lax.Precision.HIGHEST
    )
    reward_row = rewards[0]
    onehot = prompt_table(prompt_row, prompts)
    reward_sums, reward_squares = lax.psum(prompt_sums(reward_row, onehot), "group")
    advantage = advantages(reward_row, onehot, reward_sums, reward_squares)
    send_adv = jnp.dot(dest_order, advantage, precision=lax.Precision.HIGHEST)
    recv_old, recv_adv, recv_len = (
        lax.all_to_all(send_old, "group", split_axis=0, concat_axis=0, tiled=True),
        lax.all_to_all(send_adv, "group", split_axis=0, concat_axis=0, tiled=True),
        lax.all_to_all(send_len, "group", split_axis=0, concat_axis=0, tiled=True),
    )
    positions = jnp.arange(logp_new.shape[2]).astype(jnp.float32)
    live_mask = positions[None, :] < recv_len[:, None]
    prob_ratio = jnp.exp(logp_new[0] - recv_old)
    token_coef = jnp.where(
        live_mask, -(recv_adv[:, None] * prob_ratio) / (recv_len[:, None] * COMP), 0.0
    )
    loss_part = jnp.sum(token_coef)[None]
    output_gradient = (token_coef.reshape(-1, 1) * upstream.astype(jnp.float32)).astype(
        jnp.bfloat16
    )
    full_adapter = lax.all_gather(adapter_a, "group", axis=0, tiled=True)
    low_sum = jnp.dot(hidden_input_slots, full_adapter, preferred_element_type=jnp.float32)
    frozen_base_total = add_rows(
        hidden_input_slots, lax.all_gather(base_weight, "group", axis=0, tiled=True)
    )
    reduced_rank_product = low_sum.astype(jnp.bfloat16)
    projection_output = (
        frozen_base_total
        + ADAPTER_SCALING
        * jnp.dot(reduced_rank_product, adapter_up_matrix, preferred_element_type=jnp.float32)
    ).astype(jnp.bfloat16)
    gradient_up_partial = ADAPTER_SCALING * lax.dot_general(
        reduced_rank_product,
        output_gradient,
        (((0,), (0,)), ((), ())),
        preferred_element_type=jnp.float32,
    )
    back_part = lax.dot_general(
        output_gradient,
        adapter_up_matrix,
        (((1,), (1,)), ((), ())),
        preferred_element_type=jnp.float32,
    )
    backward_lowrank = lax.psum(back_part, "fsdp").astype(jnp.bfloat16)
    gradient_down_partial = ADAPTER_SCALING * lax.dot_general(
        hidden_input_slots,
        backward_lowrank,
        (((0,), (0,)), ((), ())),
        preferred_element_type=jnp.float32,
    )
    gradient_down_adapter, gradient_up_adapter = (
        lax.psum_scatter(gradient_down_partial, "group", scatter_dimension=0, tiled=True),
        lax.psum_scatter(gradient_up_partial, "group", scatter_dimension=0, tiled=True),
    )
    return (projection_output, gradient_down_adapter, gradient_up_adapter, loss_part)


def solution(mesh):
    return jax.shard_map(
        on_device,
        mesh=mesh,
        in_specs=(
            P("group", None),
            P("group", "fsdp"),
            P("group", None),
            P(None, "fsdp"),
            P("group", "fsdp"),
            P("group", None, None),
            P("group", None, None),
            P("group", None),
            P("group", None),
            P("group", None),
        ),
        out_specs=(P("group", "fsdp"), P("group", None), P("group", "fsdp"), P("group")),
        check_vma=False,
    )
```

profile of v0, /device:TPU:0, one launch (start us, length us, event | category | flops | bytes accessed | tf_op | source)
XLA Modules:
  0.0 417.1 jit_solution(3950661539554782485)
XLA Ops:
  7.2 0.7 all-gather.5.cloned.1.call-update
  7.9 1.4 fusion.11
  9.3 5.2 %all-to-all-start = ((f32[4,1,1]{2,1,0:T(1,128)}), f32[4,1,1]{2,1,0:T(1,128)S(1)}, u32[]{:S(2)}, u32[]{:S(2)}) async-start(f32[4,1,1]{2,1,0:T(1,128)} %bitcast.24), calls=%async_computation | async-start | bytes 4096 | tf_op jit(solution)/shard_map/all_to_all | solution.py:67
  14.5 1.3 select_reduce_fusion.1
  15.8 11.1 %all-reduce.1 = (f32[1]{0:T(128)}, f32[1]{0:T(128)}) all-reduce(f32[1]{0:T(128)} %bitcast.8, f32[1]{0:T(128)} %bitcast.6), channel_id=1, replica_groups=mesh['group'=4,'fsdp'=8] {'group'}, use_global_device_ids=true, to_apply=%region_1.2 | all-reduce | flops 2 | bytes 16 | tf_op jit(solution)/shard_map/psum | solution.py:61
  29.5 0.8 squeeze.13
  30.3 1.4 fusion.10
  31.7 1.4 fusion.8
  33.1 3.2 all-to-all-start.1
  36.6 4.3 %all-to-all-done.1 = f32[4,1,1]{2,1,0:T(1,128)S(1)} async-done(((f32[4,1,1]{2,1,0:T(1,128)}), f32[4,1,1]{2,1,0:T(1,128)S(1)}, u32[]{:S(2)}, u32[]{:S(2)}) %all-to-all-start.1) | async-done | bytes 48 | tf_op jit(solution)/shard_map/all_to_all | solution.py:66
  40.9 3.2 all-to-all-start.2
  44.4 4.2 %all-to-all-done.2 = f32[4,1,16]{2,1,0:T(1,128)S(1)} async-done(((f32[4,1,16]{2,1,0:T(1,128)}), f32[4,1,16]{2,1,0:T(1,128)S(1)}, u32[]{:S(2)}, u32[]{:S(2)}) %all-to-all-start.2) | async-done | bytes 288 | tf_op jit(solution)/shard_map/all_to_all | solution.py:65
  48.6 1.4 fusion.12
  51.4 1.6 convolution_convert_fusion
  53.0 2.0 convolution_multiply_fusion.1
  55.1 0.7 all-gather.3.cloned.1.call-update
  56.2 26.0 %psum.23 = bf16[64,64]{1,0:T(8,128)(2,1)S(1)} all-reduce(f32[64,64]{1,0:T(8,128)S(1)} %fusion.3), channel_id=1, replica_groups=mesh['group'=4,'fsdp'=8] {'fsdp'}, use_global_device_ids=true, to_apply=%region_2.3 | all-reduce | flops 4096 | bytes 24576 | tf_op jit(solution)/shard_map/psum | solution.py:102
  82.2 1.8 fusion
  85.2 14.5 %all-reduce.4.cloned.1.call-done = f32[64,1848]{1,0:T(8,128)} async-done(((f32[64,1848]{1,0:T(8,128)}), f32[64,1848]{1,0:T(8,128)}) %all-reduce.4.cloned.1.call-update) | async-done | bytes 473104
  99.7 1.6 constant_dynamic-slice_fusion
  101.2 270.4 %all-gather.3.cloned.1.call-done = bf16[8192,1848]{0,1:T(8,128)(2,1)} async-done(((bf16[2048,1848]{0,1:T(8,128)(2,1)}), bf16[8192,1848]{0,1:T(8,128)(2,1)}) %all-gather.3.cloned.1.call-update) | async-done | bytes 30277648 | tf_op jit(solution)/shard_map/all_gather | solution.py:82
  371.7 14.7 %fusion.34 = f32[64,1848]{1,0:T(8,128)S(1)} fusion(bf16[64,8192]{1,0:T(8,128)(2,1)S(1)} %copy-done, bf16[8192,1848]{0,1:T(8,128)(2,1)} %all-gather.3.cloned.1.call-done), kind=kOutput, calls=%fused_computation.53 | convolution fusion | flops 1937768448 | bytes 31799296 | tf_op jit(solution)/shard_map/dot_general | solution.py:33
  386.4 0.9 fusion.2
  387.3 23.3 %reduce-scatter.2.cloned.1.call-done = f32[2048,64]{0,1:T(8,128)} async-done(((f32[8192,64]{0,1:T(8,128)}), f32[2048,64]{0,1:T(8,128)}) %reduce-scatter.2.cloned.1.call-update) | async-done | bytes 524304 | tf_op jit(solution)/shard_map/reduce_scatter | solution.py:110
  (31 shorter events, 3.0 us)
Async XLA Ops:
  7.2 44.2 %copy-start = (bf16[64,8192]{1,0:T(8,128)(2,1)S(1)}, bf16[64,8192]{1,0:T(8,128)(2,1)}, u32[]{:S(2)}) copy-start(bf16[64,8192]{1,0:T(8,128)(2,1)} %param.10) | copy-start | bytes 3145732
  7.2 48.7 %copy-start.1 = (bf16[64,1848]{1,0:T(8,128)(2,1)S(1)}, bf16[64,1848]{1,0:T(8,128)(2,1)}, u32[]{:S(2)}) copy-start(bf16[64,1848]{1,0:T(8,128)(2,1)} %param.14) | copy-start | bytes 709636
  7.2 48.7 %copy-start.2 = (bf16[64,1848]{1,0:T(8,128)(2,1)S(1)}, bf16[64,1848]{1,0:T(8,128)(2,1)}, u32[]{:S(2)}) copy-start(bf16[64,1848]{1,0:T(8,128)(2,1)} %param.13) | copy-start | bytes 709636
  7.2 44.2 %all-gather.5.cloned.1.call-start = ((), (), s32[]{:S(2)}) async-start(), calls=%async_computation.5 | async-start | bytes 1310720 | tf_op jit(solution)/shard_map/all_gather | solution.py:79
  9.3 23.8 %all-to-all-start = ((f32[4,1,1]{2,1,0:T(1,128)}), f32[4,1,1]{2,1,0:T(1,128)S(1)}, u32[]{:S(2)}, u32[]{:S(2)}) async-start(f32[4,1,1]{2,1,0:T(1,128)} %bitcast.24), calls=%async_computation | async-start | bytes 4096 | tf_op jit(solution)/shard_map/all_to_all | solution.py:67
  33.1 7.8 %all-to-all-start.1 = ((f32[4,1,1]{2,1,0:T(1,128)}), f32[4,1,1]{2,1,0:T(1,128)S(1)}, u32[]{:S(2)}, u32[]{:S(2)}) async-start(f32[4,1,1]{2,1,0:T(1,128)} %bitcast.25), calls=%async_computation.1 | async-start | bytes 4096 | tf_op jit(solution)/shard_map/all_to_all | solution.py:66
  40.9 7.8 %all-to-all-start.2 = ((f32[4,1,16]{2,1,0:T(1,128)}), f32[4,1,16]{2,1,0:T(1,128)S(1)}, u32[]{:S(2)}, u32[]{:S(2)}) async-start(f32[4,1,16]{2,1,0:T(1,128)} %bitcast.15), calls=%async_computation.2 | async-start | bytes 4096 | tf_op jit(solution)/shard_map/all_to_all | solution.py:65
  44.1 55.6 %all-reduce.4.cloned.1.call-start = ((), (), s32[]{:S(2)}) async-start(), calls=%async_computation.7 | async-start | bytes 983040
  53.0 30.9 %copy-start.3 = (u32[32]{0:T(128)S(1)}, u32[32]{0:T(128)}, u32[]{:S(2)}) copy-start(u32[32]{0:T(128)} %constant.51) | copy-start | bytes 388
  55.1 316.6 %all-gather.3.cloned.1.call-start = ((), (), s32[]{:S(2)}) async-start(), calls=%async_computation.4 | async-start | bytes 37847040 | tf_op jit(solution)/shard_map/all_gather | solution.py:82
  55.8 354.7 %reduce-scatter.2.cloned.1.call-start = ((), (), s32[]{:S(2)}) async-start(), calls=%async_computation.6 | async-start | bytes 2621440 | tf_op jit(solution)/shard_map/reduce_scatter | solution.py:110
Sparse Core Ops, SparseCore 0:
  9.9 29.3 all-gather.4
  55.2 44.4 all-reduce.3
  101.7 269.9 all-gather.2
  375.3 35.1 reduce-scatter.1
where the time goes:
time: 418 us; the launch traced here: 417 us
  waiting for transfers between devices  318 us (76%)
  blocking collectives  37.1 us (9%)
  matrix products  25.5 us (6%)
  between operations  17.2 us (4%)
  starting transfers between devices  11.8 us (3%)
    all_gather x1, waiting for transfers between devices, on_device(): lax.all_gather(base_weight, 'group', axis=0, tiled=True)  270 us
    psum x1, blocking collectives, on_device(): backward_lowrank = lax.psum(back_part, 'fsdp').astype(jnp.bfloat16)  26 us
    reduce_scatter x1, waiting for transfers between devices, on_device(): lax.psum_scatter(gradient_down_partial, 'group', scatter_dimension=0, til...  23.3 us
    unnamed x5, waiting for transfers between devices  15.9 us
    dot_general x1, matrix products, add_rows(): jnp.dot(hidden_input_slots, weight_piece, preferred_element_type=jnp.floa...  14.7 us
    psum x1, blocking collectives, on_device(): lax.psum(prompt_sums(reward_row, onehot), 'group')  11.1 us
  transfers between devices with their start and end apart: 7, of which 5 were waited for; matrix products, arithmetic and copies ran while one was open for 7% of the time, Pallas kernels for 0%

commit v1 on v0

v1 whole, which is shorter than its diff:
```python
import jax
import jax.numpy as jnp
from jax import lax
from jax.sharding import PartitionSpec as P

COMP = 16


ADAPTER_SCALING = 0.25
SPREAD_FLOOR = 0.16
F32 = jnp.float32
BF16 = jnp.bfloat16


def swap(array, axis, distance):
    size = lax.axis_size(axis)
    return lax.ppermute(array, axis, [(i, i ^ distance) for i in range(size)])


def is_power(number):
    return number & (number - 1) == 0


def sum_over_pairs(partial):
    size = lax.axis_size("fsdp")
    if not is_power(size):
        return lax.psum(partial, "fsdp", axis_index_groups=[[i for i in range(size) if i % 2 == r] for r in range(2)])
    parts = [partial] + [swap(partial, "fsdp", d) for d in range(2, size, 2)]
    while len(parts) > 1:
        parts = [parts[i] + parts[i + 1] for i in range(0, len(parts), 2)]
    return parts[0]


def coefficients(table, logp_new, own_group):
    groups = logp_new.shape[0]
    length = logp_new.shape[1]
    prompts = max(groups * groups // COMP, 1)
    order = own_group ^ jnp.arange(groups, dtype=jnp.int32)
    pick = (order[:, None] == jnp.arange(groups, dtype=jnp.int32)[None, :]).astype(F32)
    rows = jnp.sum(jnp.where(pick[:, :, None, None] > 0, table[None], 0.0), axis=1)
    rewards = rows[:, :, length]
    flat = (jnp.arange(groups * groups, dtype=jnp.int32) // COMP).reshape(groups, groups)
    onehot = flat[:, :, None] == jnp.arange(prompts, dtype=jnp.int32)
    sums = jnp.sum(jnp.where(onehot, rewards[:, :, None], 0.0), axis=(0, 1))
    squares = jnp.sum(jnp.where(onehot, (rewards * rewards)[:, :, None], 0.0), axis=(0, 1))
    mean = sums / COMP
    spread = jnp.sqrt(jnp.maximum(squares / COMP - mean * mean, SPREAD_FLOOR))
    centre = jnp.sum(jnp.where(onehot, mean, 0.0), axis=-1)
    scaled = jnp.sum(jnp.where(onehot, spread, 0.0), axis=-1)
    advantage = (rewards - centre) / scaled
    mine = rows[:, :, length + 2] == own_group.astype(F32)
    recv_old = jnp.sum(jnp.where(mine[:, :, None], rows[:, :, :length], 0.0), axis=1)
    recv_adv = jnp.sum(jnp.where(mine, advantage, 0.0), axis=1)
    recv_len = jnp.sum(jnp.where(mine, rows[:, :, length + 1], 0.0), axis=1)
    positions = jnp.arange(length).astype(F32)
    live_mask = positions[None, :] < recv_len[:, None]
    prob_ratio = jnp.exp(logp_new - recv_old)
    return jnp.where(live_mask, -(recv_adv[:, None] * prob_ratio) / (recv_len[:, None] * COMP), 0.0)


def dot(a, b, dims=((1,), (0,))):
    return lax.dot_general(a, b, (dims, ((), ())), preferred_element_type=F32)


def on_device(
    hidden_input_slots,
    base_weight,
    adapter_a,
    adapter_up_matrix,
    upstream,
    logp_new,
    logp_old,
    rewards,
    comp_lengths,
    assignment,
):
    groups = lax.axis_size("group")
    own_group = lax.axis_index("group")
    core = lax.axis_index("fsdp") % 2
    depth = base_weight.shape[0]
    half = depth // 2
    rank = adapter_a.shape[1]
    others = range(1, groups)

    pieces = {
        d: lax.dynamic_slice_in_dim(hidden_input_slots, (own_group ^ d) * depth + core * half, half, 1)
        for d in others
    }
    got = {d: swap(pieces[d], "group", d) for d in others}
    small = jnp.concatenate(
        [
            logp_old[0],
            rewards[0][:, None],
            comp_lengths[0].astype(F32)[:, None],
            assignment[0].astype(F32)[:, None],
        ],
        axis=1,
    )
    table = jnp.stack([small] + [swap(small, "group", d) for d in others])
    token_coef = coefficients(table, logp_new[0], own_group)
    loss_part = jnp.sum(token_coef)[None]
    coef = token_coef.reshape(-1, 1)

    back = dot(upstream, adapter_up_matrix, ((1,), (1,)))
    back = sum_over_pairs(back)
    back = back + swap(back, "fsdp", 1)

    own_hidden = lax.dynamic_slice_in_dim(hidden_input_slots, own_group * depth, depth, 1)
    full = {0: own_hidden}
    theirs = swap(jnp.concatenate([got[d] for d in others], axis=0), "fsdp", 1)
    rows = own_hidden.shape[0]
    for d in others:
        a, b = got[d], theirs[(d - 1) * rows : d * rows]
        first = core == 0
        full[d] = jnp.concatenate([jnp.where(first, a, b), jnp.where(first, b, a)], axis=1)

    scaled_back = coef * back
    low_terms = {d: dot(full[d], adapter_a) for d in range(groups)}
    low = low_terms[0]
    backs = {0: scaled_back}
    for d in others:
        came = swap(jnp.concatenate([low_terms[d], scaled_back], axis=1), "group", d)
        low = low + came[:, :rank]
        backs[d] = came[:, rank:]
    low = low.astype(BF16)

    output = dot(full[0], base_weight) + ADAPTER_SCALING * dot(low, adapter_up_matrix)
    for d in others:
        output = output + swap(dot(full[d], base_weight).astype(BF16), "group", d).astype(F32)
    projection_output = output.astype(BF16)

    hidden_all = jnp.concatenate([full[d] for d in range(groups)], axis=0)
    back_all = jnp.concatenate([backs[d] for d in range(groups)], axis=0).astype(BF16)
    gradient_down = ADAPTER_SCALING * dot(hidden_all, back_all, ((0,), (0,)))

    output_gradient = (coef * upstream.astype(F32)).astype(BF16)
    up_term = ADAPTER_SCALING * dot(low, output_gradient, ((0,), (0,)))
    share = rank // groups
    gradient_up = lax.dynamic_slice_in_dim(up_term, own_group * share, share, 0)
    for d in others:
        term = lax.dynamic_slice_in_dim(up_term, (own_group ^ d) * share, share, 0).astype(BF16)
        gradient_up = gradient_up + swap(term, "group", d).astype(F32)
    return (projection_output, gradient_down, gradient_up, loss_part)


def solution(mesh):
    return jax.shard_map(
        on_device,
        mesh=mesh,
        in_specs=(
            P("group", None),
            P("group", "fsdp"),
            P("group", None),
            P(None, "fsdp"),
            P("group", "fsdp"),
            P("group", None, None),
            P("group", None, None),
            P("group", None),
            P("group", None),
            P("group", None),
        ),
        out_specs=(P("group", "fsdp"), P("group", None), P("group", "fsdp"), P("group")),
        check_vma=False,
    )
```

time: 418 us -> 72.7 us (0.17)
  waiting for transfers between devices: 318 us -> 9.74 us
  blocking collectives: 37.1 us -> 0 us
  between operations: 17.2 us -> 3.54 us
  starting transfers between devices: 11.8 us -> 24.6 us
    all_gather x2 -> x0, waiting for transfers between devices: 270 us -> none  [the longest x1 270 us: on_device(): lax.all_gather(base_weight, 'group', axis=0, tiled=True)]
    psum x2 -> x0, blocking collectives: 37.1 us -> none  [the longest x1 26 us: on_device(): backward_lowrank = lax.psum(back_part, 'fsdp').astype(jnp.bfloat16)]
    ppermute x0 -> x20, starting transfers between devices: none -> 24.6 us  [swap(): return lax.ppermute(array, axis, [(i, i ^ distance) for i in range(size)])]
    reduce_scatter x1 -> x0, waiting for transfers between devices: 23.3 us -> none  [on_device(): lax.psum_scatter(gradient_down_partial, 'group', scatter_dimension=0, til...]
    unnamed x5 -> x0, waiting for transfers between devices: 15.9 us -> none
    all_to_all x3 -> x0, starting transfers between devices: 11.6 us -> none  [the longest x1 5.16 us: on_device(): lax.all_to_all(send_len, 'group', split_axis=0, concat_axis=0, tiled=True)]
    ppermute x0 -> x20, waiting for transfers between devices: none -> 9.74 us  [swap(): return lax.ppermute(array, axis, [(i, i ^ distance) for i in range(size)])]
    all_to_all x3 -> x0, waiting for transfers between devices: 8.47 us -> none  [the longest x1 4.25 us: on_device(): lax.all_to_all(send_adv, 'group', split_axis=0, concat_axis=0, tiled=True)]
  transfers between devices with their start and end apart: 7 -> 20, of which waited for: 5 -> 5; matrix products, arithmetic and copies ran while one was open for 7% -> 25% of each run, Pallas kernels for 0% -> 0%
where the time goes in v1:
time: 72.7 us; the launch traced here: 72.4 us
  starting transfers between devices  24.6 us (34%)
  matrix products  23.8 us (33%)
  waiting for transfers between devices  9.74 us (13%)
  other arithmetic  5.91 us (8%)
  local copies, waits for them, and re-layouts  4.78 us (7%)
  between operations  3.54 us (5%)
    ppermute x20, starting transfers between devices, swap(): return lax.ppermute(array, axis, [(i, i ^ distance) for i in range(size)])  24.6 us
    dot_general x12, matrix products, dot(): return lax.dot_general(a, b, (dims, ((), ())), preferred_element_type=F32)  23.8 us
    ppermute x20, waiting for transfers between devices, swap(): return lax.ppermute(array, axis, [(i, i ^ distance) for i in range(size)])  9.74 us
  transfers between devices with their start and end apart: 20, of which 5 were waited for; matrix products, arithmetic and copies ran while one was open for 25% of the time, Pallas kernels for 0%

profile of v1, /device:TPU:0, one launch (start us, length us, event | category | flops | bytes accessed | tf_op | source)
XLA Modules:
  0.0 72.4 jit_solution(4374871791214073336)
XLA Ops:
  3.7 3.0 %collective-permute-start.5 = (f32[4,19]{1,0:T(4,128)S(1)}, f32[4,19]{1,0:T(4,128)S(1)}, u32[]{:S(2)}, u32[]{:S(2)}) collective-permute-start(f32[4,19]{1,0:T(4,128)S(1)} %pad_maximum_fusion.14), channel_id=1, source_target_pairs={{0,16},{8,24},{16,0},{24,8},{1,17},{9,25},{17,1},{25,9},{2,18},{10... | collective-permute-start | bytes 920 | tf_op jit(solution)/shard_map/ppermute | solution.py:17
  6.7 1.5 %collective-permute-start.4 = (f32[4,19]{1,0:T(4,128)S(1)}, f32[4,19]{1,0:T(4,128)S(1)}, u32[]{:S(2)}, u32[]{:S(2)}) collective-permute-start(f32[4,19]{1,0:T(4,128)S(1)} %pad_maximum_fusion.14), channel_id=1, source_target_pairs={{0,8},{8,0},{16,24},{24,16},{1,9},{9,1},{17,25},{25,17},{2,10},{10... | collective-permute-start | bytes 920 | tf_op jit(solution)/shard_map/ppermute | solution.py:17
  8.2 1.3 %fusion.49 = f32[64,64]{1,0:T(8,128)S(1)} fusion(bf16[64,1848]{1,0:T(8,128)(2,1)} %param.14, bf16[64,1848]{1,0:T(8,128)(2,1)} %param.13), kind=kOutput, calls=%fused_computation.119 | convolution fusion | flops 15138816 | bytes 489472 | tf_op jit(solution)/shard_map/dot_general | solution.py:62
  9.5 4.1 %collective-permute-start.9 = (f32[64,64]{1,0:T(8,128)S(1)}, f32[64,64]{1,0:T(8,128)S(1)}, u32[]{:S(2)}, u32[]{:S(2)}) collective-permute-start(f32[64,64]{1,0:T(8,128)S(1)} %fusion.49), channel_id=1, source_target_pairs={{0,6},{1,7},{2,4},{3,5},{4,2},{5,3},{6,0},{7,1},{8,14},{9,15},{10,... | collective-permute-start | bytes 49160 | tf_op jit(solution)/shard_map/ppermute | solution.py:17
  13.6 0.8 %fusion.65 = f32[1,4,19]{2,1,0:T(4,128)S(1)} fusion(f32[4,1]{1,0:T(4,128)S(1)} %copy.36, f32[4,1]{1,0:T(4,128)S(1)} %copy.35, f32[4,1]{1,0:T(4,128)S(1)} %copy.34, f32[4,16]{1,0:T(4,128)} %bitcast.31), kind=kLoop, calls=%fused_computation.120 | loop fusion | flops 228 | bytes 608 | tf_op jit(solution)/shard_map/stack | solution.py:99
  14.4 0.8 %squeeze.20 = f32[64]{0:T(128)S(1)} reshape(f32[1,4,16]{2,1,0:T(4,128)} %param.15) | data formatting | bytes 512 | tf_op jit(solution)/shard_map/squeeze | solution.py:100
  15.2 1.0 %constant_dynamic-slice_fusion.3 = bf16[64,2048]{1,0:T(8,128)(2,1)S(1)} fusion(bf16[64,8192]{1,0:T(8,128)(2,1)} %param.10, s32[]{:T(128)S(6)} %select_n.130), kind=kLoop, calls=%fused_computation.102 | loop fusion | bytes 524292 | tf_op jit(solution)/shard_map/dynamic_slice | solution.py:108
  16.2 5.5 %fusion.48 = f32[64,1848]{1,0:T(8,128)S(1)} fusion(bf16[64,2048]{1,0:T(8,128)(2,1)S(1)} %constant_dynamic-slice_fusion.3, bf16[2048,1848]{0,1:T(8,128)(2,1)} %param.11), kind=kOutput, calls=%fused_computation.118 | convolution fusion | flops 484442112 | bytes 8304640 | tf_op jit(solution)/shard_map/dot_general | solution.py:62
  21.7 1.1 %constant_dynamic-slice_fusion.2 = (bf16[64,1024]{1,0:T(8,128)(2,1)S(1)}, bf16[64,1024]{1,0:T(8,128)(2,1)S(1)}, bf16[64,1024]{1,0:T(8,128)(2,1)S(1)}) fusion(bf16[64,8192]{1,0:T(8,128)(2,1)} %param.10, s32[]{:T(128)S(6)} %select_n.133, s32[]{:T(128)S(6)} %select_n.135, s32[]{:T(128)S(6)} %select_n.134), kind=kLoop, calls=%fused_computation.101 | loop fusion | bytes 786444 | tf_op jit(solution)/shard_map/dynamic_slice | solution.py:86
  22.9 1.5 %collective-permute-start = (bf16[64,1024]{1,0:T(8,128)(2,1)S(1)}, bf16[64,1024]{1,0:T(8,128)(2,1)S(1)}, u32[]{:S(2)}, u32[]{:S(2)}) collective-permute-start(bf16[64,1024]{1,0:T(8,128)(2,1)S(1)} %get-tuple-element.12), channel_id=1, source_target_pairs={{0,8},{8,0},{16,24},{24,16},{1,9},{9,1},{17,25},{25,17},{2,10},{10... | collective-permute-start | bytes 393224 | tf_op jit(solution)/shard_map/ppermute | solution.py:17
  24.4 1.5 %collective-permute-start.2 = (bf16[64,1024]{1,0:T(8,128)(2,1)S(1)}, bf16[64,1024]{1,0:T(8,128)(2,1)S(1)}, u32[]{:S(2)}, u32[]{:S(2)}) collective-permute-start(bf16[64,1024]{1,0:T(8,128)(2,1)S(1)} %get-tuple-element.13), channel_id=1, source_target_pairs={{0,24},{8,16},{16,8},{24,0},{1,25},{9,17},{17,9},{25,1},{2,26},{10... | collective-permute-start | bytes 393224 | tf_op jit(solution)/shard_map/ppermute | solution.py:17
  32.3 2.7 %collective-permute-done.7 = f32[64,64]{1,0:T(8,128)S(1)} collective-permute-done((f32[64,64]{1,0:T(8,128)S(1)}, f32[64,64]{1,0:T(8,128)S(1)}, u32[]{:S(2)}, u32[]{:S(2)}) %collective-permute-start.7) | collective-permute-done | bytes 16416 | tf_op jit(solution)/shard_map/ppermute | solution.py:17
  36.5 5.7 %convolution_convert_fusion.2 = bf16[64,1848]{1,0:T(8,128)(2,1)S(1)} fusion(bf16[2048,1848]{0,1:T(8,128)(2,1)} %param.11, bf16[64,1024]{1,0:T(8,128)(2,1)S(1)} %get-tuple-element.16, bf16[64,1024]{1,0:T(8,128)(2,1)S(1)} %get-tuple-element.15), kind=kOutput, calls=%fused_computation.10 | convolution fusion | flops 485084672 | bytes 8068096 | tf_op jit(solution)/shard_map/dot_general | solution.py:62
  42.7 5.7 %convolution_convert_fusion.1 = bf16[64,1848]{1,0:T(8,128)(2,1)S(1)} fusion(bf16[2048,1848]{0,1:T(8,128)(2,1)} %param.11, bf16[64,1024]{1,0:T(8,128)(2,1)S(1)} %get-tuple-element.24, bf16[64,1024]{1,0:T(8,128)(2,1)S(1)} %get-tuple-element.25), kind=kOutput, calls=%fused_computation.9 | convolution fusion | flops 485084672 | bytes 8068096 | tf_op jit(solution)/shard_map/dot_general | solution.py:62
  48.7 1.6 %collective-permute-start.11 = (f32[64,128]{1,0:T(8,128)S(1)}, f32[64,128]{1,0:T(8,128)S(1)}, u32[]{:S(2)}, u32[]{:S(2)}) collective-permute-start(f32[64,128]{1,0:T(8,128)S(1)} %get-tuple-element.28), channel_id=1, source_target_pairs={{0,8},{8,0},{16,24},{24,16},{1,9},{9,1},{17,25},{25,17},{2,10},{10... | collective-permute-start | bytes 98312 | tf_op jit(solution)/shard_map/ppermute | solution.py:17
  50.3 1.5 %collective-permute-start.13 = (f32[64,128]{1,0:T(8,128)S(1)}, f32[64,128]{1,0:T(8,128)S(1)}, u32[]{:S(2)}, u32[]{:S(2)}) collective-permute-start(f32[64,128]{1,0:T(8,128)S(1)} %get-tuple-element.29), channel_id=1, source_target_pairs={{0,24},{8,16},{16,8},{24,0},{1,25},{9,17},{17,9},{25,1},{2,26},{10... | collective-permute-start | bytes 98312 | tf_op jit(solution)/shard_map/ppermute | solution.py:17
  52.3 2.4 %convolution_convert_fusion = bf16[64,1848]{1,0:T(8,128)(2,1)S(1)} fusion(bf16[2048,1848]{0,1:T(8,128)(2,1)S(1)} %bitcast.29, bf16[64,1024]{1,0:T(8,128)(2,1)S(1)} %get-tuple-element.26, bf16[64,1024]{1,0:T(8,128)(2,1)S(1)} %get-tuple-element.27), kind=kOutput, calls=%fused_computation.8 | convolution fusion | flops 485084672 | bytes 8068096 | tf_op jit(solution)/shard_map/dot_general | solution.py:62
  54.7 2.5 %collective-permute-start.16 = (bf16[64,1848]{1,0:T(8,128)(2,1)S(1)}, bf16[64,1848]{1,0:T(8,128)(2,1)S(1)}, u32[]{:S(2)}, u32[]{:S(2)}) collective-permute-start(bf16[64,1848]{1,0:T(8,128)(2,1)S(1)} %convolution_convert_fusion), channel_id=1, source_target_pairs={{0,24},{8,16},{16,8},{24,0},{1,25},{9,17},{17,9},{25,1},{2,26},{10... | collective-permute-start | bytes 709640 | tf_op jit(solution)/shard_map/ppermute | solution.py:17
  58.8 2.5 %collective-permute-start.19 = (bf16[16,1848]{1,0:T(8,128)(2,1)S(1)}, bf16[16,1848]{1,0:T(8,128)(2,1)S(1)}, u32[]{:S(2)}, u32[]{:S(2)}) collective-permute-start(bf16[16,1848]{1,0:T(8,128)(2,1)S(1)} %get-tuple-element.22), channel_id=1, source_target_pairs={{0,24},{8,16},{16,8},{24,0},{1,25},{9,17},{17,9},{25,1},{2,26},{10... | collective-permute-start | bytes 177416 | tf_op jit(solution)/shard_map/ppermute | solution.py:17
  62.0 1.1 %convolution_multiply_fusion.2 = f32[2048,64]{0,1:T(8,128)} fusion(bf16[64,1024]{1,0:T(8,128)(2,1)S(1)} %get-tuple-element.26, bf16[64,1024]{1,0:T(8,128)(2,1)S(1)} %get-tuple-element.27, bf16[64,1024]{1,0:T(8,128)(2,1)S(1)} %get-tuple-element.24, bf16[64,1024]{1,0:T(8,128)(2,1)S(1)} %get-tuple-element.25, bf16[64,1024]{1,0:T(8,128)(2,1)S(1)} %get-tuple-element.16, ...), kind=kOutput, calls=%fused_computation.6 | convolution fusion | flops 74711040 | bytes 1605632 | tf_op jit(solution)/shard_map/dot_general | solution.py:62
  63.2 1.7 %collective-permute-done.17 = bf16[16,1848]{1,0:T(8,128)(2,1)S(1)} collective-permute-done((bf16[16,1848]{1,0:T(8,128)(2,1)S(1)}, bf16[16,1848]{1,0:T(8,128)(2,1)S(1)}, u32[]{:S(2)}, u32[]{:S(2)}) %collective-permute-start.17) | collective-permute-done | bytes 59168 | tf_op jit(solution)/shard_map/ppermute | solution.py:17
  64.9 1.5 %collective-permute-start.14 = (bf16[64,1848]{1,0:T(8,128)(2,1)S(1)}, bf16[64,1848]{1,0:T(8,128)(2,1)S(1)}, u32[]{:S(2)}, u32[]{:S(2)}) collective-permute-start(bf16[64,1848]{1,0:T(8,128)(2,1)S(1)} %convolution_convert_fusion.2), channel_id=1, source_target_pairs={{0,8},{8,0},{16,24},{24,16},{1,9},{9,1},{17,25},{25,17},{2,10},{10... | collective-permute-start | bytes 709640 | tf_op jit(solution)/shard_map/ppermute | solution.py:17
  66.4 4.3 %collective-permute-done.18 = bf16[16,1848]{1,0:T(8,128)(2,1)S(1)} collective-permute-done((bf16[16,1848]{1,0:T(8,128)(2,1)S(1)}, bf16[16,1848]{1,0:T(8,128)(2,1)S(1)}, u32[]{:S(2)}, u32[]{:S(2)}) %collective-permute-start.18) | collective-permute-done | bytes 59168 | tf_op jit(solution)/shard_map/ppermute | solution.py:17
  71.4 1.0 %fusion.4 = bf16[64,1848]{1,0:T(8,128)(2,1)} fusion(f32[64,1848]{1,0:T(8,128)S(1)} %fusion.48, bf16[64,64]{1,0:T(8,128)(2,1)S(1)} %fusion.29, bf16[64,1848]{1,0:T(8,128)(2,1)S(1)} %copy-done.2, bf16[64,1848]{1,0:T(8,128)(2,1)S(1)} %collective-permute-done.16, bf16[64,1848]{1,0:T(8,128)(2,1)S(1)} %collective-permute-done.15, ...), kind=kOutput, calls=%fused_computation.7 | convolution fusion | flops 16203264 | bytes 1664000 | tf_op jit(solution)/shard_map/dot_general | solution.py:62
  (83 shorter events, 12.8 us)
Async XLA Ops:
  0.6 41.6 %copy-start = (bf16[2048,64]{0,1:T(8,128)(2,1)S(1)}, bf16[2048,64]{0,1:T(8,128)(2,1)}, u32[]{:S(2)}) copy-start(bf16[2048,64]{0,1:T(8,128)(2,1)} %param.12) | copy-start | bytes 786436
  0.6 22.1 %copy-start.3 = (f32[1,4,16]{2,1,0:T(4,128)S(1)}, f32[1,4,16]{2,1,0:T(4,128)}, u32[]{:S(2)}) copy-start(f32[1,4,16]{2,1,0:T(4,128)} %param.15) | copy-start | bytes 772
  3.7 19.2 %collective-permute-start.5 = (f32[4,19]{1,0:T(4,128)S(1)}, f32[4,19]{1,0:T(4,128)S(1)}, u32[]{:S(2)}, u32[]{:S(2)}) collective-permute-start(f32[4,19]{1,0:T(4,128)S(1)} %pad_maximum_fusion.14), channel_id=1, source_target_pairs={{0,16},{8,24},{16,0},{24,8},{1,17},{9,25},{17,1},{25,9},{2,18},{10... | collective-permute-start | bytes 920 | tf_op jit(solution)/shard_map/ppermute | solution.py:17
  6.7 17.7 %collective-permute-start.4 = (f32[4,19]{1,0:T(4,128)S(1)}, f32[4,19]{1,0:T(4,128)S(1)}, u32[]{:S(2)}, u32[]{:S(2)}) collective-permute-start(f32[4,19]{1,0:T(4,128)S(1)} %pad_maximum_fusion.14), channel_id=1, source_target_pairs={{0,8},{8,0},{16,24},{24,16},{1,9},{9,1},{17,25},{25,17},{2,10},{10... | collective-permute-start | bytes 920 | tf_op jit(solution)/shard_map/ppermute | solution.py:17
  8.2 17.7 %collective-permute-start.6 = (f32[4,19]{1,0:T(4,128)S(1)}, f32[4,19]{1,0:T(4,128)S(1)}, u32[]{:S(2)}, u32[]{:S(2)}) collective-permute-start(f32[4,19]{1,0:T(4,128)S(1)} %pad_maximum_fusion.14), channel_id=1, source_target_pairs={{0,24},{8,16},{16,8},{24,0},{1,25},{9,17},{17,9},{25,1},{2,26},{10... | collective-permute-start | bytes 920 | tf_op jit(solution)/shard_map/ppermute | solution.py:17
  9.5 22.8 %collective-permute-start.9 = (f32[64,64]{1,0:T(8,128)S(1)}, f32[64,64]{1,0:T(8,128)S(1)}, u32[]{:S(2)}, u32[]{:S(2)}) collective-permute-start(f32[64,64]{1,0:T(8,128)S(1)} %fusion.49), channel_id=1, source_target_pairs={{0,6},{1,7},{2,4},{3,5},{4,2},{5,3},{6,0},{7,1},{8,14},{9,15},{10,... | collective-permute-start | bytes 49160 | tf_op jit(solution)/shard_map/ppermute | solution.py:17
  13.6 18.7 %collective-permute-start.8 = (f32[64,64]{1,0:T(8,128)S(1)}, f32[64,64]{1,0:T(8,128)S(1)}, u32[]{:S(2)}, u32[]{:S(2)}) collective-permute-start(f32[64,64]{1,0:T(8,128)S(1)} %fusion.49), channel_id=1, source_target_pairs={{0,4},{1,5},{2,6},{3,7},{4,0},{5,1},{6,2},{7,3},{8,12},{9,13},{10,... | collective-permute-start | bytes 49160 | tf_op jit(solution)/shard_map/ppermute | solution.py:17
  22.9 8.2 %collective-permute-start = (bf16[64,1024]{1,0:T(8,128)(2,1)S(1)}, bf16[64,1024]{1,0:T(8,128)(2,1)S(1)}, u32[]{:S(2)}, u32[]{:S(2)}) collective-permute-start(bf16[64,1024]{1,0:T(8,128)(2,1)S(1)} %get-tuple-element.12), channel_id=1, source_target_pairs={{0,8},{8,0},{16,24},{24,16},{1,9},{9,1},{17,25},{25,17},{2,10},{10... | collective-permute-start | bytes 393224 | tf_op jit(solution)/shard_map/ppermute | solution.py:17
  24.4 7.4 %collective-permute-start.2 = (bf16[64,1024]{1,0:T(8,128)(2,1)S(1)}, bf16[64,1024]{1,0:T(8,128)(2,1)S(1)}, u32[]{:S(2)}, u32[]{:S(2)}) collective-permute-start(bf16[64,1024]{1,0:T(8,128)(2,1)S(1)} %get-tuple-element.13), channel_id=1, source_target_pairs={{0,24},{8,16},{16,8},{24,0},{1,25},{9,17},{17,9},{25,1},{2,26},{10... | collective-permute-start | bytes 393224 | tf_op jit(solution)/shard_map/ppermute | solution.py:17
  25.9 6.3 %collective-permute-start.1 = (bf16[64,1024]{1,0:T(8,128)(2,1)S(1)}, bf16[64,1024]{1,0:T(8,128)(2,1)S(1)}, u32[]{:S(2)}, u32[]{:S(2)}) collective-permute-start(bf16[64,1024]{1,0:T(8,128)(2,1)S(1)} %get-tuple-element.14), channel_id=1, source_target_pairs={{0,16},{8,24},{16,0},{24,8},{1,17},{9,25},{17,1},{25,9},{2,18},{10... | collective-permute-start | bytes 393224 | tf_op jit(solution)/shard_map/ppermute | solution.py:17
  31.1 4.0 %collective-permute-start.7 = (f32[64,64]{1,0:T(8,128)S(1)}, f32[64,64]{1,0:T(8,128)S(1)}, u32[]{:S(2)}, u32[]{:S(2)}) collective-permute-start(f32[64,64]{1,0:T(8,128)S(1)} %fusion.49), channel_id=1, source_target_pairs={{0,2},{1,3},{2,0},{3,1},{4,6},{5,7},{6,4},{7,5},{8,10},{9,11},{10,... | collective-permute-start | bytes 49160 | tf_op jit(solution)/shard_map/ppermute | solution.py:17
  32.2 4.2 %collective-permute-start.3 = (bf16[192,1024]{1,0:T(8,128)(2,1)S(1)}, bf16[192,1024]{1,0:T(8,128)(2,1)S(1)}, u32[]{:S(2)}, u32[]{:S(2)}) collective-permute-start(bf16[192,1024]{1,0:T(8,128)(2,1)S(1)} %pad_maximum_fusion), channel_id=1, source_target_pairs={{0,1},{1,0},{2,3},{3,2},{4,5},{5,4},{6,7},{7,6},{8,9},{9,8},{10,11... | collective-permute-start | bytes 1179656 | tf_op jit(solution)/shard_map/ppermute | solution.py:17
  35.1 1.3 %collective-permute-start.10 = (f32[64,64]{1,0:T(8,128)S(1)}, f32[64,64]{1,0:T(8,128)S(1)}, u32[]{:S(2)}, u32[]{:S(2)}) collective-permute-start(f32[64,64]{1,0:T(8,128)S(1)} %add_add_fusion), channel_id=1, source_target_pairs={{0,1},{1,0},{2,3},{3,2},{4,5},{5,4},{6,7},{7,6},{8,9},{9,8},{10,11... | collective-permute-start | bytes 49160 | tf_op jit(solution)/shard_map/ppermute | solution.py:17
  36.5 15.8 %slice-start = ((s8[7569408]{0:T(1024)(128)(4,1)}), s8[4194304]{0:T(1024)(128)(4,1)S(1)}, s32[]{:S(2)}) async-start(s8[7569408]{0:T(1024)(128)(4,1)} %bitcast.28), calls=%async_computation | async-start | bytes 8388608
  48.7 9.0 %collective-permute-start.11 = (f32[64,128]{1,0:T(8,128)S(1)}, f32[64,128]{1,0:T(8,128)S(1)}, u32[]{:S(2)}, u32[]{:S(2)}) collective-permute-start(f32[64,128]{1,0:T(8,128)S(1)} %get-tuple-element.28), channel_id=1, source_target_pairs={{0,8},{8,0},{16,24},{24,16},{1,9},{9,1},{17,25},{25,17},{2,10},{10... | collective-permute-start | bytes 98312 | tf_op jit(solution)/shard_map/ppermute | solution.py:17
  50.3 7.4 %collective-permute-start.13 = (f32[64,128]{1,0:T(8,128)S(1)}, f32[64,128]{1,0:T(8,128)S(1)}, u32[]{:S(2)}, u32[]{:S(2)}) collective-permute-start(f32[64,128]{1,0:T(8,128)S(1)} %get-tuple-element.29), channel_id=1, source_target_pairs={{0,24},{8,16},{16,8},{24,0},{1,25},{9,17},{17,9},{25,1},{2,26},{10... | collective-permute-start | bytes 98312 | tf_op jit(solution)/shard_map/ppermute | solution.py:17
  51.7 19.7 %copy-start.2 = (bf16[64,1848]{1,0:T(8,128)(2,1)S(1)}, bf16[64,1848]{1,0:T(8,128)(2,1)}, u32[]{:S(2)}) copy-start(bf16[64,1848]{1,0:T(8,128)(2,1)} %param.13) | copy-start | bytes 709636
  51.8 5.9 %collective-permute-start.12 = (f32[64,128]{1,0:T(8,128)S(1)}, f32[64,128]{1,0:T(8,128)S(1)}, u32[]{:S(2)}, u32[]{:S(2)}) collective-permute-start(f32[64,128]{1,0:T(8,128)S(1)} %get-tuple-element.30), channel_id=1, source_target_pairs={{0,16},{8,24},{16,0},{24,8},{1,17},{9,25},{17,1},{25,9},{2,18},{10... | collective-permute-start | bytes 98312 | tf_op jit(solution)/shard_map/ppermute | solution.py:17
  54.7 16.7 %collective-permute-start.16 = (bf16[64,1848]{1,0:T(8,128)(2,1)S(1)}, bf16[64,1848]{1,0:T(8,128)(2,1)S(1)}, u32[]{:S(2)}, u32[]{:S(2)}) collective-permute-start(bf16[64,1848]{1,0:T(8,128)(2,1)S(1)} %convolution_convert_fusion), channel_id=1, source_target_pairs={{0,24},{8,16},{16,8},{24,0},{1,25},{9,17},{17,9},{25,1},{2,26},{10... | collective-permute-start | bytes 709640 | tf_op jit(solution)/shard_map/ppermute | solution.py:17
  57.2 14.2 %collective-permute-start.15 = (bf16[64,1848]{1,0:T(8,128)(2,1)S(1)}, bf16[64,1848]{1,0:T(8,128)(2,1)S(1)}, u32[]{:S(2)}, u32[]{:S(2)}) collective-permute-start(bf16[64,1848]{1,0:T(8,128)(2,1)S(1)} %convolution_convert_fusion.1), channel_id=1, source_target_pairs={{0,16},{8,24},{16,0},{24,8},{1,17},{9,25},{17,1},{25,9},{2,18},{10... | collective-permute-start | bytes 709640 | tf_op jit(solution)/shard_map/ppermute | solution.py:17
  58.2 6.6 %collective-permute-start.17 = (bf16[16,1848]{1,0:T(8,128)(2,1)S(1)}, bf16[16,1848]{1,0:T(8,128)(2,1)S(1)}, u32[]{:S(2)}, u32[]{:S(2)}) collective-permute-start(bf16[16,1848]{1,0:T(8,128)(2,1)S(1)} %get-tuple-element.21), channel_id=1, source_target_pairs={{0,8},{8,0},{16,24},{24,16},{1,9},{9,1},{17,25},{25,17},{2,10},{10... | collective-permute-start | bytes 177416 | tf_op jit(solution)/shard_map/ppermute | solution.py:17
  58.8 7.5 %collective-permute-start.19 = (bf16[16,1848]{1,0:T(8,128)(2,1)S(1)}, bf16[16,1848]{1,0:T(8,128)(2,1)S(1)}, u32[]{:S(2)}, u32[]{:S(2)}) collective-permute-start(bf16[16,1848]{1,0:T(8,128)(2,1)S(1)} %get-tuple-element.22), channel_id=1, source_target_pairs={{0,24},{8,16},{16,8},{24,0},{1,25},{9,17},{17,9},{25,1},{2,26},{10... | collective-permute-start | bytes 177416 | tf_op jit(solution)/shard_map/ppermute | solution.py:17
  61.3 9.4 %collective-permute-start.18 = (bf16[16,1848]{1,0:T(8,128)(2,1)S(1)}, bf16[16,1848]{1,0:T(8,128)(2,1)S(1)}, u32[]{:S(2)}, u32[]{:S(2)}) collective-permute-start(bf16[16,1848]{1,0:T(8,128)(2,1)S(1)} %get-tuple-element.23), channel_id=1, source_target_pairs={{0,16},{8,24},{16,0},{24,8},{1,17},{9,25},{17,1},{25,9},{2,18},{10... | collective-permute-start | bytes 177416 | tf_op jit(solution)/shard_map/ppermute | solution.py:17
  64.9 6.5 %collective-permute-start.14 = (bf16[64,1848]{1,0:T(8,128)(2,1)S(1)}, bf16[64,1848]{1,0:T(8,128)(2,1)S(1)}, u32[]{:S(2)}, u32[]{:S(2)}) collective-permute-start(bf16[64,1848]{1,0:T(8,128)(2,1)S(1)} %convolution_convert_fusion.2), channel_id=1, source_target_pairs={{0,8},{8,0},{16,24},{24,16},{1,9},{9,1},{17,25},{25,17},{2,10},{10... | collective-permute-start | bytes 709640 | tf_op jit(solution)/shard_map/ppermute | solution.py:17
  (2 other events, 25.0 us)

commit v2 on v1

v2 whole, which is shorter than its diff:
```python
import functools

import jax
import jax.numpy as jnp
from jax import lax
from jax.experimental import pallas as pl
from jax.experimental.pallas import tpu as pltpu
from jax.sharding import PartitionSpec as P

COMP = 16


ADAPTER_SCALING = 0.25
SPREAD_FLOOR = 0.16
F32 = jnp.float32
BF16 = jnp.bfloat16
LANES = 128
BLOCK = 8
STEP = 512
NT = (((1,), (1,)), ((), ()))
TN = (((0,), (0,)), ((), ()))
VMEM = pl.BlockSpec(memory_space=pltpu.VMEM)
SMEM = pl.BlockSpec(memory_space=pltpu.SMEM)
HBM = pl.BlockSpec(memory_space=pltpu.HBM)
ANY = pl.BlockSpec(memory_space=pl.ANY)


def swap(array, axis, distance):
    size = lax.axis_size(axis)
    return lax.ppermute(array, axis, [(i, i ^ distance) for i in range(size)])


def sum_over_pairs(partial):
    size = lax.axis_size("fsdp")
    if size & (size - 1):
        same = [[i for i in range(size) if i % 2 == r] for r in range(2)]
        return lax.psum(partial, "fsdp", axis_index_groups=same)
    parts = [partial] + [swap(partial, "fsdp", d) for d in range(2, size, 2)]
    while len(parts) > 1:
        parts = [parts[i] + parts[i + 1] for i in range(0, len(parts), 2)]
    return parts[0]


def call(body, name, outs, ins, out_specs=None, scratch=(), limit=8, flops=0, moved=0):
    return pl.pallas_call(
        body,
        out_shape=outs,
        in_specs=ins,
        out_specs=[VMEM] * len(outs) if out_specs is None else out_specs,
        scratch_shapes=scratch,
        compiler_params=pltpu.CompilerParams(vmem_limit_bytes=limit << 20),
        cost_estimate=pl.CostEstimate(flops=flops, bytes_accessed=moved, transcendentals=0),
        name=name,
    )


def in_hbm(array):
    return pltpu.with_memory_space_constraint(array, pltpu.HBM)


def positions():
    own, member = lax.axis_index("group"), lax.axis_index("fsdp")
    return own, member, lax.rem(member, 2)


def pack_kernel(groups, depth, hidden_ref, old_hbm, reward_hbm, length_hbm, dest_hbm, *rest):
    messages, own_table, own_hidden = rest[: groups - 1], rest[groups - 1], rest[groups]
    old_ref, reward_ref, length_ref, dest_ref, sems, small_sems = rest[groups + 1 :]
    own, _, core = positions()
    half = depth // 2
    copies = []
    for d in reversed(range(1, groups)):
        start = pl.multiple_of((own ^ d) * depth + core * half, LANES)
        copies.append((hidden_ref.at[:, pl.ds(start, half)], messages[d - 1].at[:, :half]))
    copies.append((hidden_ref.at[:, pl.ds(pl.multiple_of(own * depth, LANES), depth)], own_hidden))
    copies = [pltpu.make_async_copy(a, b, sems.at[i]) for i, (a, b) in enumerate(copies)]
    small = ((old_hbm, old_ref), (reward_hbm, reward_ref), (length_hbm, length_ref), (dest_hbm, dest_ref))
    small = [pltpu.make_async_copy(a, b, small_sems.at[i]) for i, (a, b) in enumerate(small)]
    for copy in small + copies:
        copy.start()
    for copy in small:
        copy.wait()
    total, squares = jnp.float32(0), jnp.float32(0)
    for k in range(groups):
        total += reward_ref[0, k]
        squares += reward_ref[0, k] * reward_ref[0, k]
    old = old_ref[0]
    old = jnp.concatenate([old, jnp.zeros((groups, LANES - old.shape[1]), F32)], axis=1)
    for d in range(groups):
        line, reward, length = jnp.zeros((1, LANES), F32), jnp.float32(0), jnp.float32(0)
        for k in range(groups):
            chosen = dest_ref[0, k] == (own ^ d)
            line = jnp.where(chosen, old[k : k + 1], line)
            reward = jnp.where(chosen, reward_ref[0, k], reward)
            length = jnp.where(chosen, length_ref[0, k].astype(F32), length)
        lines = [line] + [jnp.full((1, LANES), x, F32) for x in (reward, length, total, squares)]
        value = jnp.concatenate(lines + [jnp.zeros((BLOCK - len(lines), LANES), F32)], axis=0)
        if d == 0:
            own_table[...] = value
            continue
        terms = []
        for _ in range(3):
            terms.append(value.astype(BF16).astype(F32))
            value = value - terms[-1]
        terms = jnp.concatenate(terms + [jnp.zeros((BLOCK, LANES), F32)], axis=0)
        messages[d - 1][: 4 * BLOCK, half:] = terms.astype(BF16)
    for copy in copies:
        copy.wait()


def back_kernel(upstream_hbm, up_hbm, upstream_ref, up_ref, back_ref, sems):
    pairs = ((upstream_hbm, upstream_ref), (up_hbm, up_ref))
    copies = [pltpu.make_async_copy(a, b, sems.at[i]) for i, (a, b) in enumerate(pairs)]
    for copy in copies:
        copy.start()
    for copy in copies:
        copy.wait()
    back_ref[...] = lax.dot_general(upstream_ref[...], up_ref[...], NT, preferred_element_type=F32)


def load_kernel(pieces, weight_hbm, at_hbm, new_hbm, after_ref, weight_ref, at_ref, new_ref, sems):
    size = weight_ref.shape[0] // 8 // pieces * 8
    starts = [i * size for i in range(pieces)] + [weight_ref.shape[0]]
    pairs = [(weight_hbm.at[a:b], weight_ref.at[a:b]) for a, b in zip(starts[:-1], starts[1:])]
    pairs += [(at_hbm, at_ref), (new_hbm, new_ref)]
    copies = [pltpu.make_async_copy(a, b, sems.at[i]) for i, (a, b) in enumerate(pairs)]
    for copy in copies:
        copy.start()
    for copy in copies:
        copy.wait()


def whole_rows(half, core, message, other):
    a, b = message[:, :half], other[:, :half]
    first = core == 0
    return jnp.concatenate([jnp.where(first, a, b), jnp.where(first, b, a)], axis=1)


def two_terms(value):
    high = value.astype(BF16).astype(F32)
    return jnp.concatenate([high, value - high], axis=1).astype(BF16)


def product_kernel(count, with_low, with_own, tokens, held_ref, at_ref, *refs):
    core = positions()[2]
    units, depth = held_ref.shape
    parts = [whole_rows(depth // 2, core, refs[i], refs[count + i]) for i in range(count)]
    refs = refs[2 * count :]
    if with_own:
        parts.append(refs[0][...])
        refs = refs[1:]
    rows = jnp.concatenate(parts, axis=0)
    lead = 0
    if with_low:
        low = lax.dot_general(rows, at_ref[...], NT, preferred_element_type=F32)
        lead = 2 * low.shape[1]
        refs[0][:, :lead] = two_terms(low)
    rows = rows.T
    for start in range(0, units, STEP):
        end = min(start + STEP, units)
        result = jnp.dot(held_ref[start:end], rows, preferred_element_type=F32).T
        for i, ref in enumerate(refs):
            ref[:, lead + start : lead + end] = result[i * tokens : (i + 1) * tokens].astype(ref.dtype)


def coef_kernel(groups, half, near, at_ref, new_ref, own_table, own_hidden, *rest):
    messages, others = rest[: groups - 1], rest[groups - 1 : groups - 1 + near]
    outs = rest[groups - 1 + near :]
    lows, coef_ref, loss_ref = outs[: near + 1], outs[near + 1], outs[near + 2]
    own, _, core = positions()
    tokens = own_hidden.shape[0]
    rows = [own_hidden[...]] + [whole_rows(half, core, messages[i], others[i]) for i in range(near)]
    low = lax.dot_general(jnp.concatenate(rows, axis=0), at_ref[...], NT, preferred_element_type=F32)
    for i, ref in enumerate(lows):
        ref[...] = low[i * tokens : (i + 1) * tokens]
    tables = [own_table[...]]
    for message in messages:
        terms = message[: 4 * BLOCK, half:].astype(F32)
        tables.append(terms[:BLOCK] + terms[BLOCK : 2 * BLOCK] + terms[2 * BLOCK : 3 * BLOCK])
    ordered = []
    for j in range(groups):
        table = tables[0]
        for d in range(1, groups):
            table = jnp.where((own ^ j) == d, tables[d], table)
        ordered.append(table)
    length = new_ref.shape[2]
    place = lax.broadcasted_iota(jnp.int32, (1, LANES), 1)
    diagonal = lax.broadcasted_iota(jnp.int32, (length, LANES), 0) == lax.broadcasted_iota(jnp.int32, (length, LANES), 1)
    new = new_ref[0]
    new = jnp.concatenate([new, jnp.zeros((groups, LANES - length), F32)], axis=1)
    together = COMP // groups
    parts = []
    loss = jnp.zeros((1, LANES), F32)
    for j in range(groups):
        prompt = ordered[j // together * together : (j // together + 1) * together]
        mean = sum(table[3:4] for table in prompt) / COMP
        square = sum(table[4:5] for table in prompt) / COMP
        spread = jnp.sqrt(jnp.maximum(square - mean * mean, SPREAD_FLOOR))
        old, reward, count = ordered[j][0:1], ordered[j][1:2], ordered[j][2:3]
        advantage = (reward - mean) / spread
        ratio = jnp.exp(new[j : j + 1] - old)
        live = (place.astype(F32) < count) & (place < length)
        coef = jnp.where(live, -(advantage * ratio) / (count * COMP), 0.0)
        loss = loss + coef
        column = jnp.sum(jnp.where(diagonal, coef, 0.0), axis=1, keepdims=True)
        parts.append(jnp.broadcast_to(column, (length, LANES)))
    coef_ref[...] = jnp.concatenate(parts, axis=0)
    loss_ref[...] = jnp.sum(loss, axis=1, keepdims=True)


def adapter_kernel(groups, share, ride_rows, *refs):
    lows, (far, back_ref, other_ref, coef_ref, upstream_ref) = refs[: groups - 1], refs[groups - 1 : groups + 4]
    messages, (own_term, own_back, low_ref, term) = refs[groups + 4 : 2 * groups + 3], refs[2 * groups + 3 :]
    own = positions()[0]
    coef = coef_ref[:, 0:1]
    rank = term.shape[0]
    low = far[:, :rank].astype(F32) + far[:, rank : 2 * rank].astype(F32)
    for ref in lows:
        low = low + ref[...]
    low = low.astype(BF16)
    low_ref[...] = low
    gradient = (coef * upstream_ref[...].astype(F32)).astype(BF16)
    term[...] = ADAPTER_SCALING * lax.dot_general(low, gradient, TN, preferred_element_type=F32)
    back = coef * (back_ref[...] + other_ref[...])
    own_back[...] = back.astype(BF16)
    stack = back.shape[0] // ride_rows
    ride = jnp.concatenate([back[i * ride_rows : (i + 1) * ride_rows] for i in range(stack)], axis=1).astype(BF16)
    lanes = stack * rank
    for d in range(groups):
        if share % 8 == 0:
            piece = term[pl.ds(pl.multiple_of((own ^ d) * share, share), share), :]
        else:
            piece = term[:share]
            for j in range(1, groups):
                piece = jnp.where((own ^ d) == j, term[j * share : (j + 1) * share], piece)
        if d == 0:
            own_term[...] = piece
            continue
        if share < ride_rows:
            piece = jnp.concatenate([piece, jnp.zeros((ride_rows - share, piece.shape[1]), F32)], axis=0)
        messages[d - 1][:, :lanes] = ride
        messages[d - 1][:, lanes:] = piece.astype(BF16)


def output_kernel(lead, total_ref, low_ref, up_ref, far, *rest):
    total = total_ref[...] + ADAPTER_SCALING * jnp.dot(low_ref[...], up_ref[...], preferred_element_type=F32)
    total = total + far[:, lead:].astype(F32)
    for ref in rest[:-1]:
        total = total + ref[...].astype(F32)
    rest[-1][...] = total.astype(BF16)


def gradient_kernel(groups, rank, share, ride_rows, own_term, own_back, own_hidden, *rest):
    arrived, messages, others = (rest[i * (groups - 1) : (i + 1) * (groups - 1)] for i in range(3))
    up_ref, down_ref = rest[3 * (groups - 1) :]
    core = positions()[2]
    half = own_hidden.shape[1] // 2
    tokens = own_hidden.shape[0]
    stack = tokens // ride_rows
    lanes = stack * rank
    hidden = [own_hidden[...]]
    backs = [own_back[...].astype(F32)]
    total = own_term[...]
    for come, message, other in zip(arrived, messages, others):
        total = total + come[:, lanes:].astype(F32)[:share]
        ride = come[:, :lanes].astype(F32)
        backs += [ride[:, i * rank : (i + 1) * rank] for i in range(stack)]
        hidden.append(whole_rows(half, core, message, other))
    up_ref[...] = total
    back = jnp.concatenate(backs, axis=0).astype(BF16)
    hidden = jnp.concatenate(hidden, axis=0)
    down_ref[...] = ADAPTER_SCALING * lax.dot_general(back, hidden, TN, preferred_element_type=F32)


def on_device(
    hidden_input_slots,
    base_weight,
    adapter_a,
    adapter_up_matrix,
    upstream,
    logp_new,
    logp_old,
    rewards,
    comp_lengths,
    assignment,
):
    groups = lax.axis_size("group")
    tokens = hidden_input_slots.shape[0]
    depth, units = base_weight.shape
    half = depth // 2
    rank = adapter_a.shape[1]
    others = range(1, groups)
    at, weight = adapter_a.T, base_weight.T

    *messages, own_table, own_hidden = call(
        functools.partial(pack_kernel, groups, depth),
        "pack",
        [pltpu.VMEM((tokens, half + LANES), BF16)] * (groups - 1)
        + [pltpu.VMEM((BLOCK, LANES), F32), pltpu.VMEM((tokens, depth), BF16)],
        [HBM] * 5,
        scratch=[
            pltpu.VMEM(logp_old.shape, F32),
            pltpu.SMEM(rewards.shape, F32),
            pltpu.SMEM(comp_lengths.shape, jnp.int32),
            pltpu.SMEM(assignment.shape, jnp.int32),
            pltpu.SemaphoreType.DMA((groups,)),
            pltpu.SemaphoreType.DMA((4,)),
        ],
        moved=2 * units * depth,
    )(*map(in_hbm, (hidden_input_slots, logp_old, rewards, comp_lengths, assignment)))
    got = {d: swap(messages[d - 1], "group", d) for d in reversed(others)}
    upstream, up, back = call(
        back_kernel,
        "back",
        [pltpu.VMEM((tokens, units), BF16), pltpu.VMEM((rank, units), BF16), pltpu.VMEM((tokens, rank), F32)],
        [HBM] * 2,
        scratch=[pltpu.SemaphoreType.DMA((2,))],
    )(*map(in_hbm, (upstream, adapter_up_matrix)))
    weight, at, new = call(
        functools.partial(load_kernel, 8),
        "load",
        [pltpu.VMEM((units, depth), BF16), pltpu.VMEM((rank, depth), BF16), pltpu.VMEM(logp_new.shape, F32)],
        [HBM] * 3 + [ANY],
        scratch=[pltpu.SemaphoreType.DMA((10,))],
    )(*map(in_hbm, (weight, at, logp_new)), back)
    weight, back, got = lax.optimization_barrier((weight, back, got))
    back = sum_over_pairs(back)
    theirs = {d: swap(got[d], "fsdp", 1) for d in reversed(others)}

    far, near = groups - 1, list(range(1, groups - 1))
    lead = 2 * rank
    came = {}
    (result,) = call(
        functools.partial(product_kernel, 1, True, False, tokens),
        "product",
        [pltpu.VMEM((tokens, lead + units), BF16)],
        [VMEM] * 4,
        flops=2 * units * tokens * depth,
        moved=units * depth * 2,
    )(weight, at, got[far], theirs[far])
    came[far] = swap(result, "group", far)
    *lows, coef, loss = call(
        functools.partial(coef_kernel, groups, half, len(near)),
        "coef",
        [pltpu.VMEM((tokens, rank), F32)] * (len(near) + 1)
        + [pltpu.VMEM((tokens, LANES), F32), jax.ShapeDtypeStruct((1, 1), F32)],
        [VMEM] * (3 + groups + len(near)),
    )(at, new, own_table, own_hidden, *[got[d] for d in others], *[theirs[d] for d in near])
    low_terms = [lows[0]] + [swap(low, "group", d) for d, low in zip(near, lows[1:])]
    *results, kept = call(
        functools.partial(product_kernel, len(near), False, True, tokens),
        "product",
        [pltpu.VMEM((tokens, units), BF16)] * len(near) + [pltpu.VMEM((tokens, units), F32)],
        [VMEM] * (3 + 2 * len(near)),
        flops=2 * units * tokens * depth * groups,
        moved=units * depth * 2,
    )(weight, at, *[got[d] for d in near], *[theirs[d] for d in near], own_hidden)
    for d, result in zip(near, results):
        came[d] = swap(result, "group", d)

    share = rank // groups
    ride_rows = max(share, 16)
    lanes = tokens // ride_rows * rank
    *pieces, own_term, own_back, low = call(
        functools.partial(adapter_kernel, groups, share, ride_rows),
        "adapter",
        [pltpu.VMEM((ride_rows, lanes + units), BF16)] * (groups - 1)
        + [pltpu.VMEM((share, units), F32), pltpu.VMEM((tokens, rank), BF16), pltpu.VMEM((tokens, rank), BF16)],
        [VMEM] * (groups + 4),
        scratch=[pltpu.VMEM((rank, units), F32)],
    )(*low_terms, came[far], back, swap(back, "fsdp", 1), coef, upstream)
    arrived = {d: swap(pieces[d - 1], "group", d) for d in reversed(others)}
    (projection_output,) = call(
        functools.partial(output_kernel, lead),
        "output",
        [jax.ShapeDtypeStruct((tokens, units), BF16)],
        [VMEM] * (4 + len(near)),
    )(kept, low, up, came[far], *[came[d] for d in near])
    gradient_up, gradient_down = call(
        functools.partial(gradient_kernel, groups, rank, share, ride_rows),
        "gradient",
        [jax.ShapeDtypeStruct((share, units), F32), jax.ShapeDtypeStruct((rank, depth), F32)],
        [VMEM] * (3 * groups),
    )(
        own_term,
        own_back,
        own_hidden,
        *[arrived[d] for d in others],
        *[got[d] for d in others],
        *[theirs[d] for d in others],
    )
    return (projection_output, gradient_down.T, gradient_up, loss[0])


def solution(mesh):
    return jax.shard_map(
        on_device,
        mesh=mesh,
        in_specs=(
            P("group", None),
            P("group", "fsdp"),
            P("group", None),
            P(None, "fsdp"),
            P("group", "fsdp"),
            P("group", None, None),
            P("group", None, None),
            P("group", None),
            P("group", None),
            P("group", None),
        ),
        out_specs=(P("group", "fsdp"), P("group", None), P("group", "fsdp"), P("group")),
        check_vma=False,
    )
```

time: 72.7 us -> 44.5 us (0.61)
  matrix products: 23.8 us -> 0 us
  Pallas kernels: 0 us -> 13.7 us
  starting transfers between devices: 24.6 us -> 18.5 us
  other arithmetic: 5.91 us -> 0.01 us
  local copies, waits for them, and re-layouts: 4.78 us -> 0 us
  between operations: 3.54 us -> 0.72 us
  waiting for transfers between devices: 9.74 us -> 11.4 us
    dot_general x12 -> x0, matrix products: 23.8 us -> none  [dot(): return lax.dot_general(a, b, (dims, ((), ())), preferred_element_type=F32)]
    pallas_call x0 -> x9, Pallas kernels: none -> 13.7 us  [the longest x1 3.28 us: on_device(): call(functools.partial(load_kernel, 8), 'load', [pltpu.VMEM((units, depth...]
    ppermute x20 -> x18, starting transfers between devices: 24.6 us -> 18.5 us  [swap(): return lax.ppermute(array, axis, [(i, i ^ distance) for i in range(size)])]
    dynamic_slice x2 -> x0, local copies, waits for them, and re-layouts: 2.04 us -> none  [the longest x1 1.07 us: on_device(): lax.dynamic_slice_in_dim(hidden_input_slots, (own_group ^ d) * depth + co...]
    reduce_sum x5 -> x0, other arithmetic: 1.7 us -> none  [the longest x1 0.68 us: coefficients(): sums = jnp.sum(jnp.where(onehot, rewards[:, :, None], 0.0), axis=(0, 1))]
    ppermute x20 -> x18, waiting for transfers between devices: 9.74 us -> 11.4 us  [swap(): return lax.ppermute(array, axis, [(i, i ^ distance) for i in range(size)])]
    convert_element_type x3 -> x0, other arithmetic: 1.37 us -> none  [the longest x1 0.71 us: on_device(): comp_lengths[0].astype(F32)[:, None]]
    concatenate x3 -> x0, other arithmetic: 0.86 us -> none  [the longest x1 0.76 us: on_device(): jnp.concatenate([logp_old[0], rewards[0][:, None], comp_lengths[0].astype...]
  transfers between devices with their start and end apart: 20 -> 18, of which waited for: 5 -> 4; matrix products, arithmetic and copies ran while one was open for 25% -> 0% of each run, Pallas kernels for 0% -> 26%
where the time goes in v2:
time: 44.5 us; the launch traced here: 44.3 us
  starting transfers between devices  18.5 us (42%)
  Pallas kernels  13.7 us (31%)
  waiting for transfers between devices  11.4 us (26%)
  between operations  0.72 us (2%)
    ppermute x18, starting transfers between devices, swap(): return lax.ppermute(array, axis, [(i, i ^ distance) for i in range(size)])  18.5 us
    ppermute x18, waiting for transfers between devices, swap(): return lax.ppermute(array, axis, [(i, i ^ distance) for i in range(size)])  11.4 us
    pallas_call x1, Pallas kernels, on_device(): call(functools.partial(load_kernel, 8), 'load', [pltpu.VMEM((units, depth...  3.28 us
    pallas_call x1, Pallas kernels, on_device(): call(functools.partial(product_kernel, len(near), False, True, tokens), '...  2.33 us
    pallas_call x1, Pallas kernels, on_device(): call(functools.partial(product_kernel, 1, True, False, tokens), 'product'...  2.27 us
    pallas_call x1, Pallas kernels, on_device(): call(back_kernel, 'back', [pltpu.VMEM((tokens, units), BF16), pltpu.VMEM(...  1.29 us
    pallas_call x1, Pallas kernels, on_device(): call(functools.partial(pack_kernel, groups, depth), 'pack', [pltpu.VMEM((...  1.24 us
    pallas_call x1, Pallas kernels, on_device(): call(functools.partial(gradient_kernel, groups, rank, share, ride_rows),...  1.19 us
  transfers between devices with their start and end apart: 18, of which 4 were waited for; matrix products, arithmetic and copies ran while one was open for 0% of the time, Pallas kernels for 26%

profile of v2, /device:TPU:0, one launch (start us, length us, event | category | flops | bytes accessed | tf_op | source)
XLA Modules:
  0.0 44.3 jit_solution(18144701558874926833)
XLA Ops:
  0.6 1.2 %pack.1 = (bf16[64,1152]{1,0:T(8,128)(2,1)S(1)}, bf16[64,1152]{1,0:T(8,128)(2,1)S(1)}, bf16[64,1152]{1,0:T(8,128)(2,1)S(1)}, f32[8,128]{1,0:T(8,128)S(1)}, bf16[64,2048]{1,0:T(8,128)(2,1)S(1)}) custom-call(bf16[64,8192]{1,0:T(8,128)(2,1)} %hidden_ref.1, f32[1,4,16]{2,1,0:T(4,128)} %old_hbm.1, f32[1,4]{1,0:T(1,128)} %reward_hbm.1, s32[1,4]{1,0:T(1,128)} %length_hbm.1, ...), custom_call_target="tpu_custom_call" | custom-call | bytes 7569408 | tf_op jit(solution)/shard_map/pack/pallas_call | solution.py:295
  1.9 3.0 %collective-permute-start = (bf16[64,1152]{1,0:T(8,128)(2,1)S(1)}, bf16[64,1152]{1,0:T(8,128)(2,1)S(1)}, u32[]{:S(2)}, u32[]{:S(2)}) collective-permute-start(bf16[64,1152]{1,0:T(8,128)(2,1)S(1)} %get-tuple-element.38), channel_id=1, source_target_pairs={{0,8},{8,0},{16,24},{24,16},{1,9},{9,1},{17,25},{25,17},{2,10},{10... | collective-permute-start | bytes 442376 | tf_op jit(solution)/shard_map/ppermute | solution.py:30
  4.9 1.5 %collective-permute-start.1 = (bf16[64,1152]{1,0:T(8,128)(2,1)S(1)}, bf16[64,1152]{1,0:T(8,128)(2,1)S(1)}, u32[]{:S(2)}, u32[]{:S(2)}) collective-permute-start(bf16[64,1152]{1,0:T(8,128)(2,1)S(1)} %get-tuple-element.39), channel_id=1, source_target_pairs={{0,16},{8,24},{16,0},{24,8},{1,17},{9,25},{17,1},{25,9},{2,18},{10... | collective-permute-start | bytes 442376 | tf_op jit(solution)/shard_map/ppermute | solution.py:30
  6.4 1.3 %back.1 = (bf16[64,1848]{1,0:T(8,128)(2,1)S(1)}, bf16[64,1848]{1,0:T(8,128)(2,1)S(1)}, f32[64,64]{1,0:T(8,128)S(1)}) custom-call(bf16[64,1848]{1,0:T(8,128)(2,1)} %upstream_hbm.1, bf16[64,1848]{1,0:T(8,128)(2,1)} %up_hbm.1), custom_call_target="tpu_custom_call" | custom-call | tf_op jit(solution)/shard_map/back/pallas_call | solution.py:312
  7.7 3.3 %load.1 = (bf16[1848,2048]{1,0:T(8,128)(2,1)S(1)}, bf16[64,2048]{1,0:T(8,128)(2,1)S(1)}, f32[1,4,16]{2,1,0:T(4,128)S(1)}) custom-call(bf16[1848,2048]{1,0:T(8,128)(2,1)} %bitcast.4, bf16[64,2048]{1,0:T(8,128)(2,1)} %bitcast.5, f32[1,4,16]{2,1,0:T(4,128)} %new_hbm.1, f32[64,64]{1,0:T(8,128)S(1)} %get-tuple-element.53.after_ref), custom_call_target="tpu_custom_call" | custom-call | tf_op jit(solution)/shard_map/load/pallas_call | solution.py:319
  11.0 2.3 %collective-permute-done.1.refs_1_.rest_1_.rest_4_ = bf16[64,1152]{1,0:T(8,128)(2,1)S(1)} collective-permute-done((bf16[64,1152]{1,0:T(8,128)(2,1)S(1)}, bf16[64,1152]{1,0:T(8,128)(2,1)S(1)}, u32[]{:S(2)}, u32[]{:S(2)}) %collective-permute-start.1) | collective-permute-done | bytes 147488 | tf_op jit(solution)/shard_map/ppermute | solution.py:30
  13.4 0.5 %collective-permute-start.3 = (bf16[64,1152]{1,0:T(8,128)(2,1)S(1)}, bf16[64,1152]{1,0:T(8,128)(2,1)S(1)}, u32[]{:S(2)}, u32[]{:S(2)}) collective-permute-start(bf16[64,1152]{1,0:T(8,128)(2,1)S(1)} %collective-permute-done.refs_0_.rest_0_.rest_3_), channel_id=1, source_target_pairs={{0,1},{1,0},{2,3},{3,2},{4,5},{5,4},{6,7},{7,6},{8,9},{9,8},{10,11... | collective-permute-start | bytes 442376 | tf_op jit(solution)/shard_map/ppermute | solution.py:30
  13.9 2.6 %collective-permute-start.10 = (f32[64,64]{1,0:T(8,128)S(1)}, f32[64,64]{1,0:T(8,128)S(1)}, u32[]{:S(2)}, u32[]{:S(2)}) collective-permute-start(f32[64,64]{1,0:T(8,128)S(1)} %get-tuple-element.53.after_ref), channel_id=1, source_target_pairs={{0,4},{1,5},{2,6},{3,7},{4,0},{5,1},{6,2},{7,3},{8,12},{9,13},{10,... | collective-permute-start | bytes 49160 | tf_op jit(solution)/shard_map/ppermute | solution.py:30
  16.5 1.3 %collective-permute-start.11 = (f32[64,64]{1,0:T(8,128)S(1)}, f32[64,64]{1,0:T(8,128)S(1)}, u32[]{:S(2)}, u32[]{:S(2)}) collective-permute-start(f32[64,64]{1,0:T(8,128)S(1)} %get-tuple-element.53.after_ref), channel_id=1, source_target_pairs={{0,6},{1,7},{2,4},{3,5},{4,2},{5,3},{6,0},{7,1},{8,14},{9,15},{10,... | collective-permute-start | bytes 49160 | tf_op jit(solution)/shard_map/ppermute | solution.py:30
  18.0 2.3 %product.3 = bf16[64,1976]{1,0:T(8,128)(2,1)S(1)} custom-call(bf16[1848,2048]{1,0:T(8,128)(2,1)S(1)} %get-tuple-element.41.held_ref, bf16[64,2048]{1,0:T(8,128)(2,1)S(1)} %get-tuple-element.42.at_ref, bf16[64,1152]{1,0:T(8,128)(2,1)S(1)} %collective-permute-done.2.rest_2_.refs_0_.rest_5_, bf16[64,1152]{1,0:T(8,128)(2,1)S(1)} %collective-permute-done.7.refs_1_.rest_8_), custom_call_target="tpu_custom_call" | custom-call | flops 484442112 | bytes 7569408 | tf_op jit(solution)/shard_map/product/pallas_call | solution.py:333
  20.3 1.6 %collective-permute-start.8 = (bf16[64,1976]{1,0:T(8,128)(2,1)S(1)}, bf16[64,1976]{1,0:T(8,128)(2,1)S(1)}, u32[]{:S(2)}, u32[]{:S(2)}) collective-permute-start(bf16[64,1976]{1,0:T(8,128)(2,1)S(1)} %product.3), channel_id=1, source_target_pairs={{0,24},{8,16},{16,8},{24,0},{1,25},{9,17},{17,9},{25,1},{2,26},{10... | collective-permute-start | bytes 758792 | tf_op jit(solution)/shard_map/ppermute | solution.py:30
  21.9 2.3 %product.2 = (bf16[64,1848]{1,0:T(8,128)(2,1)S(1)}, bf16[64,1848]{1,0:T(8,128)(2,1)S(1)}, f32[64,1848]{1,0:T(8,128)S(1)}) custom-call(bf16[1848,2048]{1,0:T(8,128)(2,1)S(1)} %get-tuple-element.41.held_ref, bf16[64,2048]{1,0:T(8,128)(2,1)S(1)} %get-tuple-element.42.at_ref, bf16[64,1152]{1,0:T(8,128)(2,1)S(1)} %collective-permute-done.refs_0_.rest_0_.rest_3_, ...), custom_call_target="tpu_custom_call" | custom-call | flops 1937768448 | bytes 7569408 | tf_op jit(solution)/shard_map/product/pallas_call | solution.py:350
  24.2 1.5 %collective-permute-start.13 = (bf16[64,1848]{1,0:T(8,128)(2,1)S(1)}, bf16[64,1848]{1,0:T(8,128)(2,1)S(1)}, u32[]{:S(2)}, u32[]{:S(2)}) collective-permute-start(bf16[64,1848]{1,0:T(8,128)(2,1)S(1)} %get-tuple-element.58), channel_id=1, source_target_pairs={{0,8},{8,0},{16,24},{24,16},{1,9},{9,1},{17,25},{25,17},{2,10},{10... | collective-permute-start | bytes 709640 | tf_op jit(solution)/shard_map/ppermute | solution.py:30
  26.4 0.8 %coef.1 = (f32[64,64]{1,0:T(8,128)S(1)}, f32[64,64]{1,0:T(8,128)S(1)}, f32[64,64]{1,0:T(8,128)S(1)}, f32[64,128]{1,0:T(8,128)S(1)}, f32[1,1]{1,0:T(1,128)}) custom-call(bf16[64,2048]{1,0:T(8,128)(2,1)S(1)} %get-tuple-element.42.at_ref, f32[1,4,16]{2,1,0:T(4,128)S(1)} %get-tuple-element.47.new_ref, f32[8,128]{1,0:T(8,128)S(1)} %get-tuple-element.48.own_table, ...), custom_call_target="tpu_custom_call" | custom-call | tf_op jit(solution)/shard_map/coef/pallas_call | solution.py:342
  27.2 1.2 %collective-permute-start.5 = (f32[64,64]{1,0:T(8,128)S(1)}, f32[64,64]{1,0:T(8,128)S(1)}, u32[]{:S(2)}, u32[]{:S(2)}) collective-permute-start(f32[64,64]{1,0:T(8,128)S(1)} %get-tuple-element.51), channel_id=1, source_target_pairs={{0,8},{8,0},{16,24},{24,16},{1,9},{9,1},{17,25},{25,17},{2,10},{10... | collective-permute-start | bytes 49160 | tf_op jit(solution)/shard_map/ppermute | solution.py:30
  28.4 0.8 %collective-permute-start.6 = (f32[64,64]{1,0:T(8,128)S(1)}, f32[64,64]{1,0:T(8,128)S(1)}, u32[]{:S(2)}, u32[]{:S(2)}) collective-permute-start(f32[64,64]{1,0:T(8,128)S(1)} %get-tuple-element.52), channel_id=1, source_target_pairs={{0,16},{8,24},{16,0},{24,8},{1,17},{9,25},{17,1},{25,9},{2,18},{10... | collective-permute-start | bytes 49160 | tf_op jit(solution)/shard_map/ppermute | solution.py:30
  29.2 6.3 %collective-permute-done.5.refs_1_ = f32[64,64]{1,0:T(8,128)S(1)} collective-permute-done((f32[64,64]{1,0:T(8,128)S(1)}, f32[64,64]{1,0:T(8,128)S(1)}, u32[]{:S(2)}, u32[]{:S(2)}) %collective-permute-start.5) | collective-permute-done | bytes 16416 | tf_op jit(solution)/shard_map/ppermute | solution.py:30
  35.9 1.2 %collective-permute-start.15 = (bf16[16,2104]{1,0:T(8,128)(2,1)S(1)}, bf16[16,2104]{1,0:T(8,128)(2,1)S(1)}, u32[]{:S(2)}, u32[]{:S(2)}) collective-permute-start(bf16[16,2104]{1,0:T(8,128)(2,1)S(1)} %get-tuple-element.62), channel_id=1, source_target_pairs={{0,8},{8,0},{16,24},{24,16},{1,9},{9,1},{17,25},{25,17},{2,10},{10... | collective-permute-start | bytes 201992 | tf_op jit(solution)/shard_map/ppermute | solution.py:30
  37.1 0.8 %collective-permute-start.16 = (bf16[16,2104]{1,0:T(8,128)(2,1)S(1)}, bf16[16,2104]{1,0:T(8,128)(2,1)S(1)}, u32[]{:S(2)}, u32[]{:S(2)}) collective-permute-start(bf16[16,2104]{1,0:T(8,128)(2,1)S(1)} %get-tuple-element.63), channel_id=1, source_target_pairs={{0,16},{8,24},{16,0},{24,8},{1,17},{9,25},{17,1},{25,9},{2,18},{10... | collective-permute-start | bytes 201992 | tf_op jit(solution)/shard_map/ppermute | solution.py:30
  37.9 1.5 %collective-permute-start.17 = (bf16[16,2104]{1,0:T(8,128)(2,1)S(1)}, bf16[16,2104]{1,0:T(8,128)(2,1)S(1)}, u32[]{:S(2)}, u32[]{:S(2)}) collective-permute-start(bf16[16,2104]{1,0:T(8,128)(2,1)S(1)} %get-tuple-element.64), channel_id=1, source_target_pairs={{0,24},{8,16},{16,8},{24,0},{1,25},{9,17},{17,9},{25,1},{2,26},{10... | collective-permute-start | bytes 201992 | tf_op jit(solution)/shard_map/ppermute | solution.py:30
  39.4 1.0 %output.1 = bf16[64,1848]{1,0:T(8,128)(2,1)} custom-call(f32[64,1848]{1,0:T(8,128)S(1)} %get-tuple-element.46.total_ref, bf16[64,64]{1,0:T(8,128)(2,1)S(1)} %get-tuple-element.56.low_ref, bf16[64,1848]{1,0:T(8,128)(2,1)S(1)} %get-tuple-element.57.up_ref, bf16[64,1976]{1,0:T(8,128)(2,1)S(1)} %collective-permute-done.8.refs_3_.far, ...), custom_call_target="tpu_custom_call" | custom-call | tf_op jit(solution)/shard_map/output/pallas_call | solution.py:373
  40.4 1.7 %collective-permute-done.16.rest_1_ = bf16[16,2104]{1,0:T(8,128)(2,1)S(1)} collective-permute-done((bf16[16,2104]{1,0:T(8,128)(2,1)S(1)}, bf16[16,2104]{1,0:T(8,128)(2,1)S(1)}, u32[]{:S(2)}, u32[]{:S(2)}) %collective-permute-start.16) | collective-permute-done | bytes 67360 | tf_op jit(solution)/shard_map/ppermute | solution.py:30
  42.2 1.0 %collective-permute-done.17.rest_2_ = bf16[16,2104]{1,0:T(8,128)(2,1)S(1)} collective-permute-done((bf16[16,2104]{1,0:T(8,128)(2,1)S(1)}, bf16[16,2104]{1,0:T(8,128)(2,1)S(1)}, u32[]{:S(2)}, u32[]{:S(2)}) %collective-permute-start.17) | collective-permute-done | bytes 67360 | tf_op jit(solution)/shard_map/ppermute | solution.py:30
  43.1 1.2 %gradient.1 = (f32[16,1848]{1,0:T(8,128)}, f32[64,2048]{1,0:T(8,128)}) custom-call(f32[16,1848]{1,0:T(8,128)S(1)} %get-tuple-element.60.own_term, bf16[64,64]{1,0:T(8,128)(2,1)S(1)} %get-tuple-element.61.own_back, bf16[64,2048]{1,0:T(8,128)(2,1)S(1)} %get-tuple-element.45.refs_4_.own_hidden, bf16[16,2104]{1,0:T(8,128)(2,1)S(1)} %collective-permute-done.15.rest_0_, ...), custom_call_target="tpu_custom_call" | custom-call | tf_op jit(solution)/shard_map/gradient/pallas_call | solution.py:379
  (22 shorter events, 1.2 us)
Async XLA Ops:
  1.9 9.1 %collective-permute-start = (bf16[64,1152]{1,0:T(8,128)(2,1)S(1)}, bf16[64,1152]{1,0:T(8,128)(2,1)S(1)}, u32[]{:S(2)}, u32[]{:S(2)}) collective-permute-start(bf16[64,1152]{1,0:T(8,128)(2,1)S(1)} %get-tuple-element.38), channel_id=1, source_target_pairs={{0,8},{8,0},{16,24},{24,16},{1,9},{9,1},{17,25},{25,17},{2,10},{10... | collective-permute-start | bytes 442376 | tf_op jit(solution)/shard_map/ppermute | solution.py:30
  4.9 8.5 %collective-permute-start.1 = (bf16[64,1152]{1,0:T(8,128)(2,1)S(1)}, bf16[64,1152]{1,0:T(8,128)(2,1)S(1)}, u32[]{:S(2)}, u32[]{:S(2)}) collective-permute-start(bf16[64,1152]{1,0:T(8,128)(2,1)S(1)} %get-tuple-element.39), channel_id=1, source_target_pairs={{0,16},{8,24},{16,0},{24,8},{1,17},{9,25},{17,1},{25,9},{2,18},{10... | collective-permute-start | bytes 442376 | tf_op jit(solution)/shard_map/ppermute | solution.py:30
  6.4 7.0 %collective-permute-start.2 = (bf16[64,1152]{1,0:T(8,128)(2,1)S(1)}, bf16[64,1152]{1,0:T(8,128)(2,1)S(1)}, u32[]{:S(2)}, u32[]{:S(2)}) collective-permute-start(bf16[64,1152]{1,0:T(8,128)(2,1)S(1)} %get-tuple-element.40), channel_id=1, source_target_pairs={{0,24},{8,16},{16,8},{24,0},{1,25},{9,17},{17,9},{25,1},{2,26},{10... | collective-permute-start | bytes 442376 | tf_op jit(solution)/shard_map/ppermute | solution.py:30
  13.4 4.5 %collective-permute-start.7 = (bf16[64,1152]{1,0:T(8,128)(2,1)S(1)}, bf16[64,1152]{1,0:T(8,128)(2,1)S(1)}, u32[]{:S(2)}, u32[]{:S(2)}) collective-permute-start(bf16[64,1152]{1,0:T(8,128)(2,1)S(1)} %collective-permute-done.2.rest_2_.refs_0_.rest_5_), channel_id=1, source_target_pairs={{0,1},{1,0},{2,3},{3,2},{4,5},{5,4},{6,7},{7,6},{8,9},{9,8},{10,11... | collective-permute-start | bytes 442376 | tf_op jit(solution)/shard_map/ppermute | solution.py:30
  13.4 7.0 %collective-permute-start.3 = (bf16[64,1152]{1,0:T(8,128)(2,1)S(1)}, bf16[64,1152]{1,0:T(8,128)(2,1)S(1)}, u32[]{:S(2)}, u32[]{:S(2)}) collective-permute-start(bf16[64,1152]{1,0:T(8,128)(2,1)S(1)} %collective-permute-done.refs_0_.rest_0_.rest_3_), channel_id=1, source_target_pairs={{0,1},{1,0},{2,3},{3,2},{4,5},{5,4},{6,7},{7,6},{8,9},{9,8},{10,11... | collective-permute-start | bytes 442376 | tf_op jit(solution)/shard_map/ppermute | solution.py:30
  13.9 8.0 %collective-permute-start.4 = (bf16[64,1152]{1,0:T(8,128)(2,1)S(1)}, bf16[64,1152]{1,0:T(8,128)(2,1)S(1)}, u32[]{:S(2)}, u32[]{:S(2)}) collective-permute-start(bf16[64,1152]{1,0:T(8,128)(2,1)S(1)} %collective-permute-done.1.refs_1_.rest_1_.rest_4_), channel_id=1, source_target_pairs={{0,1},{1,0},{2,3},{3,2},{4,5},{5,4},{6,7},{7,6},{8,9},{9,8},{10,11... | collective-permute-start | bytes 442376 | tf_op jit(solution)/shard_map/ppermute | solution.py:30
  13.9 11.9 %collective-permute-start.10 = (f32[64,64]{1,0:T(8,128)S(1)}, f32[64,64]{1,0:T(8,128)S(1)}, u32[]{:S(2)}, u32[]{:S(2)}) collective-permute-start(f32[64,64]{1,0:T(8,128)S(1)} %get-tuple-element.53.after_ref), channel_id=1, source_target_pairs={{0,4},{1,5},{2,6},{3,7},{4,0},{5,1},{6,2},{7,3},{8,12},{9,13},{10,... | collective-permute-start | bytes 49160 | tf_op jit(solution)/shard_map/ppermute | solution.py:30
  16.5 9.8 %collective-permute-start.11 = (f32[64,64]{1,0:T(8,128)S(1)}, f32[64,64]{1,0:T(8,128)S(1)}, u32[]{:S(2)}, u32[]{:S(2)}) collective-permute-start(f32[64,64]{1,0:T(8,128)S(1)} %get-tuple-element.53.after_ref), channel_id=1, source_target_pairs={{0,6},{1,7},{2,4},{3,5},{4,2},{5,3},{6,0},{7,1},{8,14},{9,15},{10,... | collective-permute-start | bytes 49160 | tf_op jit(solution)/shard_map/ppermute | solution.py:30
  17.8 8.5 %collective-permute-start.9 = (f32[64,64]{1,0:T(8,128)S(1)}, f32[64,64]{1,0:T(8,128)S(1)}, u32[]{:S(2)}, u32[]{:S(2)}) collective-permute-start(f32[64,64]{1,0:T(8,128)S(1)} %get-tuple-element.53.after_ref), channel_id=1, source_target_pairs={{0,2},{1,3},{2,0},{3,1},{4,6},{5,7},{6,4},{7,5},{8,10},{9,11},{10,... | collective-permute-start | bytes 49160 | tf_op jit(solution)/shard_map/ppermute | solution.py:30
  20.3 15.2 %collective-permute-start.8 = (bf16[64,1976]{1,0:T(8,128)(2,1)S(1)}, bf16[64,1976]{1,0:T(8,128)(2,1)S(1)}, u32[]{:S(2)}, u32[]{:S(2)}) collective-permute-start(bf16[64,1976]{1,0:T(8,128)(2,1)S(1)} %product.3), channel_id=1, source_target_pairs={{0,24},{8,16},{16,8},{24,0},{1,25},{9,17},{17,9},{25,1},{2,26},{10... | collective-permute-start | bytes 758792 | tf_op jit(solution)/shard_map/ppermute | solution.py:30
  24.2 15.2 %collective-permute-start.13 = (bf16[64,1848]{1,0:T(8,128)(2,1)S(1)}, bf16[64,1848]{1,0:T(8,128)(2,1)S(1)}, u32[]{:S(2)}, u32[]{:S(2)}) collective-permute-start(bf16[64,1848]{1,0:T(8,128)(2,1)S(1)} %get-tuple-element.58), channel_id=1, source_target_pairs={{0,8},{8,0},{16,24},{24,16},{1,9},{9,1},{17,25},{25,17},{2,10},{10... | collective-permute-start | bytes 709640 | tf_op jit(solution)/shard_map/ppermute | solution.py:30
  25.8 13.7 %collective-permute-start.14 = (bf16[64,1848]{1,0:T(8,128)(2,1)S(1)}, bf16[64,1848]{1,0:T(8,128)(2,1)S(1)}, u32[]{:S(2)}, u32[]{:S(2)}) collective-permute-start(bf16[64,1848]{1,0:T(8,128)(2,1)S(1)} %get-tuple-element.59), channel_id=1, source_target_pairs={{0,16},{8,24},{16,0},{24,8},{1,17},{9,25},{17,1},{25,9},{2,18},{10... | collective-permute-start | bytes 709640 | tf_op jit(solution)/shard_map/ppermute | solution.py:30
  26.3 2.1 %collective-permute-start.12 = (f32[64,64]{1,0:T(8,128)S(1)}, f32[64,64]{1,0:T(8,128)S(1)}, u32[]{:S(2)}, u32[]{:S(2)}) collective-permute-start(f32[64,64]{1,0:T(8,128)S(1)} %add_add_fusion.refs_4_), channel_id=1, source_target_pairs={{0,1},{1,0},{2,3},{3,2},{4,5},{5,4},{6,7},{7,6},{8,9},{9,8},{10,11... | collective-permute-start | bytes 49160 | tf_op jit(solution)/shard_map/ppermute | solution.py:30
  27.2 8.3 %collective-permute-start.5 = (f32[64,64]{1,0:T(8,128)S(1)}, f32[64,64]{1,0:T(8,128)S(1)}, u32[]{:S(2)}, u32[]{:S(2)}) collective-permute-start(f32[64,64]{1,0:T(8,128)S(1)} %get-tuple-element.51), channel_id=1, source_target_pairs={{0,8},{8,0},{16,24},{24,16},{1,9},{9,1},{17,25},{25,17},{2,10},{10... | collective-permute-start | bytes 49160 | tf_op jit(solution)/shard_map/ppermute | solution.py:30
  28.4 7.1 %collective-permute-start.6 = (f32[64,64]{1,0:T(8,128)S(1)}, f32[64,64]{1,0:T(8,128)S(1)}, u32[]{:S(2)}, u32[]{:S(2)}) collective-permute-start(f32[64,64]{1,0:T(8,128)S(1)} %get-tuple-element.52), channel_id=1, source_target_pairs={{0,16},{8,24},{16,0},{24,8},{1,17},{9,25},{17,1},{25,9},{2,18},{10... | collective-permute-start | bytes 49160 | tf_op jit(solution)/shard_map/ppermute | solution.py:30
  35.9 4.5 %collective-permute-start.15 = (bf16[16,2104]{1,0:T(8,128)(2,1)S(1)}, bf16[16,2104]{1,0:T(8,128)(2,1)S(1)}, u32[]{:S(2)}, u32[]{:S(2)}) collective-permute-start(bf16[16,2104]{1,0:T(8,128)(2,1)S(1)} %get-tuple-element.62), channel_id=1, source_target_pairs={{0,8},{8,0},{16,24},{24,16},{1,9},{9,1},{17,25},{25,17},{2,10},{10... | collective-permute-start | bytes 201992 | tf_op jit(solution)/shard_map/ppermute | solution.py:30
  37.1 5.1 %collective-permute-start.16 = (bf16[16,2104]{1,0:T(8,128)(2,1)S(1)}, bf16[16,2104]{1,0:T(8,128)(2,1)S(1)}, u32[]{:S(2)}, u32[]{:S(2)}) collective-permute-start(bf16[16,2104]{1,0:T(8,128)(2,1)S(1)} %get-tuple-element.63), channel_id=1, source_target_pairs={{0,16},{8,24},{16,0},{24,8},{1,17},{9,25},{17,1},{25,9},{2,18},{10... | collective-permute-start | bytes 201992 | tf_op jit(solution)/shard_map/ppermute | solution.py:30
  37.9 5.2 %collective-permute-start.17 = (bf16[16,2104]{1,0:T(8,128)(2,1)S(1)}, bf16[16,2104]{1,0:T(8,128)(2,1)S(1)}, u32[]{:S(2)}, u32[]{:S(2)}) collective-permute-start(bf16[16,2104]{1,0:T(8,128)(2,1)S(1)} %get-tuple-element.64), channel_id=1, source_target_pairs={{0,24},{8,16},{16,8},{24,0},{1,25},{9,17},{17,9},{25,1},{2,26},{10... | collective-permute-start | bytes 201992 | tf_op jit(solution)/shard_map/ppermute | solution.py:30

commit v3 on v2

--- a/solution.py
+++ b/solution.py
@@ -16,6 +16,7 @@
 BF16 = jnp.bfloat16
 LANES = 128
 BLOCK = 8
+PEAK_FLOPS, PEAK_BYTES = 1.15e9, 3.6e6
 STEP = 512
 NT = (((1,), (1,)), ((), ()))
 TN = (((0,), (0,)), ((), ()))
@@ -30,26 +31,33 @@
     return lax.ppermute(array, axis, [(i, i ^ distance) for i in range(size)])
 
 
-def sum_over_pairs(partial):
+def halves_over_fsdp(partial):
     size = lax.axis_size("fsdp")
     if size & (size - 1):
-        same = [[i for i in range(size) if i % 2 == r] for r in range(2)]
-        return lax.psum(partial, "fsdp", axis_index_groups=same)
-    parts = [partial] + [swap(partial, "fsdp", d) for d in range(2, size, 2)]
-    while len(parts) > 1:
-        parts = [parts[i] + parts[i + 1] for i in range(0, len(parts), 2)]
-    return parts[0]
-
-
-def call(body, name, outs, ins, out_specs=None, scratch=(), limit=8, flops=0, moved=0):
+        total = lax.psum(partial, "fsdp")
+        return total, jnp.zeros_like(total)
+    distance = 1
+    while distance < size // 2:
+        partial = partial + swap(partial, "fsdp", distance)
+        distance *= 2
+    return partial, swap(partial, "fsdp", distance)
+
+
+def after(array, earlier):
+    return lax.optimization_barrier((array, earlier))[0]
+
+
+def call(body, name, cost, outs, ins, scratch=()):
     return pl.pallas_call(
         body,
         out_shape=outs,
         in_specs=ins,
-        out_specs=[VMEM] * len(outs) if out_specs is None else out_specs,
+        out_specs=[VMEM] * len(outs),
         scratch_shapes=scratch,
-        compiler_params=pltpu.CompilerParams(vmem_limit_bytes=limit << 20),
-        cost_estimate=pl.CostEstimate(flops=flops, bytes_accessed=moved, transcendentals=0),
+        compiler_params=pltpu.CompilerParams(vmem_limit_bytes=8 << 20),
+        cost_estimate=pl.CostEstimate(
+            flops=int(cost * PEAK_FLOPS), bytes_accessed=int(cost * PEAK_BYTES), transcendentals=0
+        ),
         name=name,
     )
 
@@ -63,21 +71,29 @@
     return own, member, lax.rem(member, 2)
 
 
-def pack_kernel(groups, depth, hidden_ref, old_hbm, reward_hbm, length_hbm, dest_hbm, *rest):
+def start_all(pairs, sems, first=0):
+    copies = [pltpu.make_async_copy(a, b, sems.at[first + i]) for i, (a, b) in enumerate(pairs)]
+    for copy in copies:
+        copy.start()
+    return copies
+
+
+def pack_kernel(groups, depth, hidden_ref, old_hbm, reward_hbm, length_hbm, dest_hbm, new_hbm, at_hbm, upstream_hbm, up_hbm, *rest):
     messages, own_table, own_hidden = rest[: groups - 1], rest[groups - 1], rest[groups]
-    old_ref, reward_ref, length_ref, dest_ref, sems, small_sems = rest[groups + 1 :]
+    new_ref, at_ref, upstream_ref, up_ref, back_ref = rest[groups + 1 : groups + 6]
+    old_ref, reward_ref, length_ref, dest_ref, sems, small_sems = rest[groups + 6 :]
     own, _, core = positions()
     half = depth // 2
-    copies = []
+    small = start_all(
+        [(old_hbm, old_ref), (reward_hbm, reward_ref), (length_hbm, length_ref), (dest_hbm, dest_ref)], small_sems
+    )
+    small += start_all([(upstream_hbm, upstream_ref), (up_hbm, up_ref)], small_sems, 4)
+    pairs = []
     for d in reversed(range(1, groups)):
         start = pl.multiple_of((own ^ d) * depth + core * half, LANES)
-        copies.append((hidden_ref.at[:, pl.ds(start, half)], messages[d - 1].at[:, :half]))
-    copies.append((hidden_ref.at[:, pl.ds(pl.multiple_of(own * depth, LANES), depth)], own_hidden))
-    copies = [pltpu.make_async_copy(a, b, sems.at[i]) for i, (a, b) in enumerate(copies)]
-    small = ((old_hbm, old_ref), (reward_hbm, reward_ref), (length_hbm, length_ref), (dest_hbm, dest_ref))
-    small = [pltpu.make_async_copy(a, b, small_sems.at[i]) for i, (a, b) in enumerate(small)]
-    for copy in small + copies:
-        copy.start()
+        pairs.append((hidden_ref.at[:, pl.ds(start, half)], messages[d - 1].at[:, :half]))
+    pairs.append((hidden_ref.at[:, pl.ds(pl.multiple_of(own * depth, LANES), depth)], own_hidden))
+    copies = start_all(pairs + [(new_hbm, new_ref), (at_hbm, at_ref)], sems)
     for copy in small:
         copy.wait()
     total, squares = jnp.float32(0), jnp.float32(0)
@@ -104,28 +120,7 @@
             value = value - terms[-1]
         terms = jnp.concatenate(terms + [jnp.zeros((BLOCK, LANES), F32)], axis=0)
         messages[d - 1][: 4 * BLOCK, half:] = terms.astype(BF16)
-    for copy in copies:
-        copy.wait()
-
-
-def back_kernel(upstream_hbm, up_hbm, upstream_ref, up_ref, back_ref, sems):
-    pairs = ((upstream_hbm, upstream_ref), (up_hbm, up_ref))
-    copies = [pltpu.make_async_copy(a, b, sems.at[i]) for i, (a, b) in enumerate(pairs)]
-    for copy in copies:
-        copy.start()
-    for copy in copies:
-        copy.wait()
     back_ref[...] = lax.dot_general(upstream_ref[...], up_ref[...], NT, preferred_element_type=F32)
-
-
-def load_kernel(pieces, weight_hbm, at_hbm, new_hbm, after_ref, weight_ref, at_ref, new_ref, sems):
-    size = weight_ref.shape[0] // 8 // pieces * 8
-    starts = [i * size for i in range(pieces)] + [weight_ref.shape[0]]
-    pairs = [(weight_hbm.at[a:b], weight_ref.at[a:b]) for a, b in zip(starts[:-1], starts[1:])]
-    pairs += [(at_hbm, at_ref), (new_hbm, new_ref)]
-    copies = [pltpu.make_async_copy(a, b, sems.at[i]) for i, (a, b) in enumerate(pairs)]
-    for copy in copies:
-        copy.start()
     for copy in copies:
         copy.wait()
 
@@ -141,29 +136,32 @@
     return jnp.concatenate([high, value - high], axis=1).astype(BF16)
 
 
-def product_kernel(count, with_low, with_own, tokens, held_ref, at_ref, *refs):
-    core = positions()[2]
+def far_kernel(held_ref, at_ref, message, other, result_ref):
     units, depth = held_ref.shape
-    parts = [whole_rows(depth // 2, core, refs[i], refs[count + i]) for i in range(count)]
-    refs = refs[2 * count :]
-    if with_own:
-        parts.append(refs[0][...])
-        refs = refs[1:]
-    rows = jnp.concatenate(parts, axis=0)
-    lead = 0
-    if with_low:
-        low = lax.dot_general(rows, at_ref[...], NT, preferred_element_type=F32)
-        lead = 2 * low.shape[1]
-        refs[0][:, :lead] = two_terms(low)
+    rows = whole_rows(depth // 2, positions()[2], message, other)
+    low = lax.dot_general(rows, at_ref[...], NT, preferred_element_type=F32)
+    lead = 2 * low.shape[1]
+    result_ref[:, :lead] = two_terms(low)
     rows = rows.T
     for start in range(0, units, STEP):
         end = min(start + STEP, units)
         result = jnp.dot(held_ref[start:end], rows, preferred_element_type=F32).T
-        for i, ref in enumerate(refs):
-            ref[:, lead + start : lead + end] = result[i * tokens : (i + 1) * tokens].astype(ref.dtype)
-
-
-def coef_kernel(groups, half, near, at_ref, new_ref, own_table, own_hidden, *rest):
+        result_ref[:, lead + start : lead + end] = result.astype(BF16)
+
+
+def near_kernel(count, tokens, held_ref, early, later, *refs):
+    units, depth = held_ref.shape
+    core = positions()[2]
+    parts = [whole_rows(depth // 2, core, refs[i], refs[count + i]) for i in range(count)] + [refs[2 * count][...]]
+    rows = jnp.concatenate(parts, axis=0).T
+    for start in range(0, units, STEP):
+        end = min(start + STEP, units)
+        result = jnp.dot(held_ref[start:end], rows, preferred_element_type=F32).T
+        for i, ref in enumerate(refs[2 * count + 1 :]):
+            ref[:, start:end] = result[i * tokens : (i + 1) * tokens].astype(ref.dtype)
+
+
+def coef_kernel(groups, half, near, earlier, at_ref, new_ref, own_table, own_hidden, *rest):
     messages, others = rest[: groups - 1], rest[groups - 1 : groups - 1 + near]
     outs = rest[groups - 1 + near :]
     lows, coef_ref, loss_ref = outs[: near + 1], outs[near + 1], outs[near + 2]
@@ -292,69 +290,75 @@
     others = range(1, groups)
     at, weight = adapter_a.T, base_weight.T
 
-    *messages, own_table, own_hidden = call(
+    *messages, own_table, own_hidden, new, at, upstream, up, back = call(
         functools.partial(pack_kernel, groups, depth),
         "pack",
+        1.8,
         [pltpu.VMEM((tokens, half + LANES), BF16)] * (groups - 1)
-        + [pltpu.VMEM((BLOCK, LANES), F32), pltpu.VMEM((tokens, depth), BF16)],
-        [HBM] * 5,
+        + [
+            pltpu.VMEM((BLOCK, LANES), F32),
+            pltpu.VMEM((tokens, depth), BF16),
+            pltpu.VMEM(logp_new.shape, F32),
+            pltpu.VMEM((rank, depth), BF16),
+            pltpu.VMEM((tokens, units), BF16),
+            pltpu.VMEM((rank, units), BF16),
+            pltpu.VMEM((tokens, rank), F32),
+        ],
+        [HBM] * 9,
         scratch=[
             pltpu.VMEM(logp_old.shape, F32),
             pltpu.SMEM(rewards.shape, F32),
             pltpu.SMEM(comp_lengths.shape, jnp.int32),
             pltpu.SMEM(assignment.shape, jnp.int32),
-            pltpu.SemaphoreType.DMA((groups,)),
-            pltpu.SemaphoreType.DMA((4,)),
+            pltpu.SemaphoreType.DMA((groups + 2,)),
+            pltpu.SemaphoreType.DMA((6,)),
         ],
-        moved=2 * units * depth,
-    )(*map(in_hbm, (hidden_input_slots, logp_old, rewards, comp_lengths, assignment)))
+    )(
+        *map(
+            in_hbm,
+            (
+                hidden_input_slots,
+                logp_old,
+                rewards,
+                comp_lengths,
+                assignment,
+                logp_new,
+                at,
+                upstream,
+                adapter_up_matrix,
+            ),
+        )
+    )
     got = {d: swap(messages[d - 1], "group", d) for d in reversed(others)}
-    upstream, up, back = call(
-        back_kernel,
-        "back",
-        [pltpu.VMEM((tokens, units), BF16), pltpu.VMEM((rank, units), BF16), pltpu.VMEM((tokens, rank), F32)],
-        [HBM] * 2,
-        scratch=[pltpu.SemaphoreType.DMA((2,))],
-    )(*map(in_hbm, (upstream, adapter_up_matrix)))
-    weight, at, new = call(
-        functools.partial(load_kernel, 8),
-        "load",
-        [pltpu.VMEM((units, depth), BF16), pltpu.VMEM((rank, depth), BF16), pltpu.VMEM(logp_new.shape, F32)],
-        [HBM] * 3 + [ANY],
-        scratch=[pltpu.SemaphoreType.DMA((10,))],
-    )(*map(in_hbm, (weight, at, logp_new)), back)
-    weight, back, got = lax.optimization_barrier((weight, back, got))
-    back = sum_over_pairs(back)
-    theirs = {d: swap(got[d], "fsdp", 1) for d in reversed(others)}
-
+    held = pltpu.with_memory_space_constraint(weight, pltpu.VMEM)
     far, near = groups - 1, list(range(1, groups - 1))
+    early, last = halves_over_fsdp(back)
+    theirs = {far: swap(after(got[far], early), "fsdp", 1)}
+
     lead = 2 * rank
     came = {}
-    (result,) = call(
-        functools.partial(product_kernel, 1, True, False, tokens),
-        "product",
-        [pltpu.VMEM((tokens, lead + units), BF16)],
-        [VMEM] * 4,
-        flops=2 * units * tokens * depth,
-        moved=units * depth * 2,
-    )(weight, at, got[far], theirs[far])
+    (result,) = call(far_kernel, "far", 2.3, [pltpu.VMEM((tokens, lead + units), BF16)], [VMEM] * 4)(
+        held, at, got[far], theirs[far]
+    )
     came[far] = swap(result, "group", far)
+    for d in near:
+        theirs[d] = swap(got[d], "fsdp", 1)
     *lows, coef, loss = call(
         functools.partial(coef_kernel, groups, half, len(near)),
         "coef",
+        0.8,
         [pltpu.VMEM((tokens, rank), F32)] * (len(near) + 1)
         + [pltpu.VMEM((tokens, LANES), F32), jax.ShapeDtypeStruct((1, 1), F32)],
-        [VMEM] * (3 + groups + len(near)),
-    )(at, new, own_table, own_hidden, *[got[d] for d in others], *[theirs[d] for d in near])
+        [ANY] + [VMEM] * (3 + groups + len(near)),
+    )(result, at, new, own_table, own_hidden, *[got[d] for d in others], *[theirs[d] for d in near])
     low_terms = [lows[0]] + [swap(low, "group", d) for d, low in zip(near, lows[1:])]
     *results, kept = call(
-        functools.partial(product_kernel, len(near), False, True, tokens),
-        "product",
+        functools.partial(near_kernel, len(near), tokens),
+        "near",
+        2.4,
         [pltpu.VMEM((tokens, units), BF16)] * len(near) + [pltpu.VMEM((tokens, units), F32)],
-        [VMEM] * (3 + 2 * len(near)),
-        flops=2 * units * tokens * depth * groups,
-        moved=units * depth * 2,
-    )(weight, at, *[got[d] for d in near], *[theirs[d] for d in near], own_hidden)
+        [VMEM, ANY, ANY] + [VMEM] * (1 + 2 * len(near)),
+    )(held, last, coef, *[got[d] for d in near], *[theirs[d] for d in near], own_hidden)
     for d, result in zip(near, results):
         came[d] = swap(result, "group", d)
 
@@ -364,21 +368,24 @@
     *pieces, own_term, own_back, low = call(
         functools.partial(adapter_kernel, groups, share, ride_rows),
         "adapter",
+        4.0,
         [pltpu.VMEM((ride_rows, lanes + units), BF16)] * (groups - 1)
         + [pltpu.VMEM((share, units), F32), pltpu.VMEM((tokens, rank), BF16), pltpu.VMEM((tokens, rank), BF16)],
         [VMEM] * (groups + 4),
         scratch=[pltpu.VMEM((rank, units), F32)],
-    )(*low_terms, came[far], back, swap(back, "fsdp", 1), coef, upstream)
+    )(*low_terms, came[far], early, last, coef, upstream)
     arrived = {d: swap(pieces[d - 1], "group", d) for d in reversed(others)}
     (projection_output,) = call(
         functools.partial(output_kernel, lead),
         "output",
+        1.0,
         [jax.ShapeDtypeStruct((tokens, units), BF16)],
         [VMEM] * (4 + len(near)),
     )(kept, low, up, came[far], *[came[d] for d in near])
     gradient_up, gradient_down = call(
         functools.partial(gradient_kernel, groups, rank, share, ride_rows),
         "gradient",
+        1.2,
         [jax.ShapeDtypeStruct((share, units), F32), jax.ShapeDtypeStruct((rank, depth), F32)],
         [VMEM] * (3 * groups),
     )(

time: 44.5 us -> 37.4 us (0.84)
  Pallas kernels: 13.7 us -> 9.73 us
  waiting for transfers between devices: 11.4 us -> 8.35 us
    pallas_call x7 -> x5, Pallas kernels: 12.2 us -> 8.18 us  [the longest x1 2.33 us: on_device(): call(functools.partial(near_kernel, len(near), tokens), 'near', 2.4, [plt...]
    ppermute x18 -> x17, waiting for transfers between devices: 11.4 us -> 8.35 us  [swap(): return lax.ppermute(array, axis, [(i, i ^ distance) for i in range(size)])]
    ppermute x18 -> x17, starting transfers between devices: 18.5 us -> 18.5 us  [swap(): return lax.ppermute(array, axis, [(i, i ^ distance) for i in range(size)])]
  transfers between devices with their start and end apart: 18 -> 17, of which waited for: 4 -> 10; matrix products, arithmetic and copies ran while one was open for 0% -> 0% of each run, Pallas kernels for 26% -> 18%
where the time goes in v3:
time: 37.4 us; the launch traced here: 37.3 us
  starting transfers between devices  18.5 us (49%)
  Pallas kernels  9.73 us (26%)
  waiting for transfers between devices  8.35 us (22%)
  between operations  0.7 us (2%)
    ppermute x17, starting transfers between devices, swap(): return lax.ppermute(array, axis, [(i, i ^ distance) for i in range(size)])  18.5 us
    ppermute x17, waiting for transfers between devices, swap(): return lax.ppermute(array, axis, [(i, i ^ distance) for i in range(size)])  8.35 us
    pallas_call x1, Pallas kernels, on_device(): call(functools.partial(near_kernel, len(near), tokens), 'near', 2.4, [plt...  2.33 us
    pallas_call x1, Pallas kernels, on_device(): call(far_kernel, 'far', 2.3, [pltpu.VMEM((tokens, lead + units), BF16)],...  2.27 us
    pallas_call x1, Pallas kernels, on_device(): call(functools.partial(pack_kernel, groups, depth), 'pack', 1.8, [pltpu.V...  1.81 us
    pallas_call x1, Pallas kernels, on_device(): call(functools.partial(gradient_kernel, groups, rank, share, ride_rows),...  1.19 us
    pallas_call x1, Pallas kernels, on_device(): call(functools.partial(output_kernel, lead), 'output', 1.0, [jax.ShapeDty...  0.97 us
    pallas_call x1, Pallas kernels, on_device(): call(functools.partial(coef_kernel, groups, half, len(near)), 'coef', 0.8...  0.8 us
  transfers between devices with their start and end apart: 17, of which 10 were waited for; matrix products, arithmetic and copies ran while one was open for 0% of the time, Pallas kernels for 18%

profile of v3, /device:TPU:0, one launch (start us, length us, event | category | flops | bytes accessed | tf_op | source)
XLA Modules:
  0.0 37.3 jit_solution(10119498802371885205)
XLA Ops:
  0.6 1.8 %pack.1 = (bf16[64,1152]{1,0:T(8,128)(2,1)S(1)}, bf16[64,1152]{1,0:T(8,128)(2,1)S(1)}, bf16[64,1152]{1,0:T(8,128)(2,1)S(1)}, f32[8,128]{1,0:T(8,128)S(1)}, bf16[...) custom-call(bf16[64,8192]{1,0:T(8,128)(2,1)} %hidden_ref.1, ...), custom_call_target="tpu_custom_call" | custom-call | flops 2070000000 | bytes 6480000 | tf_op jit(solution)/shard_map/pack/pallas_call | solution.py:293
  2.5 4.0 %collective-permute-start.3 = (bf16[64,1152]{1,0:T(8,128)(2,1)S(1)}, bf16[64,1152]{1,0:T(8,128)(2,1)S(1)}, u32[]{:S(2)}, u32[]{:S(2)}) collective-permute-start(bf16[64,1152]{1,0:T(8,128)(2,1)S(1)} %get-tuple-element.33), channel_id=1, source_target_pairs={{0,24},{8,16},{16,8},{24,0},{1,25},{9,17},{17,9},{25,1},{2,26},{10... | collective-permute-start | bytes 442376 | tf_op jit(solution)/shard_map/ppermute | solution.py:31
  6.4 1.2 %collective-permute-done = f32[64,64]{1,0:T(8,128)S(1)} collective-permute-done((f32[64,64]{1,0:T(8,128)S(1)}, f32[64,64]{1,0:T(8,128)S(1)}, u32[]{:S(2)}, u32[]{:S(2)}) %collective-permute-start) | collective-permute-done | bytes 16416 | tf_op jit(solution)/shard_map/ppermute | solution.py:31
  7.6 1.6 %collective-permute-start.1 = (f32[64,64]{1,0:T(8,128)S(1)}, f32[64,64]{1,0:T(8,128)S(1)}, u32[]{:S(2)}, u32[]{:S(2)}) collective-permute-start(f32[64,64]{1,0:T(8,128)S(1)} %add.6), channel_id=1, source_target_pairs={{0,2},{1,3},{2,0},{3,1},{4,6},{5,7},{6,4},{7,5},{8,10},{9,11},{10,... | collective-permute-start | bytes 49160 | tf_op jit(solution)/shard_map/ppermute | solution.py:31
  10.3 1.3 %collective-permute-done.1 = f32[64,64]{1,0:T(8,128)S(1)} collective-permute-done((f32[64,64]{1,0:T(8,128)S(1)}, f32[64,64]{1,0:T(8,128)S(1)}, u32[]{:S(2)}, u32[]{:S(2)}) %collective-permute-start.1) | collective-permute-done | bytes 16416 | tf_op jit(solution)/shard_map/ppermute | solution.py:31
  11.6 2.7 %collective-permute-start.2 = (f32[64,64]{1,0:T(8,128)S(1)}, f32[64,64]{1,0:T(8,128)S(1)}, u32[]{:S(2)}, u32[]{:S(2)}) collective-permute-start(f32[64,64]{1,0:T(8,128)S(1)} %add.7.refs_4_), channel_id=1, source_target_pairs={{0,4},{1,5},{2,6},{3,7},{4,0},{5,1},{6,2},{7,3},{8,12},{9,13},{10,... | collective-permute-start | bytes 49160 | tf_op jit(solution)/shard_map/ppermute | solution.py:31
  14.3 0.6 %collective-permute-done.5.rest_0_.refs_0_.rest_3_ = bf16[64,1152]{1,0:T(8,128)(2,1)S(1)} collective-permute-done((bf16[64,1152]{1,0:T(8,128)(2,1)S(1)}, bf16[64,1152]{1,0:T(8,128)(2,1)S(1)}, u32[]{:S(2)}, u32[]{:S(2)}) %collective-permute-start.5) | collective-permute-done | bytes 147488 | tf_op jit(solution)/shard_map/ppermute | solution.py:31
  15.4 2.3 %far.1.earlier = bf16[64,1976]{1,0:T(8,128)(2,1)S(1)} custom-call(bf16[1848,2048]{1,0:T(8,128)(2,1)S(1)} %bitcast.4, bf16[64,2048]{1,0:T(8,128)(2,1)S(1)} %get-tuple-element.32.at_ref, bf16[64,1152]{1,0:T(8,128)(2,1)S(1)} %collective-permute-done.3.message.rest_2_.rest_5_, bf16[64,1152]{1,0:T(8,128)(2,1)S(1)} %collective-permute-done.4.other.rest_8_), custom_call_target="tpu_custom_call" | custom-call | flops 2644999936 | bytes 8279999 | tf_op jit(solution)/shard_map/far/pallas_call | solution.py:340
  17.6 1.2 %collective-permute-start.11 = (bf16[64,1976]{1,0:T(8,128)(2,1)S(1)}, bf16[64,1976]{1,0:T(8,128)(2,1)S(1)}, u32[]{:S(2)}, u32[]{:S(2)}) collective-permute-start(bf16[64,1976]{1,0:T(8,128)(2,1)S(1)} %far.1.earlier), channel_id=1, source_target_pairs={{0,24},{8,16},{16,8},{24,0},{1,25},{9,17},{17,9},{25,1},{2,26},{10... | collective-permute-start | bytes 758792 | tf_op jit(solution)/shard_map/ppermute | solution.py:31
  18.9 0.8 %coef.1 = (f32[64,64]{1,0:T(8,128)S(1)}, f32[64,64]{1,0:T(8,128)S(1)}, f32[64,64]{1,0:T(8,128)S(1)}, f32[64,128]{1,0:T(8,128)S(1)}, f32[1,1]{1,0:T(1,128)}) custom-call(bf16[64,1976]{1,0:T(8,128)(2,1)S(1)} %far.1.earlier, bf16[64,2048]{1,0:T(8,128)(2,1)S(1)} %get-tuple-element.32.at_ref, f32[1,4,16]{2,1,0:T(4,128)S(1)} %get-tuple-element.35.new_ref, ...), custom_call_target="tpu_custom_call" | custom-call | flops 920000000 | bytes 2880000 | tf_op jit(solution)/shard_map/coef/pallas_call | solution.py:346
  19.7 0.8 %collective-permute-start.9 = (f32[64,64]{1,0:T(8,128)S(1)}, f32[64,64]{1,0:T(8,128)S(1)}, u32[]{:S(2)}, u32[]{:S(2)}) collective-permute-start(f32[64,64]{1,0:T(8,128)S(1)} %get-tuple-element.43), channel_id=1, source_target_pairs={{0,8},{8,0},{16,24},{24,16},{1,9},{9,1},{17,25},{25,17},{2,10},{10... | collective-permute-start | bytes 49160 | tf_op jit(solution)/shard_map/ppermute | solution.py:31
  20.5 1.5 %collective-permute-start.10 = (f32[64,64]{1,0:T(8,128)S(1)}, f32[64,64]{1,0:T(8,128)S(1)}, u32[]{:S(2)}, u32[]{:S(2)}) collective-permute-start(f32[64,64]{1,0:T(8,128)S(1)} %get-tuple-element.44), channel_id=1, source_target_pairs={{0,16},{8,24},{16,0},{24,8},{1,17},{9,25},{17,1},{25,9},{2,18},{10... | collective-permute-start | bytes 49160 | tf_op jit(solution)/shard_map/ppermute | solution.py:31
  22.0 2.3 %near.1 = (bf16[64,1848]{1,0:T(8,128)(2,1)S(1)}, bf16[64,1848]{1,0:T(8,128)(2,1)S(1)}, f32[64,1848]{1,0:T(8,128)S(1)}) custom-call(bf16[1848,2048]{1,0:T(8,128)(2,1)S(1)} %bitcast.5, f32[64,64]{1,0:T(8,128)S(1)} %collective-permute-done.2.early.refs_5_, f32[64,128]{1,0:T(8,128)S(1)} %get-tuple-element.40.later.refs_6_, ...), custom_call_target="tpu_custom_call" | custom-call | flops 2760000000 | bytes 8640000 | tf_op jit(solution)/shard_map/near/pallas_call | solution.py:355
  24.3 1.3 %collective-permute-start.12 = (bf16[64,1848]{1,0:T(8,128)(2,1)S(1)}, bf16[64,1848]{1,0:T(8,128)(2,1)S(1)}, u32[]{:S(2)}, u32[]{:S(2)}) collective-permute-start(bf16[64,1848]{1,0:T(8,128)(2,1)S(1)} %get-tuple-element.48), channel_id=1, source_target_pairs={{0,8},{8,0},{16,24},{24,16},{1,9},{9,1},{17,25},{25,17},{2,10},{10... | collective-permute-start | bytes 709640 | tf_op jit(solution)/shard_map/ppermute | solution.py:31
  26.1 1.1 %collective-permute-done.9.refs_1_ = f32[64,64]{1,0:T(8,128)S(1)} collective-permute-done((f32[64,64]{1,0:T(8,128)S(1)}, f32[64,64]{1,0:T(8,128)S(1)}, u32[]{:S(2)}, u32[]{:S(2)}) %collective-permute-start.9) | collective-permute-done | bytes 16416 | tf_op jit(solution)/shard_map/ppermute | solution.py:31
  27.3 0.6 %collective-permute-done.10.refs_2_ = f32[64,64]{1,0:T(8,128)S(1)} collective-permute-done((f32[64,64]{1,0:T(8,128)S(1)}, f32[64,64]{1,0:T(8,128)S(1)}, u32[]{:S(2)}, u32[]{:S(2)}) %collective-permute-start.10) | collective-permute-done | bytes 16416 | tf_op jit(solution)/shard_map/ppermute | solution.py:31
  28.2 1.6 %collective-permute-start.14 = (bf16[16,2104]{1,0:T(8,128)(2,1)S(1)}, bf16[16,2104]{1,0:T(8,128)(2,1)S(1)}, u32[]{:S(2)}, u32[]{:S(2)}) collective-permute-start(bf16[16,2104]{1,0:T(8,128)(2,1)S(1)} %get-tuple-element.52), channel_id=1, source_target_pairs={{0,8},{8,0},{16,24},{24,16},{1,9},{9,1},{17,25},{25,17},{2,10},{10... | collective-permute-start | bytes 201992 | tf_op jit(solution)/shard_map/ppermute | solution.py:31
  29.8 0.9 %collective-permute-start.15 = (bf16[16,2104]{1,0:T(8,128)(2,1)S(1)}, bf16[16,2104]{1,0:T(8,128)(2,1)S(1)}, u32[]{:S(2)}, u32[]{:S(2)}) collective-permute-start(bf16[16,2104]{1,0:T(8,128)(2,1)S(1)} %get-tuple-element.53), channel_id=1, source_target_pairs={{0,16},{8,24},{16,0},{24,8},{1,17},{9,25},{17,1},{25,9},{2,18},{10... | collective-permute-start | bytes 201992 | tf_op jit(solution)/shard_map/ppermute | solution.py:31
  30.7 1.1 %collective-permute-start.16 = (bf16[16,2104]{1,0:T(8,128)(2,1)S(1)}, bf16[16,2104]{1,0:T(8,128)(2,1)S(1)}, u32[]{:S(2)}, u32[]{:S(2)}) collective-permute-start(bf16[16,2104]{1,0:T(8,128)(2,1)S(1)} %get-tuple-element.54), channel_id=1, source_target_pairs={{0,24},{8,16},{16,8},{24,0},{1,25},{9,17},{17,9},{25,1},{2,26},{10... | collective-permute-start | bytes 201992 | tf_op jit(solution)/shard_map/ppermute | solution.py:31
  31.8 1.1 %collective-permute-done.12.rest_0_ = bf16[64,1848]{1,0:T(8,128)(2,1)S(1)} collective-permute-done((bf16[64,1848]{1,0:T(8,128)(2,1)S(1)}, bf16[64,1848]{1,0:T(8,128)(2,1)S(1)}, u32[]{:S(2)}, u32[]{:S(2)}) %collective-permute-start.12) | collective-permute-done | bytes 236576 | tf_op jit(solution)/shard_map/ppermute | solution.py:31
  32.9 0.9 %collective-permute-done.13.rest_1_ = bf16[64,1848]{1,0:T(8,128)(2,1)S(1)} collective-permute-done((bf16[64,1848]{1,0:T(8,128)(2,1)S(1)}, bf16[64,1848]{1,0:T(8,128)(2,1)S(1)}, u32[]{:S(2)}, u32[]{:S(2)}) %collective-permute-start.13) | collective-permute-done | bytes 236576 | tf_op jit(solution)/shard_map/ppermute | solution.py:31
  33.8 1.0 %output.1 = bf16[64,1848]{1,0:T(8,128)(2,1)} custom-call(f32[64,1848]{1,0:T(8,128)S(1)} %get-tuple-element.41.total_ref, bf16[64,64]{1,0:T(8,128)(2,1)S(1)} %get-tuple-element.46.low_ref, bf16[64,1848]{1,0:T(8,128)(2,1)S(1)} %get-tuple-element.47.up_ref, bf16[64,1976]{1,0:T(8,128)(2,1)S(1)} %collective-permute-done.11.refs_3_.far, ...), custom_call_target="tpu_custom_call" | custom-call | flops 1150000000 | bytes 3600000 | tf_op jit(solution)/shard_map/output/pallas_call | solution.py:378
  35.2 0.9 %collective-permute-done.16.rest_2_ = bf16[16,2104]{1,0:T(8,128)(2,1)S(1)} collective-permute-done((bf16[16,2104]{1,0:T(8,128)(2,1)S(1)}, bf16[16,2104]{1,0:T(8,128)(2,1)S(1)}, u32[]{:S(2)}, u32[]{:S(2)}) %collective-permute-start.16) | collective-permute-done | bytes 67360 | tf_op jit(solution)/shard_map/ppermute | solution.py:31
  36.1 1.2 %gradient.1 = (f32[16,1848]{1,0:T(8,128)}, f32[64,2048]{1,0:T(8,128)}) custom-call(f32[16,1848]{1,0:T(8,128)S(1)} %get-tuple-element.50.own_term, bf16[64,64]{1,0:T(8,128)(2,1)S(1)} %get-tuple-element.51.own_back, bf16[64,2048]{1,0:T(8,128)(2,1)S(1)} %get-tuple-element.37.own_hidden.refs_4_, bf16[16,2104]{1,0:T(8,128)(2,1)S(1)} %collective-permute-done.14.rest_0_, ...), custom_call_target="tpu_custom_call" | custom-call | flops 1380000000 | bytes 4320000 | tf_op jit(solution)/shard_map/gradient/pallas_call | solution.py:385
  (21 shorter events, 2.9 us)
Async XLA Ops:
  0.6 14.7 %copy-start = (bf16[2048,1848]{0,1:T(8,128)(2,1)S(1)}, bf16[2048,1848]{0,1:T(8,128)(2,1)}, u32[]{:S(2)}) copy-start(bf16[2048,1848]{0,1:T(8,128)(2,1)} %param.11) | copy-start | bytes 22708228
  2.5 9.1 %collective-permute-start.3 = (bf16[64,1152]{1,0:T(8,128)(2,1)S(1)}, bf16[64,1152]{1,0:T(8,128)(2,1)S(1)}, u32[]{:S(2)}, u32[]{:S(2)}) collective-permute-start(bf16[64,1152]{1,0:T(8,128)(2,1)S(1)} %get-tuple-element.33), channel_id=1, source_target_pairs={{0,24},{8,16},{16,8},{24,0},{1,25},{9,17},{17,9},{25,1},{2,26},{10... | collective-permute-start | bytes 442376 | tf_op jit(solution)/shard_map/ppermute | solution.py:31
  6.4 1.2 %collective-permute-start = (f32[64,64]{1,0:T(8,128)S(1)}, f32[64,64]{1,0:T(8,128)S(1)}, u32[]{:S(2)}, u32[]{:S(2)}) collective-permute-start(f32[64,64]{1,0:T(8,128)S(1)} %get-tuple-element.31), channel_id=1, source_target_pairs={{0,1},{1,0},{2,3},{3,2},{4,5},{5,4},{6,7},{7,6},{8,9},{9,8},{10,11... | collective-permute-start | bytes 49160 | tf_op jit(solution)/shard_map/ppermute | solution.py:31
  7.6 3.9 %collective-permute-start.1 = (f32[64,64]{1,0:T(8,128)S(1)}, f32[64,64]{1,0:T(8,128)S(1)}, u32[]{:S(2)}, u32[]{:S(2)}) collective-permute-start(f32[64,64]{1,0:T(8,128)S(1)} %add.6), channel_id=1, source_target_pairs={{0,2},{1,3},{2,0},{3,1},{4,6},{5,7},{6,4},{7,5},{8,10},{9,11},{10,... | collective-permute-start | bytes 49160 | tf_op jit(solution)/shard_map/ppermute | solution.py:31
  9.2 5.6 %collective-permute-start.5 = (bf16[64,1152]{1,0:T(8,128)(2,1)S(1)}, bf16[64,1152]{1,0:T(8,128)(2,1)S(1)}, u32[]{:S(2)}, u32[]{:S(2)}) collective-permute-start(bf16[64,1152]{1,0:T(8,128)(2,1)S(1)} %get-tuple-element.38), channel_id=1, source_target_pairs={{0,8},{8,0},{16,24},{24,16},{1,9},{9,1},{17,25},{25,17},{2,10},{10... | collective-permute-start | bytes 442376 | tf_op jit(solution)/shard_map/ppermute | solution.py:31
  9.8 5.4 %collective-permute-start.6 = (bf16[64,1152]{1,0:T(8,128)(2,1)S(1)}, bf16[64,1152]{1,0:T(8,128)(2,1)S(1)}, u32[]{:S(2)}, u32[]{:S(2)}) collective-permute-start(bf16[64,1152]{1,0:T(8,128)(2,1)S(1)} %get-tuple-element.39), channel_id=1, source_target_pairs={{0,16},{8,24},{16,0},{24,8},{1,17},{9,25},{17,1},{25,9},{2,18},{10... | collective-permute-start | bytes 442376 | tf_op jit(solution)/shard_map/ppermute | solution.py:31
  11.6 3.8 %collective-permute-start.4 = (bf16[64,1152]{1,0:T(8,128)(2,1)S(1)}, bf16[64,1152]{1,0:T(8,128)(2,1)S(1)}, u32[]{:S(2)}, u32[]{:S(2)}) collective-permute-start(bf16[64,1152]{1,0:T(8,128)(2,1)S(1)} %collective-permute-done.3.message.rest_2_.rest_5_), channel_id=1, source_target_pairs={{0,1},{1,0},{2,3},{3,2},{4,5},{5,4},{6,7},{7,6},{8,9},{9,8},{10,11... | collective-permute-start | bytes 442376 | tf_op jit(solution)/shard_map/ppermute | solution.py:31
  11.6 10.4 %collective-permute-start.2 = (f32[64,64]{1,0:T(8,128)S(1)}, f32[64,64]{1,0:T(8,128)S(1)}, u32[]{:S(2)}, u32[]{:S(2)}) collective-permute-start(f32[64,64]{1,0:T(8,128)S(1)} %add.7.refs_4_), channel_id=1, source_target_pairs={{0,4},{1,5},{2,6},{3,7},{4,0},{5,1},{6,2},{7,3},{8,12},{9,13},{10,... | collective-permute-start | bytes 49160 | tf_op jit(solution)/shard_map/ppermute | solution.py:31
  14.9 4.0 %collective-permute-start.7 = (bf16[64,1152]{1,0:T(8,128)(2,1)S(1)}, bf16[64,1152]{1,0:T(8,128)(2,1)S(1)}, u32[]{:S(2)}, u32[]{:S(2)}) collective-permute-start(bf16[64,1152]{1,0:T(8,128)(2,1)S(1)} %collective-permute-done.5.rest_0_.refs_0_.rest_3_), channel_id=1, source_target_pairs={{0,1},{1,0},{2,3},{3,2},{4,5},{5,4},{6,7},{7,6},{8,9},{9,8},{10,11... | collective-permute-start | bytes 442376 | tf_op jit(solution)/shard_map/ppermute | solution.py:31
  15.1 3.8 %collective-permute-start.8 = (bf16[64,1152]{1,0:T(8,128)(2,1)S(1)}, bf16[64,1152]{1,0:T(8,128)(2,1)S(1)}, u32[]{:S(2)}, u32[]{:S(2)}) collective-permute-start(bf16[64,1152]{1,0:T(8,128)(2,1)S(1)} %collective-permute-done.6.rest_1_.refs_1_.rest_4_), channel_id=1, source_target_pairs={{0,1},{1,0},{2,3},{3,2},{4,5},{5,4},{6,7},{7,6},{8,9},{9,8},{10,11... | collective-permute-start | bytes 442376 | tf_op jit(solution)/shard_map/ppermute | solution.py:31
  17.6 10.2 %collective-permute-start.11 = (bf16[64,1976]{1,0:T(8,128)(2,1)S(1)}, bf16[64,1976]{1,0:T(8,128)(2,1)S(1)}, u32[]{:S(2)}, u32[]{:S(2)}) collective-permute-start(bf16[64,1976]{1,0:T(8,128)(2,1)S(1)} %far.1.earlier), channel_id=1, source_target_pairs={{0,24},{8,16},{16,8},{24,0},{1,25},{9,17},{17,9},{25,1},{2,26},{10... | collective-permute-start | bytes 758792 | tf_op jit(solution)/shard_map/ppermute | solution.py:31
  19.7 7.6 %collective-permute-start.9 = (f32[64,64]{1,0:T(8,128)S(1)}, f32[64,64]{1,0:T(8,128)S(1)}, u32[]{:S(2)}, u32[]{:S(2)}) collective-permute-start(f32[64,64]{1,0:T(8,128)S(1)} %get-tuple-element.43), channel_id=1, source_target_pairs={{0,8},{8,0},{16,24},{24,16},{1,9},{9,1},{17,25},{25,17},{2,10},{10... | collective-permute-start | bytes 49160 | tf_op jit(solution)/shard_map/ppermute | solution.py:31
  20.5 7.4 %collective-permute-start.10 = (f32[64,64]{1,0:T(8,128)S(1)}, f32[64,64]{1,0:T(8,128)S(1)}, u32[]{:S(2)}, u32[]{:S(2)}) collective-permute-start(f32[64,64]{1,0:T(8,128)S(1)} %get-tuple-element.44), channel_id=1, source_target_pairs={{0,16},{8,24},{16,0},{24,8},{1,17},{9,25},{17,1},{25,9},{2,18},{10... | collective-permute-start | bytes 49160 | tf_op jit(solution)/shard_map/ppermute | solution.py:31
  24.3 8.5 %collective-permute-start.12 = (bf16[64,1848]{1,0:T(8,128)(2,1)S(1)}, bf16[64,1848]{1,0:T(8,128)(2,1)S(1)}, u32[]{:S(2)}, u32[]{:S(2)}) collective-permute-start(bf16[64,1848]{1,0:T(8,128)(2,1)S(1)} %get-tuple-element.48), channel_id=1, source_target_pairs={{0,8},{8,0},{16,24},{24,16},{1,9},{9,1},{17,25},{25,17},{2,10},{10... | collective-permute-start | bytes 709640 | tf_op jit(solution)/shard_map/ppermute | solution.py:31
  25.6 8.2 %collective-permute-start.13 = (bf16[64,1848]{1,0:T(8,128)(2,1)S(1)}, bf16[64,1848]{1,0:T(8,128)(2,1)S(1)}, u32[]{:S(2)}, u32[]{:S(2)}) collective-permute-start(bf16[64,1848]{1,0:T(8,128)(2,1)S(1)} %get-tuple-element.49), channel_id=1, source_target_pairs={{0,16},{8,24},{16,0},{24,8},{1,17},{9,25},{17,1},{25,9},{2,18},{10... | collective-permute-start | bytes 709640 | tf_op jit(solution)/shard_map/ppermute | solution.py:31
  28.2 6.5 %collective-permute-start.14 = (bf16[16,2104]{1,0:T(8,128)(2,1)S(1)}, bf16[16,2104]{1,0:T(8,128)(2,1)S(1)}, u32[]{:S(2)}, u32[]{:S(2)}) collective-permute-start(bf16[16,2104]{1,0:T(8,128)(2,1)S(1)} %get-tuple-element.52), channel_id=1, source_target_pairs={{0,8},{8,0},{16,24},{24,16},{1,9},{9,1},{17,25},{25,17},{2,10},{10... | collective-permute-start | bytes 201992 | tf_op jit(solution)/shard_map/ppermute | solution.py:31
  29.8 5.4 %collective-permute-start.15 = (bf16[16,2104]{1,0:T(8,128)(2,1)S(1)}, bf16[16,2104]{1,0:T(8,128)(2,1)S(1)}, u32[]{:S(2)}, u32[]{:S(2)}) collective-permute-start(bf16[16,2104]{1,0:T(8,128)(2,1)S(1)} %get-tuple-element.53), channel_id=1, source_target_pairs={{0,16},{8,24},{16,0},{24,8},{1,17},{9,25},{17,1},{25,9},{2,18},{10... | collective-permute-start | bytes 201992 | tf_op jit(solution)/shard_map/ppermute | solution.py:31
  30.7 5.4 %collective-permute-start.16 = (bf16[16,2104]{1,0:T(8,128)(2,1)S(1)}, bf16[16,2104]{1,0:T(8,128)(2,1)S(1)}, u32[]{:S(2)}, u32[]{:S(2)}) collective-permute-start(bf16[16,2104]{1,0:T(8,128)(2,1)S(1)} %get-tuple-element.54), channel_id=1, source_target_pairs={{0,24},{8,16},{16,8},{24,0},{1,25},{9,17},{17,9},{25,1},{2,26},{10... | collective-permute-start | bytes 201992 | tf_op jit(solution)/shard_map/ppermute | solution.py:31

commit v4 on v3

--- a/solution.py
+++ b/solution.py
@@ -31,16 +31,24 @@
     return lax.ppermute(array, axis, [(i, i ^ distance) for i in range(size)])
 
 
-def halves_over_fsdp(partial):
+def swap_cores(array, axis, partner):
+    size = lax.axis_size(axis)
+    return lax.ppermute(array, axis, [(i, i ^ partner[i % 2]) for i in range(size)])
+
+
+def sum_over_fsdp(partial, earlier):
     size = lax.axis_size("fsdp")
     if size & (size - 1):
-        total = lax.psum(partial, "fsdp")
-        return total, jnp.zeros_like(total)
-    distance = 1
-    while distance < size // 2:
-        partial = partial + swap(partial, "fsdp", distance)
-        distance *= 2
-    return partial, swap(partial, "fsdp", distance)
+        return lax.psum(partial, "fsdp")
+    chip = partial + swap(partial, "fsdp", 1)
+    if size == 8:
+        one = swap_cores(chip, "fsdp", (2, 4))
+        chip = after(chip, earlier) + swap(chip, "fsdp", 6)
+        return chip + (one + swap(after(one, earlier), "fsdp", 1))
+    parts = [chip] + [swap(chip, "fsdp", d) for d in range(2, size, 2)]
+    while len(parts) > 1:
+        parts = [parts[i] + parts[i + 1] for i in range(0, len(parts), 2)]
+    return parts[0]
 
 
 def after(array, earlier):
@@ -131,46 +139,50 @@
     return jnp.concatenate([jnp.where(first, a, b), jnp.where(first, b, a)], axis=1)
 
 
-def two_terms(value):
-    high = value.astype(BF16).astype(F32)
-    return jnp.concatenate([high, value - high], axis=1).astype(BF16)
-
-
-def far_kernel(held_ref, at_ref, message, other, result_ref):
+def middle(units):
+    return units // 2 // LANES * LANES
+
+
+def product_kernel(groups, earlier, held_ref, at_ref, own_hidden, *refs):
+    count = groups - 1
+    messages, others, refs = refs[:count], refs[count : 2 * count], refs[2 * count :]
+    first, second, kept, nears, lows = refs[0], refs[1], refs[2], refs[3 : groups + 1], refs[groups + 1 :]
     units, depth = held_ref.shape
-    rows = whole_rows(depth // 2, positions()[2], message, other)
+    tokens = own_hidden.shape[0]
+    core = positions()[2]
+    parts = [own_hidden[...]] + [whole_rows(depth // 2, core, a, b) for a, b in zip(messages, others)]
+    rows = jnp.concatenate(parts, axis=0)
     low = lax.dot_general(rows, at_ref[...], NT, preferred_element_type=F32)
-    lead = 2 * low.shape[1]
-    result_ref[:, :lead] = two_terms(low)
-    rows = rows.T
-    for start in range(0, units, STEP):
-        end = min(start + STEP, units)
-        result = jnp.dot(held_ref[start:end], rows, preferred_element_type=F32).T
-        result_ref[:, lead + start : lead + end] = result.astype(BF16)
-
-
-def near_kernel(count, tokens, held_ref, early, later, *refs):
-    units, depth = held_ref.shape
-    core = positions()[2]
-    parts = [whole_rows(depth // 2, core, refs[i], refs[count + i]) for i in range(count)] + [refs[2 * count][...]]
-    rows = jnp.concatenate(parts, axis=0).T
-    for start in range(0, units, STEP):
-        end = min(start + STEP, units)
-        result = jnp.dot(held_ref[start:end], rows, preferred_element_type=F32).T
-        for i, ref in enumerate(refs[2 * count + 1 :]):
-            ref[:, start:end] = result[i * tokens : (i + 1) * tokens].astype(ref.dtype)
-
-
-def coef_kernel(groups, half, near, earlier, at_ref, new_ref, own_table, own_hidden, *rest):
-    messages, others = rest[: groups - 1], rest[groups - 1 : groups - 1 + near]
-    outs = rest[groups - 1 + near :]
-    lows, coef_ref, loss_ref = outs[: near + 1], outs[near + 1], outs[near + 2]
-    own, _, core = positions()
-    tokens = own_hidden.shape[0]
-    rows = [own_hidden[...]] + [whole_rows(half, core, messages[i], others[i]) for i in range(near)]
-    low = lax.dot_general(jnp.concatenate(rows, axis=0), at_ref[...], NT, preferred_element_type=F32)
     for i, ref in enumerate(lows):
         ref[...] = low[i * tokens : (i + 1) * tokens]
+    rows = rows.T
+    center = middle(units)
+    for start, end in [(i, min(i + STEP, center)) for i in range(0, center, STEP)] + [
+        (i, min(i + STEP, units)) for i in range(center, units, STEP)
+    ]:
+        result = jnp.dot(held_ref[start:end], rows, preferred_element_type=F32).T
+        for i, ref in enumerate([kept, *nears]):
+            ref[:, start:end] = result[i * tokens : (i + 1) * tokens]
+        last = result[count * tokens :].astype(BF16)
+        if end <= center:
+            first[:, start:end] = last
+        else:
+            second[:, start - center : end - center] = last
+
+
+def add_kernel(count, first, second, *refs):
+    center = first.shape[1]
+    for i, (ref, out) in enumerate(zip(refs[:count], refs[count:])):
+        out[...] = ref[...].astype(BF16)
+        if i == 0:
+            out[:, center:] = (ref[:, center:] + second[...].astype(F32)).astype(BF16)
+        if i == count - 1:
+            out[:, :center] = (ref[:, :center] + first[...].astype(F32)).astype(BF16)
+
+
+def coef_kernel(groups, half, new_ref, own_table, *rest):
+    messages, (coef_ref, loss_ref) = rest[: groups - 1], rest[groups - 1 :]
+    own = positions()[0]
     tables = [own_table[...]]
     for message in messages:
         terms = message[: 4 * BLOCK, half:].astype(F32)
@@ -207,19 +219,19 @@
 
 
 def adapter_kernel(groups, share, ride_rows, *refs):
-    lows, (far, back_ref, other_ref, coef_ref, upstream_ref) = refs[: groups - 1], refs[groups - 1 : groups + 4]
-    messages, (own_term, own_back, low_ref, term) = refs[groups + 4 : 2 * groups + 3], refs[2 * groups + 3 :]
+    lows, (back_ref, coef_ref, upstream_ref) = refs[:groups], refs[groups : groups + 3]
+    messages, (own_term, own_back, low_ref, term) = refs[groups + 3 : 2 * groups + 2], refs[2 * groups + 2 :]
     own = positions()[0]
     coef = coef_ref[:, 0:1]
     rank = term.shape[0]
-    low = far[:, :rank].astype(F32) + far[:, rank : 2 * rank].astype(F32)
-    for ref in lows:
+    low = lows[0][...]
+    for ref in lows[1:]:
         low = low + ref[...]
     low = low.astype(BF16)
     low_ref[...] = low
     gradient = (coef * upstream_ref[...].astype(F32)).astype(BF16)
     term[...] = ADAPTER_SCALING * lax.dot_general(low, gradient, TN, preferred_element_type=F32)
-    back = coef * (back_ref[...] + other_ref[...])
+    back = coef * back_ref[...]
     own_back[...] = back.astype(BF16)
     stack = back.shape[0] // ride_rows
     ride = jnp.concatenate([back[i * ride_rows : (i + 1) * ride_rows] for i in range(stack)], axis=1).astype(BF16)
@@ -240,15 +252,15 @@
         messages[d - 1][:, lanes:] = piece.astype(BF16)
 
 
-def output_kernel(lead, total_ref, low_ref, up_ref, far, *rest):
+def output_kernel(total_ref, low_ref, up_ref, *rest):
     total = total_ref[...] + ADAPTER_SCALING * jnp.dot(low_ref[...], up_ref[...], preferred_element_type=F32)
-    total = total + far[:, lead:].astype(F32)
-    for ref in rest[:-1]:
+    for ref in rest[:-2]:
         total = total + ref[...].astype(F32)
-    rest[-1][...] = total.astype(BF16)
-
-
-def gradient_kernel(groups, rank, share, ride_rows, own_term, own_back, own_hidden, *rest):
+    rest[-2][...] = total.astype(BF16)
+    rest[-1][...] = jnp.zeros_like(rest[-1])
+
+
+def gradient_kernel(groups, rank, share, ride_rows, written, own_term, own_back, own_hidden, *rest):
     arrived, messages, others = (rest[i * (groups - 1) : (i + 1) * (groups - 1)] for i in range(3))
     up_ref, down_ref = rest[3 * (groups - 1) :]
     core = positions()[2]
@@ -332,36 +344,41 @@
     got = {d: swap(messages[d - 1], "group", d) for d in reversed(others)}
     held = pltpu.with_memory_space_constraint(weight, pltpu.VMEM)
     far, near = groups - 1, list(range(1, groups - 1))
-    early, last = halves_over_fsdp(back)
-    theirs = {far: swap(after(got[far], early), "fsdp", 1)}
-
-    lead = 2 * rank
-    came = {}
-    (result,) = call(far_kernel, "far", 2.3, [pltpu.VMEM((tokens, lead + units), BF16)], [VMEM] * 4)(
-        held, at, got[far], theirs[far]
-    )
-    came[far] = swap(result, "group", far)
-    for d in near:
-        theirs[d] = swap(got[d], "fsdp", 1)
-    *lows, coef, loss = call(
-        functools.partial(coef_kernel, groups, half, len(near)),
+    coef, loss = call(
+        functools.partial(coef_kernel, groups, half),
         "coef",
-        0.8,
-        [pltpu.VMEM((tokens, rank), F32)] * (len(near) + 1)
-        + [pltpu.VMEM((tokens, LANES), F32), jax.ShapeDtypeStruct((1, 1), F32)],
-        [ANY] + [VMEM] * (3 + groups + len(near)),
-    )(result, at, new, own_table, own_hidden, *[got[d] for d in others], *[theirs[d] for d in near])
-    low_terms = [lows[0]] + [swap(low, "group", d) for d, low in zip(near, lows[1:])]
-    *results, kept = call(
-        functools.partial(near_kernel, len(near), tokens),
-        "near",
-        2.4,
-        [pltpu.VMEM((tokens, units), BF16)] * len(near) + [pltpu.VMEM((tokens, units), F32)],
-        [VMEM, ANY, ANY] + [VMEM] * (1 + 2 * len(near)),
-    )(held, last, coef, *[got[d] for d in near], *[theirs[d] for d in near], own_hidden)
-    for d, result in zip(near, results):
-        came[d] = swap(result, "group", d)
-
+        1.5,
+        [pltpu.VMEM((tokens, LANES), F32), jax.ShapeDtypeStruct((1, 1), F32)],
+        [VMEM] * (groups + 1),
+    )(new, own_table, *[got[d] for d in others])
+
+    back = sum_over_fsdp(back, coef)
+    theirs = {d: swap(got[d], "fsdp", 1) for d in reversed(others)}
+
+    first, second, kept, *terms = call(
+        functools.partial(product_kernel, groups),
+        "product",
+        3.0,
+        [
+            pltpu.VMEM((tokens, middle(units)), BF16),
+            pltpu.VMEM((tokens, units - middle(units)), BF16),
+            pltpu.VMEM((tokens, units), F32),
+        ]
+        + [pltpu.VMEM((tokens, units), F32)] * len(near)
+        + [pltpu.VMEM((tokens, rank), F32)] * groups,
+        [ANY] + [VMEM] * (1 + 2 * groups),
+    )(coef, held, at, own_hidden, *[got[d] for d in others], *[theirs[d] for d in others])
+    lows = terms[len(near) :]
+    first, second = swap(first, "group", near[0]), swap(second, "group", near[-1])
+    lows = [lows[0]] + [swap(lows[d], "group", d) for d in others]
+    results = call(
+        functools.partial(add_kernel, len(near)),
+        "add",
+        0.5,
+        [pltpu.VMEM((tokens, units), BF16)] * len(near),
+        [VMEM] * (2 + len(near)),
+    )(first, second, *terms[: len(near)])
+    came = [swap(result, "group", d) for d, result in zip(near, results)]
     share = rank // groups
     ride_rows = max(share, 16)
     lanes = tokens // ride_rows * rank
@@ -371,24 +388,25 @@
         4.0,
         [pltpu.VMEM((ride_rows, lanes + units), BF16)] * (groups - 1)
         + [pltpu.VMEM((share, units), F32), pltpu.VMEM((tokens, rank), BF16), pltpu.VMEM((tokens, rank), BF16)],
-        [VMEM] * (groups + 4),
+        [VMEM] * (groups + 3),
         scratch=[pltpu.VMEM((rank, units), F32)],
-    )(*low_terms, came[far], early, last, coef, upstream)
+    )(*lows, back, coef, upstream)
     arrived = {d: swap(pieces[d - 1], "group", d) for d in reversed(others)}
-    (projection_output,) = call(
-        functools.partial(output_kernel, lead),
+    projection_output, written = call(
+        output_kernel,
         "output",
         1.0,
-        [jax.ShapeDtypeStruct((tokens, units), BF16)],
-        [VMEM] * (4 + len(near)),
-    )(kept, low, up, came[far], *[came[d] for d in near])
+        [jax.ShapeDtypeStruct((tokens, units), BF16), pltpu.VMEM((8, LANES), F32)],
+        [VMEM] * (3 + len(near)),
+    )(kept, low, up, *came)
     gradient_up, gradient_down = call(
         functools.partial(gradient_kernel, groups, rank, share, ride_rows),
         "gradient",
         1.2,
         [jax.ShapeDtypeStruct((share, units), F32), jax.ShapeDtypeStruct((rank, depth), F32)],
-        [VMEM] * (3 * groups),
+        [ANY] + [VMEM] * (3 * groups),
     )(
+        written,
         own_term,
         own_back,
         own_hidden,

time: 37.4 us -> 36.9 us (0.987)
  starting transfers between devices: 18.5 us -> 21.9 us
  Pallas kernels: 9.73 us -> 7.56 us
  waiting for transfers between devices: 8.35 us -> 6.52 us
    pallas_call x4, Pallas kernels: 6.37 us -> 4.25 us  [the longest x1 2.6 us: on_device(): call(functools.partial(product_kernel, groups), 'product', 3.0, [pltpu.VM...]
    ppermute x0 -> x1, starting transfers between devices: none -> 2.03 us  [swap_cores(): lax.ppermute(array, axis, [(i, i ^ partner[i % 2]) for i in range(size)])]
    ppermute x17 -> x19, waiting for transfers between devices: 8.35 us -> 6.52 us  [swap(): return lax.ppermute(array, axis, [(i, i ^ distance) for i in range(size)])]
    ppermute x17 -> x19, starting transfers between devices: 18.5 us -> 19.9 us  [swap(): return lax.ppermute(array, axis, [(i, i ^ distance) for i in range(size)])]
  transfers between devices with their start and end apart: 17 -> 20, of which waited for: 10 -> 8; matrix products, arithmetic and copies ran while one was open for 0% -> 0% of each run, Pallas kernels for 18% -> 12%
where the time goes in v4:
time: 36.9 us; the launch traced here: 36.8 us
  starting transfers between devices  21.9 us (59%)
  Pallas kernels  7.56 us (20%)
  waiting for transfers between devices  6.52 us (18%)
  between operations  0.71 us (2%)
    ppermute x19, starting transfers between devices, swap(): return lax.ppermute(array, axis, [(i, i ^ distance) for i in range(size)])  19.9 us
    ppermute x19, waiting for transfers between devices, swap(): return lax.ppermute(array, axis, [(i, i ^ distance) for i in range(size)])  6.52 us
    pallas_call x1, Pallas kernels, on_device(): call(functools.partial(product_kernel, groups), 'product', 3.0, [pltpu.VM...  2.6 us
    ppermute x1, starting transfers between devices, swap_cores(): lax.ppermute(array, axis, [(i, i ^ partner[i % 2]) for i in range(size)])  2.03 us
    pallas_call x1, Pallas kernels, on_device(): call(functools.partial(pack_kernel, groups, depth), 'pack', 1.8, [pltpu.V...  1.8 us
    pallas_call x1, Pallas kernels, on_device(): call(functools.partial(gradient_kernel, groups, rank, share, ride_rows),...  1.19 us
    pallas_call x1, Pallas kernels, on_device(): call(output_kernel, 'output', 1.0, [jax.ShapeDtypeStruct((tokens, units),...  0.93 us
  transfers between devices with their start and end apart: 20, of which 8 were waited for; matrix products, arithmetic and copies ran while one was open for 0% of the time, Pallas kernels for 12%

profile of v4, /device:TPU:0, one launch (start us, length us, event | category | flops | bytes accessed | tf_op | source)
XLA Modules:
  0.0 36.8 jit_solution(18250398112709143440)
XLA Ops:
  0.7 1.8 %pack.1 = (bf16[64,1152]{1,0:T(8,128)(2,1)S(1)}, bf16[64,1152]{1,0:T(8,128)(2,1)S(1)}, bf16[64,1152]{1,0:T(8,128)(2,1)S(1)}, f32[8,128]{1,0:T(8,128)S(1)}, bf16[...) custom-call(bf16[64,8192]{1,0:T(8,128)(2,1)} %hidden_ref.1, ...), custom_call_target="tpu_custom_call" | custom-call | flops 2070000000 | bytes 6480000 | tf_op jit(solution)/shard_map/pack/pallas_call | solution.py:305
  2.5 3.0 %collective-permute-start = (bf16[64,1152]{1,0:T(8,128)(2,1)S(1)}, bf16[64,1152]{1,0:T(8,128)(2,1)S(1)}, u32[]{:S(2)}, u32[]{:S(2)}) collective-permute-start(bf16[64,1152]{1,0:T(8,128)(2,1)S(1)} %get-tuple-element.41), channel_id=1, source_target_pairs={{0,8},{8,0},{16,24},{24,16},{1,9},{9,1},{17,25},{25,17},{2,10},{10... | collective-permute-start | bytes 442376 | tf_op jit(solution)/shard_map/ppermute | solution.py:31
  5.5 1.5 %collective-permute-start.1 = (bf16[64,1152]{1,0:T(8,128)(2,1)S(1)}, bf16[64,1152]{1,0:T(8,128)(2,1)S(1)}, u32[]{:S(2)}, u32[]{:S(2)}) collective-permute-start(bf16[64,1152]{1,0:T(8,128)(2,1)S(1)} %get-tuple-element.42), channel_id=1, source_target_pairs={{0,16},{8,24},{16,0},{24,8},{1,17},{9,25},{17,1},{25,9},{2,18},{10... | collective-permute-start | bytes 442376 | tf_op jit(solution)/shard_map/ppermute | solution.py:31
  7.0 1.2 %collective-permute-done.9 = f32[64,64]{1,0:T(8,128)S(1)} collective-permute-done((f32[64,64]{1,0:T(8,128)S(1)}, f32[64,64]{1,0:T(8,128)S(1)}, u32[]{:S(2)}, u32[]{:S(2)}) %collective-permute-start.9) | collective-permute-done | bytes 16416 | tf_op jit(solution)/shard_map/ppermute | solution.py:31
  8.2 2.0 %collective-permute-start.11 = (f32[64,64]{1,0:T(8,128)S(1)}, f32[64,64]{1,0:T(8,128)S(1)}, u32[]{:S(2)}, u32[]{:S(2)}) collective-permute-start(f32[64,64]{1,0:T(8,128)S(1)} %add.13), channel_id=1, source_target_pairs={{0,2},{1,5},{2,0},{3,7},{4,6},{5,1},{6,4},{7,3},{8,10},{9,13},{10,... | collective-permute-start | bytes 49160 | tf_op jit(solution)/shard_map/ppermute | solution.py:36
  10.3 2.5 %collective-permute-start.10 = (f32[64,64]{1,0:T(8,128)S(1)}, f32[64,64]{1,0:T(8,128)S(1)}, u32[]{:S(2)}, u32[]{:S(2)}) collective-permute-start(f32[64,64]{1,0:T(8,128)S(1)} %add.13), channel_id=1, source_target_pairs={{0,6},{1,7},{2,4},{3,5},{4,2},{5,3},{6,0},{7,1},{8,14},{9,15},{10,... | collective-permute-start | bytes 49160 | tf_op jit(solution)/shard_map/ppermute | solution.py:31
  12.7 1.2 %collective-permute-done.1.rest_1_.refs_1_.rest_4_ = bf16[64,1152]{1,0:T(8,128)(2,1)S(1)} collective-permute-done((bf16[64,1152]{1,0:T(8,128)(2,1)S(1)}, bf16[64,1152]{1,0:T(8,128)(2,1)S(1)}, u32[]{:S(2)}, u32[]{:S(2)}) %collective-permute-start.1) | collective-permute-done | bytes 147488 | tf_op jit(solution)/shard_map/ppermute | solution.py:31
  14.4 0.6 %coef.1 = (f32[64,128]{1,0:T(8,128)S(1)}, f32[1,1]{1,0:T(1,128)}) custom-call(f32[1,4,16]{2,1,0:T(4,128)S(1)} %get-tuple-element.39.new_ref, f32[8,128]{1,0:T(8,128)S(1)} %get-tuple-element.40.own_table, bf16[64,1152]{1,0:T(8,128)(2,1)S(1)} %collective-permute-done.rest_0_.refs_0_.rest_3_, ...), custom_call_target="tpu_custom_call" | custom-call | flops 1724999936 | bytes 5400000 | tf_op jit(solution)/shard_map/coef/pallas_call | solution.py:347
  15.5 2.6 %product.1 = (bf16[64,896]{1,0:T(8,128)(2,1)S(1)}, bf16[64,952]{1,0:T(8,128)(2,1)S(1)}, f32[64,1848]{1,0:T(8,128)S(1)}, f32[64,1848]{1,0:T(8,128)S(1)}, f32[64,1...) custom-call(f32[64,128]{1,0:T(8,128)S(1)} %get-tuple-element.44.earl, ...), custom_call_target="tpu_custom_call" | custom-call | flops 3449999872 | bytes 10800000 | tf_op jit(solution)/shard_map/product/pallas_call | solution.py:358
  18.1 1.1 %collective-permute-start.13 = (bf16[64,896]{1,0:T(8,128)(2,1)S(1)}, bf16[64,896]{1,0:T(8,128)(2,1)S(1)}, u32[]{:S(2)}, u32[]{:S(2)}) collective-permute-start(bf16[64,896]{1,0:T(8,128)(2,1)S(1)} %get-tuple-element.58), channel_id=1, source_target_pairs={{0,8},{8,0},{16,24},{24,16},{1,9},{9,1},{17,25},{25,17},{2,10},{10... | collective-permute-start | bytes 344072 | tf_op jit(solution)/shard_map/ppermute | solution.py:31
  19.2 1.1 %collective-permute-start.14 = (bf16[64,952]{1,0:T(8,128)(2,1)S(1)}, bf16[64,952]{1,0:T(8,128)(2,1)S(1)}, u32[]{:S(2)}, u32[]{:S(2)}) collective-permute-start(bf16[64,952]{1,0:T(8,128)(2,1)S(1)} %get-tuple-element.59), channel_id=1, source_target_pairs={{0,16},{8,24},{16,0},{24,8},{1,17},{9,25},{17,1},{25,9},{2,18},{10... | collective-permute-start | bytes 365576 | tf_op jit(solution)/shard_map/ppermute | solution.py:31
  20.3 1.5 %collective-permute-start.6 = (f32[64,64]{1,0:T(8,128)S(1)}, f32[64,64]{1,0:T(8,128)S(1)}, u32[]{:S(2)}, u32[]{:S(2)}) collective-permute-start(f32[64,64]{1,0:T(8,128)S(1)} %get-tuple-element.49), channel_id=1, source_target_pairs={{0,8},{8,0},{16,24},{24,16},{1,9},{9,1},{17,25},{25,17},{2,10},{10... | collective-permute-start | bytes 49160 | tf_op jit(solution)/shard_map/ppermute | solution.py:31
  21.8 0.5 %collective-permute-start.7 = (f32[64,64]{1,0:T(8,128)S(1)}, f32[64,64]{1,0:T(8,128)S(1)}, u32[]{:S(2)}, u32[]{:S(2)}) collective-permute-start(f32[64,64]{1,0:T(8,128)S(1)} %get-tuple-element.50), channel_id=1, source_target_pairs={{0,16},{8,24},{16,0},{24,8},{1,17},{9,25},{17,1},{25,9},{2,18},{10... | collective-permute-start | bytes 49160 | tf_op jit(solution)/shard_map/ppermute | solution.py:31
  22.3 1.5 %collective-permute-start.8 = (f32[64,64]{1,0:T(8,128)S(1)}, f32[64,64]{1,0:T(8,128)S(1)}, u32[]{:S(2)}, u32[]{:S(2)}) collective-permute-start(f32[64,64]{1,0:T(8,128)S(1)} %get-tuple-element.51), channel_id=1, source_target_pairs={{0,24},{8,16},{16,8},{24,0},{1,25},{9,17},{17,9},{25,1},{2,26},{10... | collective-permute-start | bytes 49160 | tf_op jit(solution)/shard_map/ppermute | solution.py:31
  23.9 1.0 %collective-permute-done.14.second = bf16[64,952]{1,0:T(8,128)(2,1)S(1)} collective-permute-done((bf16[64,952]{1,0:T(8,128)(2,1)S(1)}, bf16[64,952]{1,0:T(8,128)(2,1)S(1)}, u32[]{:S(2)}, u32[]{:S(2)}) %collective-permute-start.14) | collective-permute-done | bytes 121888 | tf_op jit(solution)/shard_map/ppermute | solution.py:31
  24.9 1.2 %collective-permute-start.15 = (bf16[64,1848]{1,0:T(8,128)(2,1)S(1)}, bf16[64,1848]{1,0:T(8,128)(2,1)S(1)}, u32[]{:S(2)}, u32[]{:S(2)}) collective-permute-start(bf16[64,1848]{1,0:T(8,128)(2,1)S(1)} %get-tuple-element.62), channel_id=1, source_target_pairs={{0,8},{8,0},{16,24},{24,16},{1,9},{9,1},{17,25},{25,17},{2,10},{10... | collective-permute-start | bytes 709640 | tf_op jit(solution)/shard_map/ppermute | solution.py:31
  26.2 1.9 %collective-permute-start.16 = (bf16[64,1848]{1,0:T(8,128)(2,1)S(1)}, bf16[64,1848]{1,0:T(8,128)(2,1)S(1)}, u32[]{:S(2)}, u32[]{:S(2)}) collective-permute-start(bf16[64,1848]{1,0:T(8,128)(2,1)S(1)} %get-tuple-element.63), channel_id=1, source_target_pairs={{0,16},{8,24},{16,0},{24,8},{1,17},{9,25},{17,1},{25,9},{2,18},{10... | collective-permute-start | bytes 709640 | tf_op jit(solution)/shard_map/ppermute | solution.py:31
  28.6 1.3 %collective-permute-start.18 = (bf16[16,2104]{1,0:T(8,128)(2,1)S(1)}, bf16[16,2104]{1,0:T(8,128)(2,1)S(1)}, u32[]{:S(2)}, u32[]{:S(2)}) collective-permute-start(bf16[16,2104]{1,0:T(8,128)(2,1)S(1)} %get-tuple-element.69), channel_id=1, source_target_pairs={{0,16},{8,24},{16,0},{24,8},{1,17},{9,25},{17,1},{25,9},{2,18},{10... | collective-permute-start | bytes 201992 | tf_op jit(solution)/shard_map/ppermute | solution.py:31
  29.9 2.0 %collective-permute-start.19 = (bf16[16,2104]{1,0:T(8,128)(2,1)S(1)}, bf16[16,2104]{1,0:T(8,128)(2,1)S(1)}, u32[]{:S(2)}, u32[]{:S(2)}) collective-permute-start(bf16[16,2104]{1,0:T(8,128)(2,1)S(1)} %get-tuple-element.70), channel_id=1, source_target_pairs={{0,24},{8,16},{16,8},{24,0},{1,25},{9,17},{17,9},{25,1},{2,26},{10... | collective-permute-start | bytes 201992 | tf_op jit(solution)/shard_map/ppermute | solution.py:31
  31.9 1.4 %collective-permute-done.15.rest_0_ = bf16[64,1848]{1,0:T(8,128)(2,1)S(1)} collective-permute-done((bf16[64,1848]{1,0:T(8,128)(2,1)S(1)}, bf16[64,1848]{1,0:T(8,128)(2,1)S(1)}, u32[]{:S(2)}, u32[]{:S(2)}) %collective-permute-start.15) | collective-permute-done | bytes 236576 | tf_op jit(solution)/shard_map/ppermute | solution.py:31
  33.4 0.7 %collective-permute-done.16.rest_1_ = bf16[64,1848]{1,0:T(8,128)(2,1)S(1)} collective-permute-done((bf16[64,1848]{1,0:T(8,128)(2,1)S(1)}, bf16[64,1848]{1,0:T(8,128)(2,1)S(1)}, u32[]{:S(2)}, u32[]{:S(2)}) %collective-permute-start.16) | collective-permute-done | bytes 236576 | tf_op jit(solution)/shard_map/ppermute | solution.py:31
  34.1 0.9 %output.1 = (bf16[64,1848]{1,0:T(8,128)(2,1)}, f32[8,128]{1,0:T(8,128)S(1)}) custom-call(f32[64,1848]{1,0:T(8,128)S(1)} %get-tuple-element.47.total_ref, bf16[64,64]{1,0:T(8,128)(2,1)S(1)} %get-tuple-element.56.low_ref, bf16[64,1848]{1,0:T(8,128)(2,1)S(1)} %get-tuple-element.57.up_ref, bf16[64,1848]{1,0:T(8,128)(2,1)S(1)} %collective-permute-done.15.rest_0_, ...), custom_call_target="tpu_custom_call" | custom-call | flops 1150000000 | bytes 3600000 | tf_op jit(solution)/shard_map/output/pallas_call | solution.py:395
  35.0 0.6 %collective-permute-done.18.rest_1_ = bf16[16,2104]{1,0:T(8,128)(2,1)S(1)} collective-permute-done((bf16[16,2104]{1,0:T(8,128)(2,1)S(1)}, bf16[16,2104]{1,0:T(8,128)(2,1)S(1)}, u32[]{:S(2)}, u32[]{:S(2)}) %collective-permute-start.18) | collective-permute-done | bytes 67360 | tf_op jit(solution)/shard_map/ppermute | solution.py:31
  35.6 1.2 %gradient.1 = (f32[16,1848]{1,0:T(8,128)}, f32[64,2048]{1,0:T(8,128)}) custom-call(f32[8,128]{1,0:T(8,128)S(1)} %get-tuple-element.65.written, f32[16,1848]{1,0:T(8,128)S(1)} %get-tuple-element.66.own_term, bf16[64,64]{1,0:T(8,128)(2,1)S(1)} %get-tuple-element.67.own_back, bf16[64,2048]{1,0:T(8,128)(2,1)S(1)} %get-tuple-element.46.own_hidden, ...), custom_call_target="tpu_custom_call" | custom-call | flops 1380000000 | bytes 4320000 | tf_op jit(solution)/shard_map/gradient/pallas_call | solution.py:402
  (30 shorter events, 1.7 us)
Async XLA Ops:
  0.6 14.9 %slice-start = ((s8[7569408]{0:T(1024)(128)(4,1)}), s8[4194304]{0:T(1024)(128)(4,1)S(1)}, s32[]{:S(2)}) async-start(s8[7569408]{0:T(1024)(128)(4,1)} %bitcast.4), calls=%async_computation | async-start | bytes 8388608
  0.6 14.9 %slice-start.1 = ((s8[7569408]{0:T(1024)(128)(4,1)}), s8[3375104]{0:T(1024)(128)(4,1)S(1)}, s32[]{:S(2)}) async-start(s8[7569408]{0:T(1024)(128)(4,1)} %bitcast.4), calls=%async_computation.1 | async-start | bytes 6750208
  2.5 10.3 %collective-permute-start = (bf16[64,1152]{1,0:T(8,128)(2,1)S(1)}, bf16[64,1152]{1,0:T(8,128)(2,1)S(1)}, u32[]{:S(2)}, u32[]{:S(2)}) collective-permute-start(bf16[64,1152]{1,0:T(8,128)(2,1)S(1)} %get-tuple-element.41), channel_id=1, source_target_pairs={{0,8},{8,0},{16,24},{24,16},{1,9},{9,1},{17,25},{25,17},{2,10},{10... | collective-permute-start | bytes 442376 | tf_op jit(solution)/shard_map/ppermute | solution.py:31
  5.5 8.5 %collective-permute-start.1 = (bf16[64,1152]{1,0:T(8,128)(2,1)S(1)}, bf16[64,1152]{1,0:T(8,128)(2,1)S(1)}, u32[]{:S(2)}, u32[]{:S(2)}) collective-permute-start(bf16[64,1152]{1,0:T(8,128)(2,1)S(1)} %get-tuple-element.42), channel_id=1, source_target_pairs={{0,16},{8,24},{16,0},{24,8},{1,17},{9,25},{17,1},{25,9},{2,18},{10... | collective-permute-start | bytes 442376 | tf_op jit(solution)/shard_map/ppermute | solution.py:31
  7.0 7.0 %collective-permute-start.2 = (bf16[64,1152]{1,0:T(8,128)(2,1)S(1)}, bf16[64,1152]{1,0:T(8,128)(2,1)S(1)}, u32[]{:S(2)}, u32[]{:S(2)}) collective-permute-start(bf16[64,1152]{1,0:T(8,128)(2,1)S(1)} %get-tuple-element.43), channel_id=1, source_target_pairs={{0,24},{8,16},{16,8},{24,0},{1,25},{9,17},{17,9},{25,1},{2,26},{10... | collective-permute-start | bytes 442376 | tf_op jit(solution)/shard_map/ppermute | solution.py:31
  7.0 1.2 %collective-permute-start.9 = (f32[64,64]{1,0:T(8,128)S(1)}, f32[64,64]{1,0:T(8,128)S(1)}, u32[]{:S(2)}, u32[]{:S(2)}) collective-permute-start(f32[64,64]{1,0:T(8,128)S(1)} %get-tuple-element.52), channel_id=1, source_target_pairs={{0,1},{1,0},{2,3},{3,2},{4,5},{5,4},{6,7},{7,6},{8,9},{9,8},{10,11... | collective-permute-start | bytes 49160 | tf_op jit(solution)/shard_map/ppermute | solution.py:31
  8.2 6.9 %collective-permute-start.11 = (f32[64,64]{1,0:T(8,128)S(1)}, f32[64,64]{1,0:T(8,128)S(1)}, u32[]{:S(2)}, u32[]{:S(2)}) collective-permute-start(f32[64,64]{1,0:T(8,128)S(1)} %add.13), channel_id=1, source_target_pairs={{0,2},{1,5},{2,0},{3,7},{4,6},{5,1},{6,4},{7,3},{8,10},{9,13},{10,... | collective-permute-start | bytes 49160 | tf_op jit(solution)/shard_map/ppermute | solution.py:36
  10.3 10.1 %collective-permute-start.10 = (f32[64,64]{1,0:T(8,128)S(1)}, f32[64,64]{1,0:T(8,128)S(1)}, u32[]{:S(2)}, u32[]{:S(2)}) collective-permute-start(f32[64,64]{1,0:T(8,128)S(1)} %add.13), channel_id=1, source_target_pairs={{0,6},{1,7},{2,4},{3,5},{4,2},{5,3},{6,0},{7,1},{8,14},{9,15},{10,... | collective-permute-start | bytes 49160 | tf_op jit(solution)/shard_map/ppermute | solution.py:31
  12.7 2.4 %collective-permute-start.3 = (bf16[64,1152]{1,0:T(8,128)(2,1)S(1)}, bf16[64,1152]{1,0:T(8,128)(2,1)S(1)}, u32[]{:S(2)}, u32[]{:S(2)}) collective-permute-start(bf16[64,1152]{1,0:T(8,128)(2,1)S(1)} %collective-permute-done.rest_0_.refs_0_.rest_3_), channel_id=1, source_target_pairs={{0,1},{1,0},{2,3},{3,2},{4,5},{5,4},{6,7},{7,6},{8,9},{9,8},{10,11... | collective-permute-start | bytes 442376 | tf_op jit(solution)/shard_map/ppermute | solution.py:31
  13.9 1.4 %collective-permute-start.4 = (bf16[64,1152]{1,0:T(8,128)(2,1)S(1)}, bf16[64,1152]{1,0:T(8,128)(2,1)S(1)}, u32[]{:S(2)}, u32[]{:S(2)}) collective-permute-start(bf16[64,1152]{1,0:T(8,128)(2,1)S(1)} %collective-permute-done.1.rest_1_.refs_1_.rest_4_), channel_id=1, source_target_pairs={{0,1},{1,0},{2,3},{3,2},{4,5},{5,4},{6,7},{7,6},{8,9},{9,8},{10,11... | collective-permute-start | bytes 442376 | tf_op jit(solution)/shard_map/ppermute | solution.py:31
  13.9 1.6 %collective-permute-start.5 = (bf16[64,1152]{1,0:T(8,128)(2,1)S(1)}, bf16[64,1152]{1,0:T(8,128)(2,1)S(1)}, u32[]{:S(2)}, u32[]{:S(2)}) collective-permute-start(bf16[64,1152]{1,0:T(8,128)(2,1)S(1)} %collective-permute-done.2.rest_2_.refs_2_.rest_5_), channel_id=1, source_target_pairs={{0,1},{1,0},{2,3},{3,2},{4,5},{5,4},{6,7},{7,6},{8,9},{9,8},{10,11... | collective-permute-start | bytes 442376 | tf_op jit(solution)/shard_map/ppermute | solution.py:31
  15.1 5.2 %collective-permute-start.12 = (f32[64,64]{1,0:T(8,128)S(1)}, f32[64,64]{1,0:T(8,128)S(1)}, u32[]{:S(2)}, u32[]{:S(2)}) collective-permute-start(f32[64,64]{1,0:T(8,128)S(1)} %collective-permute-done.11), channel_id=1, source_target_pairs={{0,1},{1,0},{2,3},{3,2},{4,5},{5,4},{6,7},{7,6},{8,9},{9,8},{10,11... | collective-permute-start | bytes 49160 | tf_op jit(solution)/shard_map/ppermute | solution.py:31
  18.1 5.8 %collective-permute-start.13 = (bf16[64,896]{1,0:T(8,128)(2,1)S(1)}, bf16[64,896]{1,0:T(8,128)(2,1)S(1)}, u32[]{:S(2)}, u32[]{:S(2)}) collective-permute-start(bf16[64,896]{1,0:T(8,128)(2,1)S(1)} %get-tuple-element.58), channel_id=1, source_target_pairs={{0,8},{8,0},{16,24},{24,16},{1,9},{9,1},{17,25},{25,17},{2,10},{10... | collective-permute-start | bytes 344072 | tf_op jit(solution)/shard_map/ppermute | solution.py:31
  19.2 5.6 %collective-permute-start.14 = (bf16[64,952]{1,0:T(8,128)(2,1)S(1)}, bf16[64,952]{1,0:T(8,128)(2,1)S(1)}, u32[]{:S(2)}, u32[]{:S(2)}) collective-permute-start(bf16[64,952]{1,0:T(8,128)(2,1)S(1)} %get-tuple-element.59), channel_id=1, source_target_pairs={{0,16},{8,24},{16,0},{24,8},{1,17},{9,25},{17,1},{25,9},{2,18},{10... | collective-permute-start | bytes 365576 | tf_op jit(solution)/shard_map/ppermute | solution.py:31
  20.3 7.7 %collective-permute-start.6 = (f32[64,64]{1,0:T(8,128)S(1)}, f32[64,64]{1,0:T(8,128)S(1)}, u32[]{:S(2)}, u32[]{:S(2)}) collective-permute-start(f32[64,64]{1,0:T(8,128)S(1)} %get-tuple-element.49), channel_id=1, source_target_pairs={{0,8},{8,0},{16,24},{24,16},{1,9},{9,1},{17,25},{25,17},{2,10},{10... | collective-permute-start | bytes 49160 | tf_op jit(solution)/shard_map/ppermute | solution.py:31
  21.8 6.2 %collective-permute-start.7 = (f32[64,64]{1,0:T(8,128)S(1)}, f32[64,64]{1,0:T(8,128)S(1)}, u32[]{:S(2)}, u32[]{:S(2)}) collective-permute-start(f32[64,64]{1,0:T(8,128)S(1)} %get-tuple-element.50), channel_id=1, source_target_pairs={{0,16},{8,24},{16,0},{24,8},{1,17},{9,25},{17,1},{25,9},{2,18},{10... | collective-permute-start | bytes 49160 | tf_op jit(solution)/shard_map/ppermute | solution.py:31
  22.3 5.7 %collective-permute-start.8 = (f32[64,64]{1,0:T(8,128)S(1)}, f32[64,64]{1,0:T(8,128)S(1)}, u32[]{:S(2)}, u32[]{:S(2)}) collective-permute-start(f32[64,64]{1,0:T(8,128)S(1)} %get-tuple-element.51), channel_id=1, source_target_pairs={{0,24},{8,16},{16,8},{24,0},{1,25},{9,17},{17,9},{25,1},{2,26},{10... | collective-permute-start | bytes 49160 | tf_op jit(solution)/shard_map/ppermute | solution.py:31
  24.9 8.4 %collective-permute-start.15 = (bf16[64,1848]{1,0:T(8,128)(2,1)S(1)}, bf16[64,1848]{1,0:T(8,128)(2,1)S(1)}, u32[]{:S(2)}, u32[]{:S(2)}) collective-permute-start(bf16[64,1848]{1,0:T(8,128)(2,1)S(1)} %get-tuple-element.62), channel_id=1, source_target_pairs={{0,8},{8,0},{16,24},{24,16},{1,9},{9,1},{17,25},{25,17},{2,10},{10... | collective-permute-start | bytes 709640 | tf_op jit(solution)/shard_map/ppermute | solution.py:31
  26.2 7.9 %collective-permute-start.16 = (bf16[64,1848]{1,0:T(8,128)(2,1)S(1)}, bf16[64,1848]{1,0:T(8,128)(2,1)S(1)}, u32[]{:S(2)}, u32[]{:S(2)}) collective-permute-start(bf16[64,1848]{1,0:T(8,128)(2,1)S(1)} %get-tuple-element.63), channel_id=1, source_target_pairs={{0,16},{8,24},{16,0},{24,8},{1,17},{9,25},{17,1},{25,9},{2,18},{10... | collective-permute-start | bytes 709640 | tf_op jit(solution)/shard_map/ppermute | solution.py:31
  28.4 6.6 %collective-permute-start.17 = (bf16[16,2104]{1,0:T(8,128)(2,1)S(1)}, bf16[16,2104]{1,0:T(8,128)(2,1)S(1)}, u32[]{:S(2)}, u32[]{:S(2)}) collective-permute-start(bf16[16,2104]{1,0:T(8,128)(2,1)S(1)} %get-tuple-element.68), channel_id=1, source_target_pairs={{0,8},{8,0},{16,24},{24,16},{1,9},{9,1},{17,25},{25,17},{2,10},{10... | collective-permute-start | bytes 201992 | tf_op jit(solution)/shard_map/ppermute | solution.py:31
  28.6 7.0 %collective-permute-start.18 = (bf16[16,2104]{1,0:T(8,128)(2,1)S(1)}, bf16[16,2104]{1,0:T(8,128)(2,1)S(1)}, u32[]{:S(2)}, u32[]{:S(2)}) collective-permute-start(bf16[16,2104]{1,0:T(8,128)(2,1)S(1)} %get-tuple-element.69), channel_id=1, source_target_pairs={{0,16},{8,24},{16,0},{24,8},{1,17},{9,25},{17,1},{25,9},{2,18},{10... | collective-permute-start | bytes 201992 | tf_op jit(solution)/shard_map/ppermute | solution.py:31
  29.9 5.7 %collective-permute-start.19 = (bf16[16,2104]{1,0:T(8,128)(2,1)S(1)}, bf16[16,2104]{1,0:T(8,128)(2,1)S(1)}, u32[]{:S(2)}, u32[]{:S(2)}) collective-permute-start(bf16[16,2104]{1,0:T(8,128)(2,1)S(1)} %get-tuple-element.70), channel_id=1, source_target_pairs={{0,24},{8,16},{16,8},{24,0},{1,25},{9,17},{17,9},{25,1},{2,26},{10... | collective-permute-start | bytes 201992 | tf_op jit(solution)/shard_map/ppermute | solution.py:31

commit v5 on v4

v5 whole, which is shorter than its diff:
```python
import functools

import jax
import jax.numpy as jnp
from jax import lax
from jax.experimental import pallas as pl
from jax.experimental.pallas import tpu as pltpu
from jax.sharding import PartitionSpec as P

COMP = 16


ADAPTER_SCALING = 0.25
SPREAD_FLOOR = 0.16
F32 = jnp.float32
BF16 = jnp.bfloat16
LANES = 128
BLOCK = 8
PEAK_FLOPS, PEAK_BYTES = 1.15e9, 3.6e6
STEP = 512
NT = (((1,), (1,)), ((), ()))
TN = (((0,), (0,)), ((), ()))
VMEM = pl.BlockSpec(memory_space=pltpu.VMEM)
SMEM = pl.BlockSpec(memory_space=pltpu.SMEM)
HBM = pl.BlockSpec(memory_space=pltpu.HBM)
ANY = pl.BlockSpec(memory_space=pl.ANY)


def swap(array, axis, distance):
    size = lax.axis_size(axis)
    return lax.ppermute(array, axis, [(i, i ^ distance) for i in range(size)])


def swap_cores(array, axis, partner):
    size = lax.axis_size(axis)
    return lax.ppermute(array, axis, [(i, i ^ partner[i % 2]) for i in range(size)])


def swap_pair(array, partner):
    groups, size = lax.axis_size("group"), lax.axis_size("fsdp")
    return lax.ppermute(
        array,
        ("group", "fsdp"),
        [(g * size + f, (g ^ partner[f % 2]) * size + f) for g in range(groups) for f in range(size)],
    )


def sum_over_fsdp(partial, earlier):
    size = lax.axis_size("fsdp")
    if size & (size - 1):
        return lax.psum(partial, "fsdp")
    chip = partial + swap(partial, "fsdp", 1)
    if size == 8:
        one = swap_cores(chip, "fsdp", (2, 4))
        chip = after(chip, earlier) + swap(chip, "fsdp", 6)
        return chip + (one + swap(after(one, earlier), "fsdp", 1))
    parts = [chip] + [swap(chip, "fsdp", d) for d in range(2, size, 2)]
    while len(parts) > 1:
        parts = [parts[i] + parts[i + 1] for i in range(0, len(parts), 2)]
    return parts[0]


def after(array, earlier):
    return lax.optimization_barrier((array, earlier))[0]


def call(body, name, cost, outs, ins, scratch=(), out_specs=None):
    return pl.pallas_call(
        body,
        out_shape=outs,
        in_specs=ins,
        out_specs=out_specs or [VMEM] * len(outs),
        scratch_shapes=scratch,
        compiler_params=pltpu.CompilerParams(vmem_limit_bytes=8 << 20),
        cost_estimate=pl.CostEstimate(
            flops=int(cost * PEAK_FLOPS), bytes_accessed=int(cost * PEAK_BYTES), transcendentals=0
        ),
        name=name,
    )


def in_hbm(array):
    return pltpu.with_memory_space_constraint(array, pltpu.HBM)


def positions():
    own, member = lax.axis_index("group"), lax.axis_index("fsdp")
    return own, member, lax.rem(member, 2)


def start_all(pairs, sems, first=0):
    copies = [pltpu.make_async_copy(a, b, sems.at[first + i]) for i, (a, b) in enumerate(pairs)]
    for copy in copies:
        copy.start()
    return copies


def pack_kernel(groups, depth, hidden_ref, old_hbm, reward_hbm, length_hbm, dest_hbm, new_hbm, at_hbm, upstream_hbm, up_hbm, *rest):
    messages, table_ref, own_hidden = rest[: groups - 1], rest[groups - 1], rest[groups]
    new_ref, at_ref, upstream_ref, up_ref, back_ref = rest[groups + 1 : groups + 6]
    old_ref, reward_ref, length_ref, dest_ref, sems, small_sems = rest[groups + 6 :]
    own, _, core = positions()
    half = depth // 2
    small = start_all(
        [(old_hbm, old_ref), (reward_hbm, reward_ref), (length_hbm, length_ref), (dest_hbm, dest_ref)], small_sems
    )
    small += start_all([(upstream_hbm, upstream_ref), (up_hbm, up_ref)], small_sems, 4)
    pairs = []
    for d in reversed(range(1, groups)):
        start = pl.multiple_of((own ^ d) * depth + core * half, LANES)
        pairs.append((hidden_ref.at[:, pl.ds(start, half)], messages[d - 1]))
    pairs.append((hidden_ref.at[:, pl.ds(pl.multiple_of(own * depth, LANES), depth)], own_hidden))
    copies = start_all(pairs + [(new_hbm, new_ref), (at_hbm, at_ref)], sems)
    for copy in small:
        copy.wait()
    total, squares = jnp.float32(0), jnp.float32(0)
    for k in range(groups):
        total += reward_ref[0, k]
        squares += reward_ref[0, k] * reward_ref[0, k]
    old = old_ref[0]
    old = jnp.concatenate([old, jnp.zeros((groups, LANES - old.shape[1]), F32)], axis=1)
    for d in range(groups):
        line, reward, length = jnp.zeros((1, LANES), F32), jnp.float32(0), jnp.float32(0)
        for k in range(groups):
            chosen = dest_ref[0, k] == (own ^ d)
            line = jnp.where(chosen, old[k : k + 1], line)
            reward = jnp.where(chosen, reward_ref[0, k], reward)
            length = jnp.where(chosen, length_ref[0, k].astype(F32), length)
        lines = [line] + [jnp.full((1, LANES), x, F32) for x in (reward, length, total, squares)]
        table_ref[d * BLOCK : (d + 1) * BLOCK] = jnp.concatenate(
            lines + [jnp.zeros((BLOCK - len(lines), LANES), F32)], axis=0
        )
    back_ref[...] = lax.dot_general(upstream_ref[...], up_ref[...], NT, preferred_element_type=F32)
    for copy in copies:
        copy.wait()


def whole_rows(half, core, message, other):
    a, b = message[:, :half], other[:, :half]
    first = core == 0
    return jnp.concatenate([jnp.where(first, a, b), jnp.where(first, b, a)], axis=1)


def first_kernel(held_ref, at_ref, own_hidden, *refs):
    *messages, sums_ref, low_ref = refs
    messages = messages[::-1]
    units, depth = held_ref.shape
    half = depth // 2
    mine = pl.ds(pl.multiple_of(positions()[2] * half, LANES), half)
    rows = jnp.concatenate([own_hidden[:, mine]] + [ref[...] for ref in messages], axis=0)
    low_ref[...] = lax.dot_general(rows, at_ref[:, mine], NT, preferred_element_type=F32)
    rows = rows.T
    for start in range(0, units, STEP):
        end = min(start + STEP, units)
        sums_ref[start:end] = jnp.dot(held_ref[start:end, mine], rows, preferred_element_type=F32)


def second_kernel(groups, held_ref, at_ref, own_hidden, table_ref, sums_ref, low_ref, *refs):
    count = groups - 1
    others, refs = refs[:count][::-1], refs[count:]
    far, early, late, kept, nears, lows = *refs[:4], refs[4 : groups], refs[groups:]
    units, depth = held_ref.shape
    tokens, rank = own_hidden.shape[0], low_ref.shape[1]
    half = depth // 2
    core = positions()[2]
    rest = pl.ds(pl.multiple_of((1 - core) * half, LANES), half)
    rows = jnp.concatenate([own_hidden[:, rest]] + [ref[...] for ref in others], axis=0)
    low = low_ref[...] + lax.dot_general(rows, at_ref[:, rest], NT, preferred_element_type=F32)
    for i, ref in enumerate(lows):
        ref[:tokens] = low[i * tokens : (i + 1) * tokens]
        ref[tokens:] = table_ref[i * BLOCK : (i + 1) * BLOCK, :rank]
    rows = rows.T
    for start in range(0, units, STEP):
        end = min(start + STEP, units)
        result = sums_ref[start:end] + jnp.dot(held_ref[start:end, rest], rows, preferred_element_type=F32)
        result = result.T
        parts = [result[i * tokens : (i + 1) * tokens] for i in range(groups)]
        kept[:, start:end] = parts[0]
        far[:, start:end] = parts[-1].astype(BF16)
        early[:, start:end] = jnp.where(core == 0, parts[1], parts[-2]).astype(BF16)
        late[:, start:end] = jnp.where(core == 0, parts[-2], parts[1])
        for ref, part in zip(nears, parts[2:-2]):
            ref[:, start:end] = part.astype(BF16)


def add_kernel(late, came, out):
    out[...] = (late[...] + came[...].astype(F32)).astype(BF16)


def token_coefs(groups, new_ref, tables):
    own = positions()[0]
    lanes = tables[0].shape[1]
    ordered = []
    for j in range(groups):
        table = tables[0]
        for d in range(1, groups):
            table = jnp.where((own ^ j) == d, tables[d], table)
        ordered.append(table)
    length = new_ref.shape[2]
    place = lax.broadcasted_iota(jnp.int32, (1, lanes), 1)
    diagonal = lax.broadcasted_iota(jnp.int32, (length, lanes), 0) == lax.broadcasted_iota(jnp.int32, (length, lanes), 1)
    new = new_ref[0]
    new = jnp.concatenate([new, jnp.zeros((groups, lanes - length), F32)], axis=1)
    together = COMP // groups
    parts = []
    loss = jnp.zeros((1, lanes), F32)
    for j in range(groups):
        prompt = ordered[j // together * together : (j // together + 1) * together]
        mean = sum(table[3:4] for table in prompt) / COMP
        square = sum(table[4:5] for table in prompt) / COMP
        spread = jnp.sqrt(jnp.maximum(square - mean * mean, SPREAD_FLOOR))
        old, reward, count = ordered[j][0:1], ordered[j][1:2], ordered[j][2:3]
        advantage = (reward - mean) / spread
        ratio = jnp.exp(new[j : j + 1] - old)
        live = (place.astype(F32) < count) & (place < length)
        coef = jnp.where(live, -(advantage * ratio) / (count * COMP), 0.0)
        loss = loss + coef
        column = jnp.sum(jnp.where(diagonal, coef, 0.0), axis=1, keepdims=True)
        parts.append(column)
    return jnp.concatenate(parts, axis=0), jnp.sum(loss, axis=1, keepdims=True)


def adapter_kernel(groups, share, ride_rows, *refs):
    lows, (back_ref, new_ref, upstream_ref) = refs[:groups][::-1], refs[groups : groups + 3]
    messages, (own_term, own_back, low_ref, loss_ref, term) = refs[groups + 3 : 2 * groups + 2], refs[2 * groups + 2 :]
    own = positions()[0]
    rank = term.shape[0]
    tokens = back_ref.shape[0]
    coef, loss_ref[...] = token_coefs(groups, new_ref, [ref[tokens:] for ref in lows])
    low = lows[0][:tokens]
    for ref in lows[1:]:
        low = low + ref[:tokens]
    low = low.astype(BF16)
    low_ref[...] = low
    gradient = (coef * upstream_ref[...].astype(F32)).astype(BF16)
    term[...] = ADAPTER_SCALING * lax.dot_general(low, gradient, TN, preferred_element_type=F32)
    back = coef * back_ref[...]
    own_back[...] = back.astype(BF16)
    stack = back.shape[0] // ride_rows
    ride = jnp.concatenate([back[i * ride_rows : (i + 1) * ride_rows] for i in range(stack)], axis=1).astype(BF16)
    lanes = stack * rank
    for d in range(groups):
        if share % 8 == 0:
            piece = term[pl.ds(pl.multiple_of((own ^ d) * share, share), share), :]
        else:
            piece = term[:share]
            for j in range(1, groups):
                piece = jnp.where((own ^ d) == j, term[j * share : (j + 1) * share], piece)
        if d == 0:
            own_term[...] = piece
            continue
        if share < ride_rows:
            piece = jnp.concatenate([piece, jnp.zeros((ride_rows - share, piece.shape[1]), F32)], axis=0)
        messages[d - 1][:, :lanes] = ride
        messages[d - 1][:, lanes:] = piece.astype(BF16)


def output_kernel(total_ref, low_ref, up_ref, *rest):
    total = total_ref[...] + ADAPTER_SCALING * jnp.dot(low_ref[...], up_ref[...], preferred_element_type=F32)
    for ref in rest[:-2]:
        total = total + ref[...].astype(F32)
    rest[-2][...] = total.astype(BF16)
    rest[-1][...] = jnp.zeros_like(rest[-1])


def gradient_kernel(groups, rank, share, ride_rows, written, own_term, own_back, own_hidden, *rest):
    arrived, messages, others = (rest[i * (groups - 1) : (i + 1) * (groups - 1)][::-1] for i in range(3))
    up_hbm, down_hbm, up_ref, down_ref, sems = rest[3 * (groups - 1) :]
    core = positions()[2]
    tokens, depth = own_hidden.shape
    half = depth // 2
    stack = tokens // ride_rows
    lanes = stack * rank
    backs = [own_back[...].astype(F32)]
    for come in arrived:
        ride = come[:, :lanes].astype(F32)
        backs += [ride[:, i * rank : (i + 1) * rank] for i in range(stack)]
    back = jnp.concatenate(backs, axis=0).astype(BF16)
    copies = []
    for i in range(2):
        span = slice(i * half, (i + 1) * half)
        rows = [own_hidden[:, span]]
        rows += [jnp.where(core == i, a[...], b[...]) for a, b in zip(messages, others)]
        rows = jnp.concatenate(rows, axis=0)
        down_ref[:, span] = ADAPTER_SCALING * lax.dot_general(back, rows, TN, preferred_element_type=F32)
        copies += start_all([(down_ref.at[:, span], down_hbm.at[:, span])], sems, i)
    total = own_term[...]
    for come in arrived:
        total = total + come[:, lanes:].astype(F32)[:share]
    up_ref[...] = total
    copies += start_all([(up_ref, up_hbm)], sems, 2)
    for copy in copies:
        copy.wait()


def on_device(
    hidden_input_slots,
    base_weight,
    adapter_a,
    adapter_up_matrix,
    upstream,
    logp_new,
    logp_old,
    rewards,
    comp_lengths,
    assignment,
):
    groups = lax.axis_size("group")
    tokens = hidden_input_slots.shape[0]
    depth, units = base_weight.shape
    half = depth // 2
    rank = adapter_a.shape[1]
    others = range(1, groups)
    at, weight = adapter_a.T, base_weight.T

    *messages, table, own_hidden, new, at, upstream, up, back = call(
        functools.partial(pack_kernel, groups, depth),
        "pack",
        1.8,
        [pltpu.VMEM((tokens, half), BF16)] * (groups - 1)
        + [
            pltpu.VMEM((groups * BLOCK, LANES), F32),
            pltpu.VMEM((tokens, depth), BF16),
            pltpu.VMEM(logp_new.shape, F32),
            pltpu.VMEM((rank, depth), BF16),
            pltpu.VMEM((tokens, units), BF16),
            pltpu.VMEM((rank, units), BF16),
            pltpu.VMEM((tokens, rank), F32),
        ],
        [HBM] * 9,
        scratch=[
            pltpu.VMEM(logp_old.shape, F32),
            pltpu.SMEM(rewards.shape, F32),
            pltpu.SMEM(comp_lengths.shape, jnp.int32),
            pltpu.SMEM(assignment.shape, jnp.int32),
            pltpu.SemaphoreType.DMA((groups + 2,)),
            pltpu.SemaphoreType.DMA((6,)),
        ],
    )(
        *map(
            in_hbm,
            (
                hidden_input_slots,
                logp_old,
                rewards,
                comp_lengths,
                assignment,
                logp_new,
                at,
                upstream,
                adapter_up_matrix,
            ),
        )
    )
    got = {d: swap(messages[d - 1], "group", d) for d in reversed(others)}
    held = pltpu.with_memory_space_constraint(weight, pltpu.VMEM)
    far, near = groups - 1, list(range(1, groups - 1))
    held_sums, held_lows = call(
        first_kernel,
        "first",
        1.5,
        [pltpu.VMEM((units, groups * tokens), F32), pltpu.VMEM((groups * tokens, rank), F32)],
        [VMEM] * (2 + groups),
    )(held, at, own_hidden, *[got[d] for d in reversed(others)])
    back = sum_over_fsdp(back, held_lows)
    theirs = {d: swap(got[d], "fsdp", 1) for d in reversed(others)}
    far_term, early, late, kept, *terms = call(
        functools.partial(second_kernel, groups),
        "second",
        1.5,
        [
            pltpu.VMEM((tokens, units), BF16),
            pltpu.VMEM((tokens, units), BF16),
            pltpu.VMEM((tokens, units), F32),
            pltpu.VMEM((tokens, units), F32),
        ]
        + [pltpu.VMEM((tokens, units), BF16)] * (groups - 4)
        + [pltpu.VMEM((tokens + BLOCK, rank), F32)] * groups,
        [VMEM] * (5 + groups),
    )(held, at, own_hidden, table, held_sums, held_lows, *[theirs[d] for d in reversed(others)])
    own_low, *lows = terms[groups - 4 :]
    came = [swap(term, "group", d) for d, term in enumerate(terms[: groups - 4], 2)]
    ways = (1, far ^ 1)
    far_term = swap_pair(far_term, ways)
    came.append(swap_pair(early, ways))
    lows = [swap(lows[d - 1], "group", d) for d in reversed(others)][::-1]
    (late,) = call(add_kernel, "add", 0.5, [pltpu.VMEM((tokens, units), BF16)], [VMEM] * 2)(late, far_term)
    came.append(swap_pair(late, ways[::-1]))

    share = rank // groups
    ride_rows = max(share, 16)
    lanes = tokens // ride_rows * rank
    *pieces, own_term, own_back, low, loss = call(
        functools.partial(adapter_kernel, groups, share, ride_rows),
        "adapter",
        4.0,
        [pltpu.VMEM((ride_rows, lanes + units), BF16)] * (groups - 1)
        + [
            pltpu.VMEM((share, units), F32),
            pltpu.VMEM((tokens, rank), BF16),
            pltpu.VMEM((tokens, rank), BF16),
            jax.ShapeDtypeStruct((1, 1), F32),
        ],
        [VMEM] * (groups + 3),
        scratch=[pltpu.VMEM((rank, units), F32)],
    )(*lows[::-1], own_low, back, new, upstream)
    arrived = {d: swap(pieces[d - 1], "group", d) for d in reversed(others)}
    projection_output, written = call(
        output_kernel,
        "output",
        1.0,
        [jax.ShapeDtypeStruct((tokens, units), BF16), pltpu.VMEM((8, LANES), F32)],
        [VMEM] * (3 + len(came)),
    )(kept, low, up, *came)
    gradient_up, gradient_down = call(
        functools.partial(gradient_kernel, groups, rank, share, ride_rows),
        "gradient",
        1.2,
        [jax.ShapeDtypeStruct((share, units), F32), jax.ShapeDtypeStruct((rank, depth), F32)],
        [ANY] + [VMEM] * (3 * groups),
        scratch=[
            pltpu.VMEM((share, units), F32),
            pltpu.VMEM((rank, depth), F32),
            pltpu.SemaphoreType.DMA((3,)),
        ],
        out_specs=[HBM] * 2,
    )(
        written,
        own_term,
        own_back,
        own_hidden,
        *[arrived[d] for d in reversed(others)],
        *[got[d] for d in reversed(others)],
        *[theirs[d] for d in reversed(others)],
    )
    return (projection_output, gradient_down.T, gradient_up, loss[0])


def solution(mesh):
    return jax.shard_map(
        on_device,
        mesh=mesh,
        in_specs=(
            P("group", None),
            P("group", "fsdp"),
            P("group", None),
            P(None, "fsdp"),
            P("group", "fsdp"),
            P("group", None, None),
            P("group", None, None),
            P("group", None),
            P("group", None),
            P("group", None),
        ),
        out_specs=(P("group", "fsdp"), P("group", None), P("group", "fsdp"), P("group")),
        check_vma=False,
    )
```

time: 36.9 us -> 34.8 us (0.943)
  waiting for transfers between devices: 6.52 us -> 5.37 us
  starting transfers between devices: 21.9 us -> 21.1 us
    ppermute x19 -> x15, starting transfers between devices: 19.9 us -> 15.2 us  [swap(): return lax.ppermute(array, axis, [(i, i ^ distance) for i in range(size)])]
    ppermute x19 -> x15, waiting for transfers between devices: 6.52 us -> 2.5 us  [swap(): return lax.ppermute(array, axis, [(i, i ^ distance) for i in range(size)])]
    ppermute x0 -> x3, starting transfers between devices: none -> 3.93 us  [swap_pair(): lax.ppermute(array, ('group', 'fsdp'), [(g * size + f, (g ^ partner[f % 2...]
    ppermute x0 -> x3, waiting for transfers between devices: none -> 2.87 us  [swap_pair(): lax.ppermute(array, ('group', 'fsdp'), [(g * size + f, (g ^ partner[f % 2...]
    pallas_call x3, Pallas kernels: 3.32 us -> 2.82 us  [the longest x1 1.47 us: on_device(): call(functools.partial(second_kernel, groups), 'second', 1.5, [pltpu.VMEM...]
    pallas_call x1, Pallas kernels: 0.32 us -> 0.74 us  [on_device(): call(functools.partial(adapter_kernel, groups, share, ride_rows), 'adapte...]
  transfers between devices with their start and end apart: 20 -> 19, of which waited for: 8 -> 7; matrix products, arithmetic and copies ran while one was open for 0% -> 0% of each run, Pallas kernels for 12% -> 13%
where the time goes in v5:
time: 34.8 us; the launch traced here: 34.7 us
  starting transfers between devices  21.1 us (61%)
  Pallas kernels  7.49 us (22%)
  waiting for transfers between devices  5.37 us (15%)
  between operations  0.71 us (2%)
    ppermute x15, starting transfers between devices, swap(): return lax.ppermute(array, axis, [(i, i ^ distance) for i in range(size)])  15.2 us
    ppermute x3, starting transfers between devices, swap_pair(): lax.ppermute(array, ('group', 'fsdp'), [(g * size + f, (g ^ partner[f % 2...  3.93 us
    ppermute x3, waiting for transfers between devices, swap_pair(): lax.ppermute(array, ('group', 'fsdp'), [(g * size + f, (g ^ partner[f % 2...  2.87 us
    ppermute x15, waiting for transfers between devices, swap(): return lax.ppermute(array, axis, [(i, i ^ distance) for i in range(size)])  2.5 us
    ppermute x1, starting transfers between devices, swap_cores(): lax.ppermute(array, axis, [(i, i ^ partner[i % 2]) for i in range(size)])  1.97 us
    pallas_call x1, Pallas kernels, on_device(): call(functools.partial(pack_kernel, groups, depth), 'pack', 1.8, [pltpu.V...  1.81 us
    pallas_call x1, Pallas kernels, on_device(): call(functools.partial(second_kernel, groups), 'second', 1.5, [pltpu.VMEM...  1.47 us
    pallas_call x1, Pallas kernels, on_device(): call(first_kernel, 'first', 1.5, [pltpu.VMEM((units, groups * tokens), F3...  1.29 us
  transfers between devices with their start and end apart: 19, of which 7 were waited for; matrix products, arithmetic and copies ran while one was open for 0% of the time, Pallas kernels for 13%

profile of v5, /device:TPU:0, one launch (start us, length us, event | category | flops | bytes accessed | tf_op | source)
XLA Modules:
  0.0 34.7 jit_solution(9918937261294334069)
XLA Ops:
  0.6 1.8 %pack.1 = (bf16[64,1024]{1,0:T(8,128)(2,1)S(1)}, bf16[64,1024]{1,0:T(8,128)(2,1)S(1)}, bf16[64,1024]{1,0:T(8,128)(2,1)S(1)}, f32[32,128]{1,0:T(8,128)S(1)}, bf16...) custom-call(bf16[64,8192]{1,0:T(8,128)(2,1)} %hidden_ref.1, ...), custom_call_target="tpu_custom_call" | custom-call | flops 2070000000 | bytes 6480000 | tf_op jit(solution)/shard_map/pack/pallas_call | solution.py:316
  2.5 4.0 %collective-permute-start = (bf16[64,1024]{1,0:T(8,128)(2,1)S(1)}, bf16[64,1024]{1,0:T(8,128)(2,1)S(1)}, u32[]{:S(2)}, u32[]{:S(2)}) collective-permute-start(bf16[64,1024]{1,0:T(8,128)(2,1)S(1)} %get-tuple-element.40), channel_id=1, source_target_pairs={{0,24},{8,16},{16,8},{24,0},{1,25},{9,17},{17,9},{25,1},{2,26},{10... | collective-permute-start | bytes 393224 | tf_op jit(solution)/shard_map/ppermute | solution.py:31
  6.4 0.5 %collective-permute-start.1 = (bf16[64,1024]{1,0:T(8,128)(2,1)S(1)}, bf16[64,1024]{1,0:T(8,128)(2,1)S(1)}, u32[]{:S(2)}, u32[]{:S(2)}) collective-permute-start(bf16[64,1024]{1,0:T(8,128)(2,1)S(1)} %get-tuple-element.41), channel_id=1, source_target_pairs={{0,16},{8,24},{16,0},{24,8},{1,17},{9,25},{17,1},{25,9},{2,18},{10... | collective-permute-start | bytes 393224 | tf_op jit(solution)/shard_map/ppermute | solution.py:31
  7.1 1.2 %collective-permute-done.9 = f32[64,64]{1,0:T(8,128)S(1)} collective-permute-done((f32[64,64]{1,0:T(8,128)S(1)}, f32[64,64]{1,0:T(8,128)S(1)}, u32[]{:S(2)}, u32[]{:S(2)}) %collective-permute-start.9) | collective-permute-done | bytes 16416 | tf_op jit(solution)/shard_map/ppermute | solution.py:31
  8.3 2.0 %collective-permute-start.11 = (f32[64,64]{1,0:T(8,128)S(1)}, f32[64,64]{1,0:T(8,128)S(1)}, u32[]{:S(2)}, u32[]{:S(2)}) collective-permute-start(f32[64,64]{1,0:T(8,128)S(1)} %add.13), channel_id=1, source_target_pairs={{0,2},{1,5},{2,0},{3,7},{4,6},{5,1},{6,4},{7,3},{8,10},{9,13},{10,... | collective-permute-start | bytes 49160 | tf_op jit(solution)/shard_map/ppermute | solution.py:36
  10.3 2.5 %collective-permute-start.10 = (f32[64,64]{1,0:T(8,128)S(1)}, f32[64,64]{1,0:T(8,128)S(1)}, u32[]{:S(2)}, u32[]{:S(2)}) collective-permute-start(f32[64,64]{1,0:T(8,128)S(1)} %add.13), channel_id=1, source_target_pairs={{0,6},{1,7},{2,4},{3,5},{4,2},{5,3},{6,0},{7,1},{8,14},{9,15},{10,... | collective-permute-start | bytes 49160 | tf_op jit(solution)/shard_map/ppermute | solution.py:31
  13.3 1.3 %first.1 = (f32[1848,256]{1,0:T(8,128)S(1)}, f32[256,64]{1,0:T(8,128)S(1)}) custom-call(bf16[1848,2048]{1,0:T(8,128)(2,1)S(1)} %bitcast.4, bf16[64,2048]{1,0:T(8,128)(2,1)S(1)} %get-tuple-element.37.at_ref, bf16[64,2048]{1,0:T(8,128)(2,1)S(1)} %get-tuple-element.38.own_hidden, bf16[64,1024]{1,0:T(8,128)(2,1)S(1)} %collective-permute-done.refs_0_.rest_3_, ...), custom_call_target="tpu_custom_call" | custom-call | flops 1724999936 | bytes 5400000 | tf_op jit(solution)/shard_map/first/pallas_call | solution.py:358
  15.2 1.5 %second.1 = (bf16[64,1848]{1,0:T(8,128)(2,1)S(1)}, bf16[64,1848]{1,0:T(8,128)(2,1)S(1)}, f32[64,1848]{1,0:T(8,128)S(1)}, f32[64,1848]{1,0:T(8,128)S(1)}, f32[72,...) custom-call(bf16[1848,2048]{1,0:T(8,128)(2,1)S(1)} %bitcast.5, ...), custom_call_target="tpu_custom_call" | custom-call | flops 1724999936 | bytes 5400000 | tf_op jit(solution)/shard_map/second/pallas_call | solution.py:367
  16.6 1.6 %collective-permute-start.14 = (bf16[64,1848]{1,0:T(8,128)(2,1)S(1)}, bf16[64,1848]{1,0:T(8,128)(2,1)S(1)}, u32[]{:S(2)}, u32[]{:S(2)}) collective-permute-start(bf16[64,1848]{1,0:T(8,128)(2,1)S(1)} %get-tuple-element.59), channel_id=1, source_target_pairs={{0,8},{1,17},{2,10},{3,19},{4,12},{5,21},{6,14},{7,23},{8,0},{9,25... | collective-permute-start | bytes 709640 | tf_op jit(solution)/shard_map/ppermute | solution.py:41
  18.2 1.6 %collective-permute-start.6 = (f32[72,64]{1,0:T(8,128)S(1)}, f32[72,64]{1,0:T(8,128)S(1)}, u32[]{:S(2)}, u32[]{:S(2)}) collective-permute-start(f32[72,64]{1,0:T(8,128)S(1)} %get-tuple-element.46), channel_id=1, source_target_pairs={{0,24},{8,16},{16,8},{24,0},{1,25},{9,17},{17,9},{25,1},{2,26},{10... | collective-permute-start | bytes 55304 | tf_op jit(solution)/shard_map/ppermute | solution.py:31
  19.8 0.5 %collective-permute-start.7 = (f32[72,64]{1,0:T(8,128)S(1)}, f32[72,64]{1,0:T(8,128)S(1)}, u32[]{:S(2)}, u32[]{:S(2)}) collective-permute-start(f32[72,64]{1,0:T(8,128)S(1)} %get-tuple-element.47), channel_id=1, source_target_pairs={{0,16},{8,24},{16,0},{24,8},{1,17},{9,25},{17,1},{25,9},{2,18},{10... | collective-permute-start | bytes 55304 | tf_op jit(solution)/shard_map/ppermute | solution.py:31
  20.3 1.5 %collective-permute-start.8 = (f32[72,64]{1,0:T(8,128)S(1)}, f32[72,64]{1,0:T(8,128)S(1)}, u32[]{:S(2)}, u32[]{:S(2)}) collective-permute-start(f32[72,64]{1,0:T(8,128)S(1)} %get-tuple-element.48), channel_id=1, source_target_pairs={{0,8},{8,0},{16,24},{24,16},{1,9},{9,1},{17,25},{25,17},{2,10},{10... | collective-permute-start | bytes 55304 | tf_op jit(solution)/shard_map/ppermute | solution.py:31
  21.8 0.5 %collective-permute-start.13 = (bf16[64,1848]{1,0:T(8,128)(2,1)S(1)}, bf16[64,1848]{1,0:T(8,128)(2,1)S(1)}, u32[]{:S(2)}, u32[]{:S(2)}) collective-permute-start(bf16[64,1848]{1,0:T(8,128)(2,1)S(1)} %get-tuple-element.57), channel_id=1, source_target_pairs={{0,8},{1,17},{2,10},{3,19},{4,12},{5,21},{6,14},{7,23},{8,0},{9,25... | collective-permute-start | bytes 709640 | tf_op jit(solution)/shard_map/ppermute | solution.py:41
  22.3 1.1 %collective-permute-done.14.came = bf16[64,1848]{1,0:T(8,128)(2,1)S(1)} collective-permute-done((bf16[64,1848]{1,0:T(8,128)(2,1)S(1)}, bf16[64,1848]{1,0:T(8,128)(2,1)S(1)}, u32[]{:S(2)}, u32[]{:S(2)}) %collective-permute-start.14) | collective-permute-done | bytes 236576 | tf_op jit(solution)/shard_map/ppermute | solution.py:41
  23.5 1.8 %collective-permute-start.15 = (bf16[64,1848]{1,0:T(8,128)(2,1)S(1)}, bf16[64,1848]{1,0:T(8,128)(2,1)S(1)}, u32[]{:S(2)}, u32[]{:S(2)}) collective-permute-start(bf16[64,1848]{1,0:T(8,128)(2,1)S(1)} %add.20), channel_id=1, source_target_pairs={{0,16},{1,9},{2,18},{3,11},{4,20},{5,13},{6,22},{7,15},{8,24},{9,1... | collective-permute-start | bytes 709640 | tf_op jit(solution)/shard_map/ppermute | solution.py:41
  25.3 0.7 %adapter.1 = (bf16[16,2104]{1,0:T(8,128)(2,1)S(1)}, bf16[16,2104]{1,0:T(8,128)(2,1)S(1)}, bf16[16,2104]{1,0:T(8,128)(2,1)S(1)}, f32[16,1848]{1,0:T(8,128)S(1)}, ...) custom-call(f32[72,64]{1,0:T(8,128)S(1)} %collective-permute-done.6.refs_0_, ...), custom_call_target="tpu_custom_call" | custom-call | flops 4600000000 | bytes 14400000 | tf_op jit(solution)/shard_map/adapter/pallas_call | solution.py:393
  26.1 1.6 %collective-permute-start.16 = (bf16[16,2104]{1,0:T(8,128)(2,1)S(1)}, bf16[16,2104]{1,0:T(8,128)(2,1)S(1)}, u32[]{:S(2)}, u32[]{:S(2)}) collective-permute-start(bf16[16,2104]{1,0:T(8,128)(2,1)S(1)} %get-tuple-element.64), channel_id=1, source_target_pairs={{0,24},{8,16},{16,8},{24,0},{1,25},{9,17},{17,9},{25,1},{2,26},{10... | collective-permute-start | bytes 201992 | tf_op jit(solution)/shard_map/ppermute | solution.py:31
  27.6 1.4 %collective-permute-start.17 = (bf16[16,2104]{1,0:T(8,128)(2,1)S(1)}, bf16[16,2104]{1,0:T(8,128)(2,1)S(1)}, u32[]{:S(2)}, u32[]{:S(2)}) collective-permute-start(bf16[16,2104]{1,0:T(8,128)(2,1)S(1)} %get-tuple-element.65), channel_id=1, source_target_pairs={{0,16},{8,24},{16,0},{24,8},{1,17},{9,25},{17,1},{25,9},{2,18},{10... | collective-permute-start | bytes 201992 | tf_op jit(solution)/shard_map/ppermute | solution.py:31
  29.0 0.5 %collective-permute-start.18 = (bf16[16,2104]{1,0:T(8,128)(2,1)S(1)}, bf16[16,2104]{1,0:T(8,128)(2,1)S(1)}, u32[]{:S(2)}, u32[]{:S(2)}) collective-permute-start(bf16[16,2104]{1,0:T(8,128)(2,1)S(1)} %get-tuple-element.66), channel_id=1, source_target_pairs={{0,8},{8,0},{16,24},{24,16},{1,9},{9,1},{17,25},{25,17},{2,10},{10... | collective-permute-start | bytes 201992 | tf_op jit(solution)/shard_map/ppermute | solution.py:31
  29.6 1.0 %collective-permute-done.13.rest_0_ = bf16[64,1848]{1,0:T(8,128)(2,1)S(1)} collective-permute-done((bf16[64,1848]{1,0:T(8,128)(2,1)S(1)}, bf16[64,1848]{1,0:T(8,128)(2,1)S(1)}, u32[]{:S(2)}, u32[]{:S(2)}) %collective-permute-start.13) | collective-permute-done | bytes 236576 | tf_op jit(solution)/shard_map/ppermute | solution.py:41
  30.6 0.7 %collective-permute-done.15.rest_1_ = bf16[64,1848]{1,0:T(8,128)(2,1)S(1)} collective-permute-done((bf16[64,1848]{1,0:T(8,128)(2,1)S(1)}, bf16[64,1848]{1,0:T(8,128)(2,1)S(1)}, u32[]{:S(2)}, u32[]{:S(2)}) %collective-permute-start.15) | collective-permute-done | bytes 236576 | tf_op jit(solution)/shard_map/ppermute | solution.py:41
  31.3 0.9 %output.1 = (bf16[64,1848]{1,0:T(8,128)(2,1)}, f32[8,128]{1,0:T(8,128)S(1)}) custom-call(f32[64,1848]{1,0:T(8,128)S(1)} %get-tuple-element.45.total_ref, bf16[64,64]{1,0:T(8,128)(2,1)S(1)} %get-tuple-element.55.low_ref, bf16[64,1848]{1,0:T(8,128)(2,1)S(1)} %get-tuple-element.56.up_ref, bf16[64,1848]{1,0:T(8,128)(2,1)S(1)} %collective-permute-done.13.rest_0_, ...), custom_call_target="tpu_custom_call" | custom-call | flops 1150000000 | bytes 3600000 | tf_op jit(solution)/shard_map/output/pallas_call | solution.py:408
  32.2 0.8 %collective-permute-done.16.rest_0_ = bf16[16,2104]{1,0:T(8,128)(2,1)S(1)} collective-permute-done((bf16[16,2104]{1,0:T(8,128)(2,1)S(1)}, bf16[16,2104]{1,0:T(8,128)(2,1)S(1)}, u32[]{:S(2)}, u32[]{:S(2)}) %collective-permute-start.16) | collective-permute-done | bytes 67360 | tf_op jit(solution)/shard_map/ppermute | solution.py:31
  33.5 1.2 %gradient.1 = (f32[16,1848]{1,0:T(8,128)}, f32[64,2048]{1,0:T(8,128)}) custom-call(f32[8,128]{1,0:T(8,128)S(1)} %get-tuple-element.61.written, f32[16,1848]{1,0:T(8,128)S(1)} %get-tuple-element.62.own_term, bf16[64,64]{1,0:T(8,128)(2,1)S(1)} %get-tuple-element.63.own_back, bf16[64,2048]{1,0:T(8,128)(2,1)S(1)} %get-tuple-element.38.own_hidden, ...), custom_call_target="tpu_custom_call" | custom-call | flops 1380000000 | bytes 4320000 | tf_op jit(solution)/shard_map/gradient/pallas_call | solution.py:415
  (25 shorter events, 1.8 us)
Async XLA Ops:
  0.6 12.7 %copy-start = (bf16[2048,1848]{0,1:T(8,128)(2,1)S(1)}, bf16[2048,1848]{0,1:T(8,128)(2,1)}, u32[]{:S(2)}) copy-start(bf16[2048,1848]{0,1:T(8,128)(2,1)} %param.11) | copy-start | bytes 22708228
  2.5 10.3 %collective-permute-start = (bf16[64,1024]{1,0:T(8,128)(2,1)S(1)}, bf16[64,1024]{1,0:T(8,128)(2,1)S(1)}, u32[]{:S(2)}, u32[]{:S(2)}) collective-permute-start(bf16[64,1024]{1,0:T(8,128)(2,1)S(1)} %get-tuple-element.40), channel_id=1, source_target_pairs={{0,24},{8,16},{16,8},{24,0},{1,25},{9,17},{17,9},{25,1},{2,26},{10... | collective-permute-start | bytes 393224 | tf_op jit(solution)/shard_map/ppermute | solution.py:31
  6.4 6.3 %collective-permute-start.1 = (bf16[64,1024]{1,0:T(8,128)(2,1)S(1)}, bf16[64,1024]{1,0:T(8,128)(2,1)S(1)}, u32[]{:S(2)}, u32[]{:S(2)}) collective-permute-start(bf16[64,1024]{1,0:T(8,128)(2,1)S(1)} %get-tuple-element.41), channel_id=1, source_target_pairs={{0,16},{8,24},{16,0},{24,8},{1,17},{9,25},{17,1},{25,9},{2,18},{10... | collective-permute-start | bytes 393224 | tf_op jit(solution)/shard_map/ppermute | solution.py:31
  6.9 6.3 %collective-permute-start.2 = (bf16[64,1024]{1,0:T(8,128)(2,1)S(1)}, bf16[64,1024]{1,0:T(8,128)(2,1)S(1)}, u32[]{:S(2)}, u32[]{:S(2)}) collective-permute-start(bf16[64,1024]{1,0:T(8,128)(2,1)S(1)} %get-tuple-element.42), channel_id=1, source_target_pairs={{0,8},{8,0},{16,24},{24,16},{1,9},{9,1},{17,25},{25,17},{2,10},{10... | collective-permute-start | bytes 393224 | tf_op jit(solution)/shard_map/ppermute | solution.py:31
  7.1 1.2 %collective-permute-start.9 = (f32[64,64]{1,0:T(8,128)S(1)}, f32[64,64]{1,0:T(8,128)S(1)}, u32[]{:S(2)}, u32[]{:S(2)}) collective-permute-start(f32[64,64]{1,0:T(8,128)S(1)} %get-tuple-element.50), channel_id=1, source_target_pairs={{0,1},{1,0},{2,3},{3,2},{4,5},{5,4},{6,7},{7,6},{8,9},{9,8},{10,11... | collective-permute-start | bytes 49160 | tf_op jit(solution)/shard_map/ppermute | solution.py:31
  8.3 6.3 %collective-permute-start.11 = (f32[64,64]{1,0:T(8,128)S(1)}, f32[64,64]{1,0:T(8,128)S(1)}, u32[]{:S(2)}, u32[]{:S(2)}) collective-permute-start(f32[64,64]{1,0:T(8,128)S(1)} %add.13), channel_id=1, source_target_pairs={{0,2},{1,5},{2,0},{3,7},{4,6},{5,1},{6,4},{7,3},{8,10},{9,13},{10,... | collective-permute-start | bytes 49160 | tf_op jit(solution)/shard_map/ppermute | solution.py:36
  10.3 7.9 %collective-permute-start.10 = (f32[64,64]{1,0:T(8,128)S(1)}, f32[64,64]{1,0:T(8,128)S(1)}, u32[]{:S(2)}, u32[]{:S(2)}) collective-permute-start(f32[64,64]{1,0:T(8,128)S(1)} %add.13), channel_id=1, source_target_pairs={{0,6},{1,7},{2,4},{3,5},{4,2},{5,3},{6,0},{7,1},{8,14},{9,15},{10,... | collective-permute-start | bytes 49160 | tf_op jit(solution)/shard_map/ppermute | solution.py:31
  12.7 2.4 %collective-permute-start.3 = (bf16[64,1024]{1,0:T(8,128)(2,1)S(1)}, bf16[64,1024]{1,0:T(8,128)(2,1)S(1)}, u32[]{:S(2)}, u32[]{:S(2)}) collective-permute-start(bf16[64,1024]{1,0:T(8,128)(2,1)S(1)} %collective-permute-done.refs_0_.rest_3_), channel_id=1, source_target_pairs={{0,1},{1,0},{2,3},{3,2},{4,5},{5,4},{6,7},{7,6},{8,9},{9,8},{10,11... | collective-permute-start | bytes 393224 | tf_op jit(solution)/shard_map/ppermute | solution.py:31
  12.7 2.4 %collective-permute-start.4 = (bf16[64,1024]{1,0:T(8,128)(2,1)S(1)}, bf16[64,1024]{1,0:T(8,128)(2,1)S(1)}, u32[]{:S(2)}, u32[]{:S(2)}) collective-permute-start(bf16[64,1024]{1,0:T(8,128)(2,1)S(1)} %collective-permute-done.1.refs_1_.rest_4_), channel_id=1, source_target_pairs={{0,1},{1,0},{2,3},{3,2},{4,5},{5,4},{6,7},{7,6},{8,9},{9,8},{10,11... | collective-permute-start | bytes 393224 | tf_op jit(solution)/shard_map/ppermute | solution.py:31
  13.2 1.9 %collective-permute-start.5 = (bf16[64,1024]{1,0:T(8,128)(2,1)S(1)}, bf16[64,1024]{1,0:T(8,128)(2,1)S(1)}, u32[]{:S(2)}, u32[]{:S(2)}) collective-permute-start(bf16[64,1024]{1,0:T(8,128)(2,1)S(1)} %collective-permute-done.2.refs_2_.rest_5_), channel_id=1, source_target_pairs={{0,1},{1,0},{2,3},{3,2},{4,5},{5,4},{6,7},{7,6},{8,9},{9,8},{10,11... | collective-permute-start | bytes 393224 | tf_op jit(solution)/shard_map/ppermute | solution.py:31
  14.6 3.6 %collective-permute-start.12 = (f32[64,64]{1,0:T(8,128)S(1)}, f32[64,64]{1,0:T(8,128)S(1)}, u32[]{:S(2)}, u32[]{:S(2)}) collective-permute-start(f32[64,64]{1,0:T(8,128)S(1)} %collective-permute-done.11), channel_id=1, source_target_pairs={{0,1},{1,0},{2,3},{3,2},{4,5},{5,4},{6,7},{7,6},{8,9},{9,8},{10,11... | collective-permute-start | bytes 49160 | tf_op jit(solution)/shard_map/ppermute | solution.py:31
  16.6 6.8 %collective-permute-start.14 = (bf16[64,1848]{1,0:T(8,128)(2,1)S(1)}, bf16[64,1848]{1,0:T(8,128)(2,1)S(1)}, u32[]{:S(2)}, u32[]{:S(2)}) collective-permute-start(bf16[64,1848]{1,0:T(8,128)(2,1)S(1)} %get-tuple-element.59), channel_id=1, source_target_pairs={{0,8},{1,17},{2,10},{3,19},{4,12},{5,21},{6,14},{7,23},{8,0},{9,25... | collective-permute-start | bytes 709640 | tf_op jit(solution)/shard_map/ppermute | solution.py:41
  18.2 7.1 %collective-permute-start.6 = (f32[72,64]{1,0:T(8,128)S(1)}, f32[72,64]{1,0:T(8,128)S(1)}, u32[]{:S(2)}, u32[]{:S(2)}) collective-permute-start(f32[72,64]{1,0:T(8,128)S(1)} %get-tuple-element.46), channel_id=1, source_target_pairs={{0,24},{8,16},{16,8},{24,0},{1,25},{9,17},{17,9},{25,1},{2,26},{10... | collective-permute-start | bytes 55304 | tf_op jit(solution)/shard_map/ppermute | solution.py:31
  19.8 5.6 %collective-permute-start.7 = (f32[72,64]{1,0:T(8,128)S(1)}, f32[72,64]{1,0:T(8,128)S(1)}, u32[]{:S(2)}, u32[]{:S(2)}) collective-permute-start(f32[72,64]{1,0:T(8,128)S(1)} %get-tuple-element.47), channel_id=1, source_target_pairs={{0,16},{8,24},{16,0},{24,8},{1,17},{9,25},{17,1},{25,9},{2,18},{10... | collective-permute-start | bytes 55304 | tf_op jit(solution)/shard_map/ppermute | solution.py:31
  20.3 5.1 %collective-permute-start.8 = (f32[72,64]{1,0:T(8,128)S(1)}, f32[72,64]{1,0:T(8,128)S(1)}, u32[]{:S(2)}, u32[]{:S(2)}) collective-permute-start(f32[72,64]{1,0:T(8,128)S(1)} %get-tuple-element.48), channel_id=1, source_target_pairs={{0,8},{8,0},{16,24},{24,16},{1,9},{9,1},{17,25},{25,17},{2,10},{10... | collective-permute-start | bytes 55304 | tf_op jit(solution)/shard_map/ppermute | solution.py:31
  21.8 8.8 %collective-permute-start.13 = (bf16[64,1848]{1,0:T(8,128)(2,1)S(1)}, bf16[64,1848]{1,0:T(8,128)(2,1)S(1)}, u32[]{:S(2)}, u32[]{:S(2)}) collective-permute-start(bf16[64,1848]{1,0:T(8,128)(2,1)S(1)} %get-tuple-element.57), channel_id=1, source_target_pairs={{0,8},{1,17},{2,10},{3,19},{4,12},{5,21},{6,14},{7,23},{8,0},{9,25... | collective-permute-start | bytes 709640 | tf_op jit(solution)/shard_map/ppermute | solution.py:41
  23.5 7.8 %collective-permute-start.15 = (bf16[64,1848]{1,0:T(8,128)(2,1)S(1)}, bf16[64,1848]{1,0:T(8,128)(2,1)S(1)}, u32[]{:S(2)}, u32[]{:S(2)}) collective-permute-start(bf16[64,1848]{1,0:T(8,128)(2,1)S(1)} %add.20), channel_id=1, source_target_pairs={{0,16},{1,9},{2,18},{3,11},{4,20},{5,13},{6,22},{7,15},{8,24},{9,1... | collective-permute-start | bytes 709640 | tf_op jit(solution)/shard_map/ppermute | solution.py:41
  26.1 6.9 %collective-permute-start.16 = (bf16[16,2104]{1,0:T(8,128)(2,1)S(1)}, bf16[16,2104]{1,0:T(8,128)(2,1)S(1)}, u32[]{:S(2)}, u32[]{:S(2)}) collective-permute-start(bf16[16,2104]{1,0:T(8,128)(2,1)S(1)} %get-tuple-element.64), channel_id=1, source_target_pairs={{0,24},{8,16},{16,8},{24,0},{1,25},{9,17},{17,9},{25,1},{2,26},{10... | collective-permute-start | bytes 201992 | tf_op jit(solution)/shard_map/ppermute | solution.py:31
  27.6 5.8 %collective-permute-start.17 = (bf16[16,2104]{1,0:T(8,128)(2,1)S(1)}, bf16[16,2104]{1,0:T(8,128)(2,1)S(1)}, u32[]{:S(2)}, u32[]{:S(2)}) collective-permute-start(bf16[16,2104]{1,0:T(8,128)(2,1)S(1)} %get-tuple-element.65), channel_id=1, source_target_pairs={{0,16},{8,24},{16,0},{24,8},{1,17},{9,25},{17,1},{25,9},{2,18},{10... | collective-permute-start | bytes 201992 | tf_op jit(solution)/shard_map/ppermute | solution.py:31
  29.0 4.5 %collective-permute-start.18 = (bf16[16,2104]{1,0:T(8,128)(2,1)S(1)}, bf16[16,2104]{1,0:T(8,128)(2,1)S(1)}, u32[]{:S(2)}, u32[]{:S(2)}) collective-permute-start(bf16[16,2104]{1,0:T(8,128)(2,1)S(1)} %get-tuple-element.66), channel_id=1, source_target_pairs={{0,8},{8,0},{16,24},{24,16},{1,9},{9,1},{17,25},{25,17},{2,10},{10... | collective-permute-start | bytes 201992 | tf_op jit(solution)/shard_map/ppermute | solution.py:31

commit v6 on v5

v6 whole, which is shorter than its diff:
```python
import functools

import jax
import jax.numpy as jnp
from jax import lax
from jax.experimental import pallas as pl
from jax.experimental.pallas import tpu as pltpu
from jax.sharding import PartitionSpec as P

COMP = 16


ADAPTER_SCALING = 0.25
SPREAD_FLOOR = 0.16
F32 = jnp.float32
BF16 = jnp.bfloat16
LANES = 128
BLOCK = 8
PEAK_FLOPS, PEAK_BYTES = 1.15e9, 3.6e6
STEP = 512
NT = (((1,), (1,)), ((), ()))
TN = (((0,), (0,)), ((), ()))
VMEM = pl.BlockSpec(memory_space=pltpu.VMEM)
SMEM = pl.BlockSpec(memory_space=pltpu.SMEM)
HBM = pl.BlockSpec(memory_space=pltpu.HBM)
ANY = pl.BlockSpec(memory_space=pl.ANY)


def swap(array, axis, distance):
    size = lax.axis_size(axis)
    return lax.ppermute(array, axis, [(i, i ^ distance) for i in range(size)])


def swap_cores(array, axis, partner):
    size = lax.axis_size(axis)
    return lax.ppermute(array, axis, [(i, i ^ partner[i % 2]) for i in range(size)])


def swap_pair(array, partner):
    groups, size = lax.axis_size("group"), lax.axis_size("fsdp")
    return lax.ppermute(
        array,
        ("group", "fsdp"),
        [(g * size + f, (g ^ partner[f % 2]) * size + f) for g in range(groups) for f in range(size)],
    )


def sum_over_fsdp(partial, earlier, later):
    size = lax.axis_size("fsdp")
    if size & (size - 1):
        return lax.psum(partial, "fsdp")
    chip = partial + swap(partial, "fsdp", 1)
    if size == 8:
        one = swap_cores(chip, "fsdp", (2, 4))
        chip = after(chip, earlier) + swap(chip, "fsdp", 6)
        return chip + (one + swap(after(one, earlier), "fsdp", 1))
    parts = [chip] + [swap(chip, "fsdp", d) for d in range(2, size, 2)]
    while len(parts) > 1:
        parts = [parts[i] + parts[i + 1] for i in range(0, len(parts), 2)]
    return parts[0]


def after(array, earlier):
    return lax.optimization_barrier((array, earlier))[0]


def call(body, name, cost, outs, ins, scratch=(), out_specs=None):
    return pl.pallas_call(
        body,
        out_shape=outs,
        in_specs=ins,
        out_specs=out_specs or [VMEM] * len(outs),
        scratch_shapes=scratch,
        compiler_params=pltpu.CompilerParams(vmem_limit_bytes=8 << 20),
        cost_estimate=pl.CostEstimate(
            flops=int(cost * PEAK_FLOPS), bytes_accessed=int(cost * PEAK_BYTES), transcendentals=0
        ),
        name=name,
    )


def in_hbm(array):
    return pltpu.with_memory_space_constraint(array, pltpu.HBM)


def positions():
    own, member = lax.axis_index("group"), lax.axis_index("fsdp")
    return own, member, lax.rem(member, 2)


def start_all(pairs, sems, first=0):
    copies = [pltpu.make_async_copy(a, b, sems.at[first + i]) for i, (a, b) in enumerate(pairs)]
    for copy in copies:
        copy.start()
    return copies


def pack_kernel(groups, depth, hidden_ref, old_hbm, reward_hbm, length_hbm, dest_hbm, new_hbm, at_hbm, upstream_hbm, up_hbm, *rest):
    messages, tail_ref, own_hidden = rest[: groups - 1], rest[groups - 1], rest[groups]
    at_ref, upstream_ref, up_ref, back_ref = rest[groups + 1 : groups + 5]
    old_ref, new_ref, reward_ref, length_ref, dest_ref, sems, small_sems = rest[groups + 5 :]
    own, _, core = positions()
    half = depth // 2
    small = [(old_hbm, old_ref), (reward_hbm, reward_ref), (length_hbm, length_ref), (dest_hbm, dest_ref)]
    small += [(new_hbm, new_ref), (upstream_hbm, upstream_ref), (up_hbm, up_ref)]
    small = start_all(small, small_sems)
    pairs = []
    for d in reversed(range(1, groups)):
        start = pl.multiple_of((own ^ d) * depth + core * half, LANES)
        pairs.append((hidden_ref.at[:, pl.ds(start, half)], messages[d - 1]))
    pairs.append((hidden_ref.at[:, pl.ds(pl.multiple_of(own * depth, LANES), depth)], own_hidden))
    copies = start_all(pairs + [(at_hbm, at_ref)], sems)
    for copy in small:
        copy.wait()
    total, squares = jnp.float32(0), jnp.float32(0)
    for k in range(groups):
        total += reward_ref[0, k]
        squares += reward_ref[0, k] * reward_ref[0, k]
    length = old_ref.shape[2]
    lanes = -(-groups * length // LANES) * LANES
    place = lax.broadcasted_iota(jnp.int32, (1, lanes), 1)
    old, new = (jnp.concatenate([ref[0]] * (lanes // length), axis=1) for ref in (old_ref, new_ref))
    line, reward, count = (jnp.zeros((1, lanes), F32) for _ in range(3))
    for k in range(groups):
        start = dest_ref[0, k] * length
        chosen = (place >= start) & (place < start + length)
        line = jnp.where(chosen, old[k : k + 1], line)
        reward = jnp.where(chosen, reward_ref[0, k], reward)
        count = jnp.where(chosen, length_ref[0, k].astype(F32), count)
    lines = [line, reward, count] + [jnp.full((1, lanes), x, F32) for x in (total, squares)]
    lines.append(jnp.zeros((BLOCK - len(lines), lanes), F32))
    chosen = (place >= own * length) & (place < (own + 1) * length)
    lines.append(jnp.where(chosen, new, 0.0))
    if groups % BLOCK:
        lines.append(jnp.zeros((BLOCK - groups % BLOCK, lanes), F32))
    value = jnp.concatenate(lines, axis=0)
    rows = value.shape[0]
    for i in range(lanes // LANES):
        tail_ref[i * rows : (i + 1) * rows] = value[:, i * LANES : (i + 1) * LANES]
    back_ref[...] = lax.dot_general(upstream_ref[...], up_ref[...], NT, preferred_element_type=F32)
    for copy in copies:
        copy.wait()


def whole_rows(half, core, message, other):
    a, b = message[:, :half], other[:, :half]
    first = core == 0
    return jnp.concatenate([jnp.where(first, a, b), jnp.where(first, b, a)], axis=1)


def first_kernel(held_ref, at_ref, own_hidden, *refs):
    *messages, sums_ref, low_ref = refs
    messages = messages[::-1]
    units, depth = held_ref.shape
    half = depth // 2
    mine = pl.ds(pl.multiple_of(positions()[2] * half, LANES), half)
    rows = jnp.concatenate([own_hidden[:, mine]] + [ref[...] for ref in messages], axis=0)
    low_ref[...] = lax.dot_general(rows, at_ref[:, mine], NT, preferred_element_type=F32)
    rows = rows.T
    for start in range(0, units, STEP):
        end = min(start + STEP, units)
        sums_ref[start:end] = jnp.dot(held_ref[start:end, mine], rows, preferred_element_type=F32)


def second_kernel(groups, held_ref, at_ref, own_hidden, sums_ref, low_ref, *refs):
    count = groups - 1
    others, refs = refs[:count][::-1], refs[count:]
    far, early, late, kept, nears, lows = *refs[:4], refs[4 : groups], refs[groups:]
    units, depth = held_ref.shape
    tokens, rank = own_hidden.shape[0], low_ref.shape[1]
    half = depth // 2
    core = positions()[2]
    rest = pl.ds(pl.multiple_of((1 - core) * half, LANES), half)
    rows = jnp.concatenate([own_hidden[:, rest]] + [ref[...] for ref in others], axis=0)
    low = low_ref[...] + lax.dot_general(rows, at_ref[:, rest], NT, preferred_element_type=F32)
    for i, ref in enumerate(lows):
        ref[...] = low[i * tokens : (i + 1) * tokens]
    rows = rows.T
    for start in range(0, units, STEP):
        end = min(start + STEP, units)
        result = sums_ref[start:end] + jnp.dot(held_ref[start:end, rest], rows, preferred_element_type=F32)
        result = result.T
        parts = [result[i * tokens : (i + 1) * tokens] for i in range(groups)]
        kept[:, start:end] = parts[0]
        far[:, start:end] = parts[-1].astype(BF16)
        early[:, start:end] = jnp.where(core == 0, parts[1], parts[-2]).astype(BF16)
        late[:, start:end] = jnp.where(core == 0, parts[-2], parts[1])
        for ref, part in zip(nears, parts[2:-2]):
            ref[:, start:end] = part.astype(BF16)


def add_kernel(late, came, out):
    out[...] = (late[...] + came[...].astype(F32)).astype(BF16)


def letter_kernel(back_ref, tail_ref, *refs):
    count = len(refs) // 2
    tokens, rank = back_ref.shape
    for low, letter in zip(refs[:count], refs[count:]):
        letter[:tokens, :rank] = low[...]
        letter[:tokens, rank:] = back_ref[...]
        letter[tokens:] = tail_ref[...]


def token_coefs(groups, length, tails):
    own = positions()[0]
    chunks = -(-groups * length // LANES)
    rows = tails[0].shape[0] // chunks
    tails = [jnp.concatenate([tail[i * rows : (i + 1) * rows] for i in range(chunks)], axis=1) for tail in tails]
    new = sum(tail[BLOCK : BLOCK + groups] for tail in tails)
    ordered = []
    for j in range(groups):
        table = tails[0][:BLOCK]
        for d in range(1, groups):
            table = jnp.where((own ^ j) == d, tails[d][:BLOCK], table)
        ordered.append(table)
    lanes = new.shape[1]
    place = lax.broadcasted_iota(jnp.int32, (1, lanes), 1)
    together = COMP // groups
    means, squares = [], []
    for j in range(0, groups, together):
        prompt = ordered[j : j + together]
        means += [sum(table[3:4] for table in prompt) / COMP] * together
        squares += [sum(table[4:5] for table in prompt) / COMP] * together
    mean, square = jnp.concatenate(means, axis=0), jnp.concatenate(squares, axis=0)
    old, reward, count = (jnp.concatenate([table[i : i + 1] for table in ordered], axis=0) for i in range(3))
    spread = jnp.sqrt(jnp.maximum(square - mean * mean, SPREAD_FLOOR))
    advantage = (reward - mean) / spread
    ratio = jnp.exp(new - old)
    position = jnp.bitwise_and(place, length - 1).astype(F32)
    live = (position < count) & (place < groups * length)
    coef = jnp.where(live, -(advantage * ratio) / (jnp.maximum(count, 1.0) * COMP), 0.0)
    coef = jnp.concatenate([jnp.broadcast_to(coef[j : j + 1], (length, lanes)) for j in range(groups)], axis=0)
    row = jnp.concatenate([lax.broadcasted_iota(jnp.int32, (length, lanes), 0)] * groups, axis=0)
    offset = lax.broadcasted_iota(jnp.int32, (groups * length, lanes), 1) - row
    return [
        jnp.sum(jnp.where(offset == (own ^ d) * length, coef, 0.0), axis=1, keepdims=True) for d in range(groups)
    ]


def adapter_kernel(groups, length, share, own_low, own_back, own_tail, upstream_ref, *refs):
    count = groups - 1
    letters, messages, (own_term, back_ref, low_ref, loss_ref, term) = refs[:count][::-1], refs[count : 2 * count], refs[2 * count :]
    own = positions()[0]
    tokens, rank = own_back.shape
    coefs = token_coefs(groups, length, [own_tail[...]] + [ref[tokens:] for ref in letters])
    loss_ref[...] = jnp.sum(coefs[0], axis=0, keepdims=True)
    low = own_low[...]
    for ref in letters:
        low = low + ref[:tokens, :rank]
    low = low.astype(BF16)
    low_ref[...] = low
    gradient = (coefs[0] * upstream_ref[...].astype(F32)).astype(BF16)
    term[...] = ADAPTER_SCALING * lax.dot_general(low, gradient, TN, preferred_element_type=F32)
    backs = [own_back[...]] + [ref[:tokens, rank:] for ref in letters]
    for d in range(groups):
        back_ref[d * tokens : (d + 1) * tokens] = (coefs[d] * backs[d]).astype(BF16)
        if share % BLOCK == 0:
            piece = term[pl.ds(pl.multiple_of((own ^ d) * share, share), share), :]
        else:
            piece = term[:share]
            for j in range(1, groups):
                piece = jnp.where((own ^ d) == j, term[j * share : (j + 1) * share], piece)
        if d == 0:
            own_term[...] = piece
            continue
        rows = messages[d - 1].shape[0]
        if share < rows:
            piece = jnp.concatenate([piece, jnp.zeros((rows - share, piece.shape[1]), F32)], axis=0)
        messages[d - 1][...] = piece.astype(BF16)


def output_kernel(total_ref, low_ref, up_ref, *rest):
    total = total_ref[...] + ADAPTER_SCALING * jnp.dot(low_ref[...], up_ref[...], preferred_element_type=F32)
    for ref in rest[:-2]:
        total = total + ref[...].astype(F32)
    rest[-2][...] = total.astype(BF16)
    rest[-1][...] = jnp.zeros_like(rest[-1])


def down_kernel(back_ref, own_hidden, *rest):
    count = len(rest) // 2 - 1
    messages, others = rest[:count][::-1], rest[count : 2 * count][::-1]
    down_hbm, down_ref, sems = rest[2 * count :]
    core = positions()[2]
    half = own_hidden.shape[1] // 2
    copies = []
    for i in range(2):
        span = slice(i * half, (i + 1) * half)
        rows = [own_hidden[:, span]]
        rows += [jnp.where(core == i, a[...], b[...]) for a, b in zip(messages, others)]
        rows = jnp.concatenate(rows, axis=0)
        down_ref[:, span] = ADAPTER_SCALING * lax.dot_general(back_ref[...], rows, TN, preferred_element_type=F32)
        copies += start_all([(down_ref.at[:, span], down_hbm.at[:, span])], sems, i)
    for copy in copies:
        copy.wait()


def gradient_kernel(written, own_term, *rest):
    total = own_term[...]
    for come in rest[:-1]:
        total = total + come[...].astype(F32)[: total.shape[0]]
    rest[-1][...] = total


def on_device(
    hidden_input_slots,
    base_weight,
    adapter_a,
    adapter_up_matrix,
    upstream,
    logp_new,
    logp_old,
    rewards,
    comp_lengths,
    assignment,
):
    groups = lax.axis_size("group")
    tokens = hidden_input_slots.shape[0]
    depth, units = base_weight.shape
    half = depth // 2
    rank = adapter_a.shape[1]
    others = range(1, groups)
    at, weight = adapter_a.T, base_weight.T

    length = logp_new.shape[2]
    chunks = -(-groups * length // LANES)
    tail_rows = chunks * (BLOCK + -(-groups // BLOCK) * BLOCK)
    *messages, tail, own_hidden, at, upstream, up, back = call(
        functools.partial(pack_kernel, groups, depth),
        "pack",
        1.8,
        [pltpu.VMEM((tokens, half), BF16)] * (groups - 1)
        + [
            pltpu.VMEM((tail_rows, LANES), F32),
            pltpu.VMEM((tokens, depth), BF16),
            pltpu.VMEM((rank, depth), BF16),
            pltpu.VMEM((tokens, units), BF16),
            pltpu.VMEM((rank, units), BF16),
            pltpu.VMEM((tokens, rank), F32),
        ],
        [HBM] * 9,
        scratch=[
            pltpu.VMEM(logp_old.shape, F32),
            pltpu.VMEM(logp_new.shape, F32),
            pltpu.SMEM(rewards.shape, F32),
            pltpu.SMEM(comp_lengths.shape, jnp.int32),
            pltpu.SMEM(assignment.shape, jnp.int32),
            pltpu.SemaphoreType.DMA((groups + 1,)),
            pltpu.SemaphoreType.DMA((7,)),
        ],
    )(
        *map(
            in_hbm,
            (
                hidden_input_slots,
                logp_old,
                rewards,
                comp_lengths,
                assignment,
                logp_new,
                at,
                upstream,
                adapter_up_matrix,
            ),
        )
    )
    got = {d: swap(messages[d - 1], "group", d) for d in reversed(others)}
    held = pltpu.with_memory_space_constraint(weight, pltpu.VMEM)
    far, near = groups - 1, list(range(1, groups - 1))
    held_sums, held_lows = call(
        first_kernel,
        "first",
        1.5,
        [pltpu.VMEM((units, groups * tokens), F32), pltpu.VMEM((groups * tokens, rank), F32)],
        [VMEM] * (2 + groups),
    )(held, at, own_hidden, *[got[d] for d in reversed(others)])
    theirs = {d: swap(got[d], "fsdp", 1) for d in reversed(others)}
    far_term, early, late, kept, *terms = call(
        functools.partial(second_kernel, groups),
        "second",
        1.5,
        [
            pltpu.VMEM((tokens, units), BF16),
            pltpu.VMEM((tokens, units), BF16),
            pltpu.VMEM((tokens, units), F32),
            pltpu.VMEM((tokens, units), F32),
        ]
        + [pltpu.VMEM((tokens, units), BF16)] * (groups - 4)
        + [pltpu.VMEM((tokens, rank), F32)] * groups,
        [VMEM] * (4 + groups),
    )(held, at, own_hidden, held_sums, held_lows, *[theirs[d] for d in reversed(others)])
    own_low, *lows = terms[groups - 4 :]
    back = sum_over_fsdp(back, held_lows, own_low)
    came = [swap(term, "group", d) for d, term in enumerate(terms[: groups - 4], 2)]
    ways = (1, far ^ 1)
    far_term = swap_pair(far_term, ways)
    letters = call(
        letter_kernel,
        "letter",
        0.3,
        [pltpu.VMEM((tokens + tail_rows, 2 * rank), F32)] * (groups - 1),
        [VMEM] * (1 + groups),
    )(back, tail, *lows)
    letters = [swap(letters[d - 1], "group", d) for d in reversed(others)]
    came.append(swap_pair(early, ways))
    (late,) = call(add_kernel, "add", 0.5, [pltpu.VMEM((tokens, units), BF16)], [VMEM] * 2)(late, far_term)
    came.append(swap_pair(late, ways[::-1]))

    share = rank // groups
    ride_rows = max(share, 16)
    *pieces, own_term, back_all, low, loss = call(
        functools.partial(adapter_kernel, groups, length, share),
        "adapter",
        1.0,
        [pltpu.VMEM((ride_rows, units), BF16)] * (groups - 1)
        + [
            pltpu.VMEM((share, units), F32),
            pltpu.VMEM((groups * tokens, rank), BF16),
            pltpu.VMEM((tokens, rank), BF16),
            jax.ShapeDtypeStruct((1, 1), F32),
        ],
        [VMEM] * (groups + 3),
        scratch=[pltpu.VMEM((rank, units), F32)],
    )(own_low, back, tail, upstream, *letters)
    arrived = {d: swap(pieces[d - 1], "group", d) for d in reversed(others)}
    (gradient_down,) = call(
        down_kernel,
        "down",
        1.0,
        [jax.ShapeDtypeStruct((rank, depth), F32)],
        [VMEM] * (2 * groups),
        scratch=[pltpu.VMEM((rank, depth), F32), pltpu.SemaphoreType.DMA((2,))],
        out_specs=[HBM],
    )(back_all, own_hidden, *[got[d] for d in reversed(others)], *[theirs[d] for d in reversed(others)])
    projection_output, written = call(
        output_kernel,
        "output",
        1.0,
        [jax.ShapeDtypeStruct((tokens, units), BF16), pltpu.VMEM((8, LANES), F32)],
        [VMEM] * (3 + len(came)),
    )(kept, low, up, *came)
    (gradient_up,) = call(
        gradient_kernel,
        "gradient",
        2.5,
        [jax.ShapeDtypeStruct((share, units), F32)],
        [ANY] + [VMEM] * groups,
    )(written, own_term, *[arrived[d] for d in reversed(others)])
    return (projection_output, gradient_down.T, gradient_up, loss[0])


def solution(mesh):
    return jax.shard_map(
        on_device,
        mesh=mesh,
        in_specs=(
            P("group", None),
            P("group", "fsdp"),
            P("group", None),
            P(None, "fsdp"),
            P("group", "fsdp"),
            P("group", None, None),
            P("group", None, None),
            P("group", None),
            P("group", None),
            P("group", None),
        ),
        out_specs=(P("group", "fsdp"), P("group", None), P("group", "fsdp"), P("group")),
        check_vma=False,
    )
```

time: 34.8 us -> 34.2 us (0.983)
  waiting for transfers between devices: 5.37 us -> 3.97 us
  Pallas kernels: 7.49 us -> 8.14 us
    ppermute x3, waiting for transfers between devices: 2.87 us -> 1.43 us  [swap_pair(): lax.ppermute(array, ('group', 'fsdp'), [(g * size + f, (g ^ partner[f % 2...]
    pallas_call x2 -> x4, Pallas kernels: 1.92 us -> 2.53 us  [the longest x1 1.05 us: on_device(): call(down_kernel, 'down', 1.0, [jax.ShapeDtypeStruct((rank, depth), F32)]...]
  transfers between devices with their start and end apart: 19 -> 19, of which waited for: 7 -> 5; matrix products, arithmetic and copies ran while one was open for 0% -> 0% of each run, Pallas kernels for 13% -> 16%
where the time goes in v6:
time: 34.2 us; the launch traced here: 34.1 us
  starting transfers between devices  21.2 us (62%)
  Pallas kernels  8.14 us (24%)
  waiting for transfers between devices  3.97 us (12%)
  between operations  0.73 us (2%)
    ppermute x15, starting transfers between devices, swap(): return lax.ppermute(array, axis, [(i, i ^ distance) for i in range(size)])  15.2 us
    ppermute x3, starting transfers between devices, swap_pair(): lax.ppermute(array, ('group', 'fsdp'), [(g * size + f, (g ^ partner[f % 2...  4.02 us
    ppermute x15, waiting for transfers between devices, swap(): return lax.ppermute(array, axis, [(i, i ^ distance) for i in range(size)])  2.54 us
    ppermute x1, starting transfers between devices, swap_cores(): lax.ppermute(array, axis, [(i, i ^ partner[i % 2]) for i in range(size)])  1.98 us
    pallas_call x1, Pallas kernels, on_device(): call(functools.partial(pack_kernel, groups, depth), 'pack', 1.8, [pltpu.V...  1.85 us
    pallas_call x1, Pallas kernels, on_device(): call(functools.partial(second_kernel, groups), 'second', 1.5, [pltpu.VMEM...  1.47 us
    ppermute x3, waiting for transfers between devices, swap_pair(): lax.ppermute(array, ('group', 'fsdp'), [(g * size + f, (g ^ partner[f % 2...  1.43 us
    pallas_call x1, Pallas kernels, on_device(): call(first_kernel, 'first', 1.5, [pltpu.VMEM((units, groups * tokens), F3...  1.29 us
  transfers between devices with their start and end apart: 19, of which 5 were waited for; matrix products, arithmetic and copies ran while one was open for 0% of the time, Pallas kernels for 16%

profile of v6, /device:TPU:0, one launch (start us, length us, event | category | flops | bytes accessed | tf_op | source)
XLA Modules:
  0.0 34.1 jit_solution(8762233811014899280)
XLA Ops:
  0.6 1.8 %pack.1 = (bf16[64,1024]{1,0:T(8,128)(2,1)S(1)}, bf16[64,1024]{1,0:T(8,128)(2,1)S(1)}, bf16[64,1024]{1,0:T(8,128)(2,1)S(1)}, f32[16,128]{1,0:T(8,128)S(1)}, bf16...) custom-call(bf16[64,8192]{1,0:T(8,128)(2,1)} %hidden_ref.1, ...), custom_call_target="tpu_custom_call" | custom-call | flops 2070000000 | bytes 6480000 | tf_op jit(solution)/shard_map/pack/pallas_call | solution.py:329
  2.5 4.0 %collective-permute-start = (bf16[64,1024]{1,0:T(8,128)(2,1)S(1)}, bf16[64,1024]{1,0:T(8,128)(2,1)S(1)}, u32[]{:S(2)}, u32[]{:S(2)}) collective-permute-start(bf16[64,1024]{1,0:T(8,128)(2,1)S(1)} %get-tuple-element.39), channel_id=1, source_target_pairs={{0,24},{8,16},{16,8},{24,0},{1,25},{9,17},{17,9},{25,1},{2,26},{10... | collective-permute-start | bytes 393224 | tf_op jit(solution)/shard_map/ppermute | solution.py:31
  6.5 0.5 %collective-permute-start.1 = (bf16[64,1024]{1,0:T(8,128)(2,1)S(1)}, bf16[64,1024]{1,0:T(8,128)(2,1)S(1)}, u32[]{:S(2)}, u32[]{:S(2)}) collective-permute-start(bf16[64,1024]{1,0:T(8,128)(2,1)S(1)} %get-tuple-element.40), channel_id=1, source_target_pairs={{0,16},{8,24},{16,0},{24,8},{1,17},{9,25},{17,1},{25,9},{2,18},{10... | collective-permute-start | bytes 393224 | tf_op jit(solution)/shard_map/ppermute | solution.py:31
  7.1 1.2 %collective-permute-done.6 = f32[64,64]{1,0:T(8,128)S(1)} collective-permute-done((f32[64,64]{1,0:T(8,128)S(1)}, f32[64,64]{1,0:T(8,128)S(1)}, u32[]{:S(2)}, u32[]{:S(2)}) %collective-permute-start.6) | collective-permute-done | bytes 16416 | tf_op jit(solution)/shard_map/ppermute | solution.py:31
  8.3 2.0 %collective-permute-start.8 = (f32[64,64]{1,0:T(8,128)S(1)}, f32[64,64]{1,0:T(8,128)S(1)}, u32[]{:S(2)}, u32[]{:S(2)}) collective-permute-start(f32[64,64]{1,0:T(8,128)S(1)} %add.13), channel_id=1, source_target_pairs={{0,2},{1,5},{2,0},{3,7},{4,6},{5,1},{6,4},{7,3},{8,10},{9,13},{10,... | collective-permute-start | bytes 49160 | tf_op jit(solution)/shard_map/ppermute | solution.py:36
  10.3 2.5 %collective-permute-start.7 = (f32[64,64]{1,0:T(8,128)S(1)}, f32[64,64]{1,0:T(8,128)S(1)}, u32[]{:S(2)}, u32[]{:S(2)}) collective-permute-start(f32[64,64]{1,0:T(8,128)S(1)} %add.13), channel_id=1, source_target_pairs={{0,6},{1,7},{2,4},{3,5},{4,2},{5,3},{6,0},{7,1},{8,14},{9,15},{10,... | collective-permute-start | bytes 49160 | tf_op jit(solution)/shard_map/ppermute | solution.py:31
  13.4 1.3 %first.1 = (f32[1848,256]{1,0:T(8,128)S(1)}, f32[256,64]{1,0:T(8,128)S(1)}) custom-call(bf16[1848,2048]{1,0:T(8,128)(2,1)S(1)} %bitcast.4, bf16[64,2048]{1,0:T(8,128)(2,1)S(1)} %get-tuple-element.37.at_ref, bf16[64,2048]{1,0:T(8,128)(2,1)S(1)} %get-tuple-element.38.own_hidden, bf16[64,1024]{1,0:T(8,128)(2,1)S(1)} %collective-permute-done.refs_0_.rest_0_, ...), custom_call_target="tpu_custom_call" | custom-call | flops 1724999936 | bytes 5400000 | tf_op jit(solution)/shard_map/first/pallas_call | solution.py:371
  14.7 0.5 %collective-permute-start.9 = (f32[64,64]{1,0:T(8,128)S(1)}, f32[64,64]{1,0:T(8,128)S(1)}, u32[]{:S(2)}, u32[]{:S(2)}) collective-permute-start(f32[64,64]{1,0:T(8,128)S(1)} %collective-permute-done.8), channel_id=1, source_target_pairs={{0,1},{1,0},{2,3},{3,2},{4,5},{5,4},{6,7},{7,6},{8,9},{9,8},{10,11... | collective-permute-start | bytes 49160 | tf_op jit(solution)/shard_map/ppermute | solution.py:31
  15.2 1.5 %second.1 = (bf16[64,1848]{1,0:T(8,128)(2,1)S(1)}, bf16[64,1848]{1,0:T(8,128)(2,1)S(1)}, f32[64,1848]{1,0:T(8,128)S(1)}, f32[64,1848]{1,0:T(8,128)S(1)}, f32[64,...) custom-call(bf16[1848,2048]{1,0:T(8,128)(2,1)S(1)} %bitcast.5, ...), custom_call_target="tpu_custom_call" | custom-call | flops 1724999936 | bytes 5400000 | tf_op jit(solution)/shard_map/second/pallas_call | solution.py:379
  16.7 1.6 %collective-permute-start.14 = (bf16[64,1848]{1,0:T(8,128)(2,1)S(1)}, bf16[64,1848]{1,0:T(8,128)(2,1)S(1)}, u32[]{:S(2)}, u32[]{:S(2)}) collective-permute-start(bf16[64,1848]{1,0:T(8,128)(2,1)S(1)} %get-tuple-element.61), channel_id=1, source_target_pairs={{0,8},{1,17},{2,10},{3,19},{4,12},{5,21},{6,14},{7,23},{8,0},{9,25... | collective-permute-start | bytes 709640 | tf_op jit(solution)/shard_map/ppermute | solution.py:41
  18.3 1.6 %collective-permute-start.10 = (f32[80,128]{1,0:T(8,128)S(1)}, f32[80,128]{1,0:T(8,128)S(1)}, u32[]{:S(2)}, u32[]{:S(2)}) collective-permute-start(f32[80,128]{1,0:T(8,128)S(1)} %get-tuple-element.54), channel_id=1, source_target_pairs={{0,24},{8,16},{16,8},{24,0},{1,25},{9,17},{17,9},{25,1},{2,26},{10... | collective-permute-start | bytes 122888 | tf_op jit(solution)/shard_map/ppermute | solution.py:31
  19.9 0.5 %collective-permute-start.11 = (f32[80,128]{1,0:T(8,128)S(1)}, f32[80,128]{1,0:T(8,128)S(1)}, u32[]{:S(2)}, u32[]{:S(2)}) collective-permute-start(f32[80,128]{1,0:T(8,128)S(1)} %get-tuple-element.55), channel_id=1, source_target_pairs={{0,16},{8,24},{16,0},{24,8},{1,17},{9,25},{17,1},{25,9},{2,18},{10... | collective-permute-start | bytes 122888 | tf_op jit(solution)/shard_map/ppermute | solution.py:31
  20.4 1.5 %collective-permute-start.12 = (f32[80,128]{1,0:T(8,128)S(1)}, f32[80,128]{1,0:T(8,128)S(1)}, u32[]{:S(2)}, u32[]{:S(2)}) collective-permute-start(f32[80,128]{1,0:T(8,128)S(1)} %get-tuple-element.56), channel_id=1, source_target_pairs={{0,8},{8,0},{16,24},{24,16},{1,9},{9,1},{17,25},{25,17},{2,10},{10... | collective-permute-start | bytes 122888 | tf_op jit(solution)/shard_map/ppermute | solution.py:31
  21.9 0.5 %collective-permute-start.13 = (bf16[64,1848]{1,0:T(8,128)(2,1)S(1)}, bf16[64,1848]{1,0:T(8,128)(2,1)S(1)}, u32[]{:S(2)}, u32[]{:S(2)}) collective-permute-start(bf16[64,1848]{1,0:T(8,128)(2,1)S(1)} %get-tuple-element.59), channel_id=1, source_target_pairs={{0,8},{1,17},{2,10},{3,19},{4,12},{5,21},{6,14},{7,23},{8,0},{9,25... | collective-permute-start | bytes 709640 | tf_op jit(solution)/shard_map/ppermute | solution.py:41
  22.4 1.0 %collective-permute-done.14.came = bf16[64,1848]{1,0:T(8,128)(2,1)S(1)} collective-permute-done((bf16[64,1848]{1,0:T(8,128)(2,1)S(1)}, bf16[64,1848]{1,0:T(8,128)(2,1)S(1)}, u32[]{:S(2)}, u32[]{:S(2)}) %collective-permute-start.14) | collective-permute-done | bytes 236576 | tf_op jit(solution)/shard_map/ppermute | solution.py:41
  23.5 1.9 %collective-permute-start.15 = (bf16[64,1848]{1,0:T(8,128)(2,1)S(1)}, bf16[64,1848]{1,0:T(8,128)(2,1)S(1)}, u32[]{:S(2)}, u32[]{:S(2)}) collective-permute-start(bf16[64,1848]{1,0:T(8,128)(2,1)S(1)} %add.20), channel_id=1, source_target_pairs={{0,16},{1,9},{2,18},{3,11},{4,20},{5,13},{6,22},{7,15},{8,24},{9,1... | collective-permute-start | bytes 709640 | tf_op jit(solution)/shard_map/ppermute | solution.py:41
  25.5 0.7 %adapter.1 = (bf16[16,1848]{1,0:T(8,128)(2,1)S(1)}, bf16[16,1848]{1,0:T(8,128)(2,1)S(1)}, bf16[16,1848]{1,0:T(8,128)(2,1)S(1)}, f32[16,1848]{1,0:T(8,128)S(1)}, ...) custom-call(f32[64,64]{1,0:T(8,128)S(1)} %get-tuple-element.45.own_low, ...), custom_call_target="tpu_custom_call" | custom-call | flops 1150000000 | bytes 3600000 | tf_op jit(solution)/shard_map/adapter/pallas_call | solution.py:412
  26.2 1.7 %collective-permute-start.16 = (bf16[16,1848]{1,0:T(8,128)(2,1)S(1)}, bf16[16,1848]{1,0:T(8,128)(2,1)S(1)}, u32[]{:S(2)}, u32[]{:S(2)}) collective-permute-start(bf16[16,1848]{1,0:T(8,128)(2,1)S(1)} %get-tuple-element.66), channel_id=1, source_target_pairs={{0,24},{8,16},{16,8},{24,0},{1,25},{9,17},{17,9},{25,1},{2,26},{10... | collective-permute-start | bytes 177416 | tf_op jit(solution)/shard_map/ppermute | solution.py:31
  27.8 1.3 %collective-permute-start.17 = (bf16[16,1848]{1,0:T(8,128)(2,1)S(1)}, bf16[16,1848]{1,0:T(8,128)(2,1)S(1)}, u32[]{:S(2)}, u32[]{:S(2)}) collective-permute-start(bf16[16,1848]{1,0:T(8,128)(2,1)S(1)} %get-tuple-element.67), channel_id=1, source_target_pairs={{0,16},{8,24},{16,0},{24,8},{1,17},{9,25},{17,1},{25,9},{2,18},{10... | collective-permute-start | bytes 177416 | tf_op jit(solution)/shard_map/ppermute | solution.py:31
  29.1 0.5 %collective-permute-start.18 = (bf16[16,1848]{1,0:T(8,128)(2,1)S(1)}, bf16[16,1848]{1,0:T(8,128)(2,1)S(1)}, u32[]{:S(2)}, u32[]{:S(2)}) collective-permute-start(bf16[16,1848]{1,0:T(8,128)(2,1)S(1)} %get-tuple-element.68), channel_id=1, source_target_pairs={{0,8},{8,0},{16,24},{24,16},{1,9},{9,1},{17,25},{25,17},{2,10},{10... | collective-permute-start | bytes 177416 | tf_op jit(solution)/shard_map/ppermute | solution.py:31
  29.7 1.0 %down.1 = f32[64,2048]{1,0:T(8,128)} custom-call(bf16[256,64]{1,0:T(8,128)(2,1)S(1)} %get-tuple-element.63.back_ref, bf16[64,2048]{1,0:T(8,128)(2,1)S(1)} %get-tuple-element.38.own_hidden, bf16[64,1024]{1,0:T(8,128)(2,1)S(1)} %collective-permute-done.refs_0_.rest_0_, bf16[64,1024]{1,0:T(8,128)(2,1)S(1)} %collective-permute-done.1.refs_1_.rest_1_, ...), custom_call_target="tpu_custom_call" | custom-call | flops 1150000000 | bytes 3600000 | tf_op jit(solution)/shard_map/down/pallas_call | solution.py:427
  31.1 0.9 %output.1 = (bf16[64,1848]{1,0:T(8,128)(2,1)}, f32[8,128]{1,0:T(8,128)S(1)}) custom-call(f32[64,1848]{1,0:T(8,128)S(1)} %get-tuple-element.44.total_ref, bf16[64,64]{1,0:T(8,128)(2,1)S(1)} %get-tuple-element.57.low_ref, bf16[64,1848]{1,0:T(8,128)(2,1)S(1)} %get-tuple-element.58.up_ref, bf16[64,1848]{1,0:T(8,128)(2,1)S(1)} %collective-permute-done.13.rest_0_, ...), custom_call_target="tpu_custom_call" | custom-call | flops 1150000000 | bytes 3600000 | tf_op jit(solution)/shard_map/output/pallas_call | solution.py:436
  32.1 1.0 %collective-permute-done.16.rest_0_ = bf16[16,1848]{1,0:T(8,128)(2,1)S(1)} collective-permute-done((bf16[16,1848]{1,0:T(8,128)(2,1)S(1)}, bf16[16,1848]{1,0:T(8,128)(2,1)S(1)}, u32[]{:S(2)}, u32[]{:S(2)}) %collective-permute-start.16) | collective-permute-done | bytes 59168 | tf_op jit(solution)/shard_map/ppermute | solution.py:31
  33.4 0.7 %gradient.1 = f32[16,1848]{1,0:T(8,128)} custom-call(f32[8,128]{1,0:T(8,128)S(1)} %get-tuple-element.64.written, f32[16,1848]{1,0:T(8,128)S(1)} %get-tuple-element.65.own_term, bf16[16,1848]{1,0:T(8,128)(2,1)S(1)} %collective-permute-done.16.rest_0_, bf16[16,1848]{1,0:T(8,128)(2,1)S(1)} %collective-permute-done.17.rest_1_, ...), custom_call_target="tpu_custom_call" | custom-call | flops 2875000064 | bytes 9000000 | tf_op jit(solution)/shard_map/gradient/pallas_call | solution.py:443
  (27 shorter events, 1.6 us)
Async XLA Ops:
  0.6 12.7 %copy-start = (bf16[2048,1848]{0,1:T(8,128)(2,1)S(1)}, bf16[2048,1848]{0,1:T(8,128)(2,1)}, u32[]{:S(2)}) copy-start(bf16[2048,1848]{0,1:T(8,128)(2,1)} %param.11) | copy-start | bytes 22708228
  2.5 10.3 %collective-permute-start = (bf16[64,1024]{1,0:T(8,128)(2,1)S(1)}, bf16[64,1024]{1,0:T(8,128)(2,1)S(1)}, u32[]{:S(2)}, u32[]{:S(2)}) collective-permute-start(bf16[64,1024]{1,0:T(8,128)(2,1)S(1)} %get-tuple-element.39), channel_id=1, source_target_pairs={{0,24},{8,16},{16,8},{24,0},{1,25},{9,17},{17,9},{25,1},{2,26},{10... | collective-permute-start | bytes 393224 | tf_op jit(solution)/shard_map/ppermute | solution.py:31
  6.5 6.3 %collective-permute-start.1 = (bf16[64,1024]{1,0:T(8,128)(2,1)S(1)}, bf16[64,1024]{1,0:T(8,128)(2,1)S(1)}, u32[]{:S(2)}, u32[]{:S(2)}) collective-permute-start(bf16[64,1024]{1,0:T(8,128)(2,1)S(1)} %get-tuple-element.40), channel_id=1, source_target_pairs={{0,16},{8,24},{16,0},{24,8},{1,17},{9,25},{17,1},{25,9},{2,18},{10... | collective-permute-start | bytes 393224 | tf_op jit(solution)/shard_map/ppermute | solution.py:31
  7.0 6.3 %collective-permute-start.2 = (bf16[64,1024]{1,0:T(8,128)(2,1)S(1)}, bf16[64,1024]{1,0:T(8,128)(2,1)S(1)}, u32[]{:S(2)}, u32[]{:S(2)}) collective-permute-start(bf16[64,1024]{1,0:T(8,128)(2,1)S(1)} %get-tuple-element.41), channel_id=1, source_target_pairs={{0,8},{8,0},{16,24},{24,16},{1,9},{9,1},{17,25},{25,17},{2,10},{10... | collective-permute-start | bytes 393224 | tf_op jit(solution)/shard_map/ppermute | solution.py:31
  7.1 1.2 %collective-permute-start.6 = (f32[64,64]{1,0:T(8,128)S(1)}, f32[64,64]{1,0:T(8,128)S(1)}, u32[]{:S(2)}, u32[]{:S(2)}) collective-permute-start(f32[64,64]{1,0:T(8,128)S(1)} %get-tuple-element.46), channel_id=1, source_target_pairs={{0,1},{1,0},{2,3},{3,2},{4,5},{5,4},{6,7},{7,6},{8,9},{9,8},{10,11... | collective-permute-start | bytes 49160 | tf_op jit(solution)/shard_map/ppermute | solution.py:31
  8.3 6.3 %collective-permute-start.8 = (f32[64,64]{1,0:T(8,128)S(1)}, f32[64,64]{1,0:T(8,128)S(1)}, u32[]{:S(2)}, u32[]{:S(2)}) collective-permute-start(f32[64,64]{1,0:T(8,128)S(1)} %add.13), channel_id=1, source_target_pairs={{0,2},{1,5},{2,0},{3,7},{4,6},{5,1},{6,4},{7,3},{8,10},{9,13},{10,... | collective-permute-start | bytes 49160 | tf_op jit(solution)/shard_map/ppermute | solution.py:36
  10.3 7.9 %collective-permute-start.7 = (f32[64,64]{1,0:T(8,128)S(1)}, f32[64,64]{1,0:T(8,128)S(1)}, u32[]{:S(2)}, u32[]{:S(2)}) collective-permute-start(f32[64,64]{1,0:T(8,128)S(1)} %add.13), channel_id=1, source_target_pairs={{0,6},{1,7},{2,4},{3,5},{4,2},{5,3},{6,0},{7,1},{8,14},{9,15},{10,... | collective-permute-start | bytes 49160 | tf_op jit(solution)/shard_map/ppermute | solution.py:31
  12.8 2.4 %collective-permute-start.3 = (bf16[64,1024]{1,0:T(8,128)(2,1)S(1)}, bf16[64,1024]{1,0:T(8,128)(2,1)S(1)}, u32[]{:S(2)}, u32[]{:S(2)}) collective-permute-start(bf16[64,1024]{1,0:T(8,128)(2,1)S(1)} %collective-permute-done.refs_0_.rest_0_), channel_id=1, source_target_pairs={{0,1},{1,0},{2,3},{3,2},{4,5},{5,4},{6,7},{7,6},{8,9},{9,8},{10,11... | collective-permute-start | bytes 393224 | tf_op jit(solution)/shard_map/ppermute | solution.py:31
  12.8 2.4 %collective-permute-start.4 = (bf16[64,1024]{1,0:T(8,128)(2,1)S(1)}, bf16[64,1024]{1,0:T(8,128)(2,1)S(1)}, u32[]{:S(2)}, u32[]{:S(2)}) collective-permute-start(bf16[64,1024]{1,0:T(8,128)(2,1)S(1)} %collective-permute-done.1.refs_1_.rest_1_), channel_id=1, source_target_pairs={{0,1},{1,0},{2,3},{3,2},{4,5},{5,4},{6,7},{7,6},{8,9},{9,8},{10,11... | collective-permute-start | bytes 393224 | tf_op jit(solution)/shard_map/ppermute | solution.py:31
  13.3 1.9 %collective-permute-start.5 = (bf16[64,1024]{1,0:T(8,128)(2,1)S(1)}, bf16[64,1024]{1,0:T(8,128)(2,1)S(1)}, u32[]{:S(2)}, u32[]{:S(2)}) collective-permute-start(bf16[64,1024]{1,0:T(8,128)(2,1)S(1)} %collective-permute-done.2.refs_2_.rest_2_), channel_id=1, source_target_pairs={{0,1},{1,0},{2,3},{3,2},{4,5},{5,4},{6,7},{7,6},{8,9},{9,8},{10,11... | collective-permute-start | bytes 393224 | tf_op jit(solution)/shard_map/ppermute | solution.py:31
  14.7 3.6 %collective-permute-start.9 = (f32[64,64]{1,0:T(8,128)S(1)}, f32[64,64]{1,0:T(8,128)S(1)}, u32[]{:S(2)}, u32[]{:S(2)}) collective-permute-start(f32[64,64]{1,0:T(8,128)S(1)} %collective-permute-done.8), channel_id=1, source_target_pairs={{0,1},{1,0},{2,3},{3,2},{4,5},{5,4},{6,7},{7,6},{8,9},{9,8},{10,11... | collective-permute-start | bytes 49160 | tf_op jit(solution)/shard_map/ppermute | solution.py:31
  16.7 6.8 %collective-permute-start.14 = (bf16[64,1848]{1,0:T(8,128)(2,1)S(1)}, bf16[64,1848]{1,0:T(8,128)(2,1)S(1)}, u32[]{:S(2)}, u32[]{:S(2)}) collective-permute-start(bf16[64,1848]{1,0:T(8,128)(2,1)S(1)} %get-tuple-element.61), channel_id=1, source_target_pairs={{0,8},{1,17},{2,10},{3,19},{4,12},{5,21},{6,14},{7,23},{8,0},{9,25... | collective-permute-start | bytes 709640 | tf_op jit(solution)/shard_map/ppermute | solution.py:41
  18.3 7.1 %collective-permute-start.10 = (f32[80,128]{1,0:T(8,128)S(1)}, f32[80,128]{1,0:T(8,128)S(1)}, u32[]{:S(2)}, u32[]{:S(2)}) collective-permute-start(f32[80,128]{1,0:T(8,128)S(1)} %get-tuple-element.54), channel_id=1, source_target_pairs={{0,24},{8,16},{16,8},{24,0},{1,25},{9,17},{17,9},{25,1},{2,26},{10... | collective-permute-start | bytes 122888 | tf_op jit(solution)/shard_map/ppermute | solution.py:31
  19.9 5.6 %collective-permute-start.11 = (f32[80,128]{1,0:T(8,128)S(1)}, f32[80,128]{1,0:T(8,128)S(1)}, u32[]{:S(2)}, u32[]{:S(2)}) collective-permute-start(f32[80,128]{1,0:T(8,128)S(1)} %get-tuple-element.55), channel_id=1, source_target_pairs={{0,16},{8,24},{16,0},{24,8},{1,17},{9,25},{17,1},{25,9},{2,18},{10... | collective-permute-start | bytes 122888 | tf_op jit(solution)/shard_map/ppermute | solution.py:31
  20.4 5.1 %collective-permute-start.12 = (f32[80,128]{1,0:T(8,128)S(1)}, f32[80,128]{1,0:T(8,128)S(1)}, u32[]{:S(2)}, u32[]{:S(2)}) collective-permute-start(f32[80,128]{1,0:T(8,128)S(1)} %get-tuple-element.56), channel_id=1, source_target_pairs={{0,8},{8,0},{16,24},{24,16},{1,9},{9,1},{17,25},{25,17},{2,10},{10... | collective-permute-start | bytes 122888 | tf_op jit(solution)/shard_map/ppermute | solution.py:31
  21.9 8.8 %collective-permute-start.13 = (bf16[64,1848]{1,0:T(8,128)(2,1)S(1)}, bf16[64,1848]{1,0:T(8,128)(2,1)S(1)}, u32[]{:S(2)}, u32[]{:S(2)}) collective-permute-start(bf16[64,1848]{1,0:T(8,128)(2,1)S(1)} %get-tuple-element.59), channel_id=1, source_target_pairs={{0,8},{1,17},{2,10},{3,19},{4,12},{5,21},{6,14},{7,23},{8,0},{9,25... | collective-permute-start | bytes 709640 | tf_op jit(solution)/shard_map/ppermute | solution.py:41
  23.5 7.6 %collective-permute-start.15 = (bf16[64,1848]{1,0:T(8,128)(2,1)S(1)}, bf16[64,1848]{1,0:T(8,128)(2,1)S(1)}, u32[]{:S(2)}, u32[]{:S(2)}) collective-permute-start(bf16[64,1848]{1,0:T(8,128)(2,1)S(1)} %add.20), channel_id=1, source_target_pairs={{0,16},{1,9},{2,18},{3,11},{4,20},{5,13},{6,22},{7,15},{8,24},{9,1... | collective-permute-start | bytes 709640 | tf_op jit(solution)/shard_map/ppermute | solution.py:41
  26.2 6.9 %collective-permute-start.16 = (bf16[16,1848]{1,0:T(8,128)(2,1)S(1)}, bf16[16,1848]{1,0:T(8,128)(2,1)S(1)}, u32[]{:S(2)}, u32[]{:S(2)}) collective-permute-start(bf16[16,1848]{1,0:T(8,128)(2,1)S(1)} %get-tuple-element.66), channel_id=1, source_target_pairs={{0,24},{8,16},{16,8},{24,0},{1,25},{9,17},{17,9},{25,1},{2,26},{10... | collective-permute-start | bytes 177416 | tf_op jit(solution)/shard_map/ppermute | solution.py:31
  27.8 5.5 %collective-permute-start.17 = (bf16[16,1848]{1,0:T(8,128)(2,1)S(1)}, bf16[16,1848]{1,0:T(8,128)(2,1)S(1)}, u32[]{:S(2)}, u32[]{:S(2)}) collective-permute-start(bf16[16,1848]{1,0:T(8,128)(2,1)S(1)} %get-tuple-element.67), channel_id=1, source_target_pairs={{0,16},{8,24},{16,0},{24,8},{1,17},{9,25},{17,1},{25,9},{2,18},{10... | collective-permute-start | bytes 177416 | tf_op jit(solution)/shard_map/ppermute | solution.py:31
  29.1 4.2 %collective-permute-start.18 = (bf16[16,1848]{1,0:T(8,128)(2,1)S(1)}, bf16[16,1848]{1,0:T(8,128)(2,1)S(1)}, u32[]{:S(2)}, u32[]{:S(2)}) collective-permute-start(bf16[16,1848]{1,0:T(8,128)(2,1)S(1)} %get-tuple-element.68), channel_id=1, source_target_pairs={{0,8},{8,0},{16,24},{24,16},{1,9},{9,1},{17,25},{25,17},{2,10},{10... | collective-permute-start | bytes 177416 | tf_op jit(solution)/shard_map/ppermute | solution.py:31

commit v7 on v6

--- a/solution.py
+++ b/solution.py
@@ -230,31 +230,31 @@
     position = jnp.bitwise_and(place, length - 1).astype(F32)
     live = (position < count) & (place < groups * length)
     coef = jnp.where(live, -(advantage * ratio) / (jnp.maximum(count, 1.0) * COMP), 0.0)
-    coef = jnp.concatenate([jnp.broadcast_to(coef[j : j + 1], (length, lanes)) for j in range(groups)], axis=0)
-    row = jnp.concatenate([lax.broadcasted_iota(jnp.int32, (length, lanes), 0)] * groups, axis=0)
-    offset = lax.broadcasted_iota(jnp.int32, (groups * length, lanes), 1) - row
-    return [
-        jnp.sum(jnp.where(offset == (own ^ d) * length, coef, 0.0), axis=1, keepdims=True) for d in range(groups)
-    ]
-
-
-def adapter_kernel(groups, length, share, own_low, own_back, own_tail, upstream_ref, *refs):
+    return jnp.concatenate([jnp.broadcast_to(coef[j : j + 1], (length, lanes)) for j in range(groups)], axis=0)
+
+
+def coef_column(groups, length, target, coefs):
+    row = jnp.concatenate([lax.broadcasted_iota(jnp.int32, (length, coefs.shape[1]), 0)] * groups, axis=0)
+    offset = lax.broadcasted_iota(jnp.int32, coefs.shape, 1) - row
+    return jnp.sum(jnp.where(offset == target * length, coefs, 0.0), axis=1, keepdims=True)
+
+
+def adapter_kernel(groups, length, share, own_low, own_tail, upstream_ref, *refs):
     count = groups - 1
-    letters, messages, (own_term, back_ref, low_ref, loss_ref, term) = refs[:count][::-1], refs[count : 2 * count], refs[2 * count :]
+    letters, messages, (own_term, coef_ref, low_ref, term) = refs[:count][::-1], refs[count : 2 * count], refs[2 * count :]
     own = positions()[0]
-    tokens, rank = own_back.shape
+    tokens, rank = own_low.shape
     coefs = token_coefs(groups, length, [own_tail[...]] + [ref[tokens:] for ref in letters])
-    loss_ref[...] = jnp.sum(coefs[0], axis=0, keepdims=True)
+    coef_ref[...] = coefs
+    coef = coef_column(groups, length, own, coefs)
     low = own_low[...]
     for ref in letters:
         low = low + ref[:tokens, :rank]
     low = low.astype(BF16)
     low_ref[...] = low
-    gradient = (coefs[0] * upstream_ref[...].astype(F32)).astype(BF16)
+    gradient = (coef * upstream_ref[...].astype(F32)).astype(BF16)
     term[...] = ADAPTER_SCALING * lax.dot_general(low, gradient, TN, preferred_element_type=F32)
-    backs = [own_back[...]] + [ref[:tokens, rank:] for ref in letters]
     for d in range(groups):
-        back_ref[d * tokens : (d + 1) * tokens] = (coefs[d] * backs[d]).astype(BF16)
         if share % BLOCK == 0:
             piece = term[pl.ds(pl.multiple_of((own ^ d) * share, share), share), :]
         else:
@@ -278,10 +278,17 @@
     rest[-1][...] = jnp.zeros_like(rest[-1])
 
 
-def down_kernel(back_ref, own_hidden, *rest):
-    count = len(rest) // 2 - 1
-    messages, others = rest[:count][::-1], rest[count : 2 * count][::-1]
-    down_hbm, down_ref, sems = rest[2 * count :]
+def down_kernel(groups, length, coef_ref, own_back, own_hidden, *rest):
+    count = groups - 1
+    letters, messages, others = (rest[i * count : (i + 1) * count][::-1] for i in range(3))
+    down_hbm, loss_ref, down_ref, sems = rest[3 * count :]
+    own = positions()[0]
+    tokens, rank = own_back.shape
+    coefs = coef_ref[...]
+    backs = [own_back[...]] + [ref[:tokens, rank:] for ref in letters]
+    columns = [coef_column(groups, length, own ^ d, coefs) for d in range(groups)]
+    loss_ref[...] = jnp.sum(columns[0], axis=0, keepdims=True)
+    back = jnp.concatenate([column * part for column, part in zip(columns, backs)], axis=0).astype(BF16)
     core = positions()[2]
     half = own_hidden.shape[1] // 2
     copies = []
@@ -290,7 +297,7 @@
         rows = [own_hidden[:, span]]
         rows += [jnp.where(core == i, a[...], b[...]) for a, b in zip(messages, others)]
         rows = jnp.concatenate(rows, axis=0)
-        down_ref[:, span] = ADAPTER_SCALING * lax.dot_general(back_ref[...], rows, TN, preferred_element_type=F32)
+        down_ref[:, span] = ADAPTER_SCALING * lax.dot_general(back, rows, TN, preferred_element_type=F32)
         copies += start_all([(down_ref.at[:, span], down_hbm.at[:, span])], sems, i)
     for copy in copies:
         copy.wait()
@@ -409,30 +416,29 @@
 
     share = rank // groups
     ride_rows = max(share, 16)
-    *pieces, own_term, back_all, low, loss = call(
+    *pieces, own_term, coefs, low = call(
         functools.partial(adapter_kernel, groups, length, share),
         "adapter",
         1.0,
         [pltpu.VMEM((ride_rows, units), BF16)] * (groups - 1)
         + [
             pltpu.VMEM((share, units), F32),
-            pltpu.VMEM((groups * tokens, rank), BF16),
+            pltpu.VMEM((groups * length, chunks * LANES), F32),
             pltpu.VMEM((tokens, rank), BF16),
-            jax.ShapeDtypeStruct((1, 1), F32),
         ],
-        [VMEM] * (groups + 3),
+        [VMEM] * (groups + 2),
         scratch=[pltpu.VMEM((rank, units), F32)],
-    )(own_low, back, tail, upstream, *letters)
+    )(own_low, tail, upstream, *letters)
     arrived = {d: swap(pieces[d - 1], "group", d) for d in reversed(others)}
-    (gradient_down,) = call(
-        down_kernel,
+    gradient_down, loss = call(
+        functools.partial(down_kernel, groups, length),
         "down",
         1.0,
-        [jax.ShapeDtypeStruct((rank, depth), F32)],
-        [VMEM] * (2 * groups),
+        [jax.ShapeDtypeStruct((rank, depth), F32), jax.ShapeDtypeStruct((1, 1), F32)],
+        [VMEM] * (3 * groups),
         scratch=[pltpu.VMEM((rank, depth), F32), pltpu.SemaphoreType.DMA((2,))],
-        out_specs=[HBM],
-    )(back_all, own_hidden, *[got[d] for d in reversed(others)], *[theirs[d] for d in reversed(others)])
+        out_specs=[HBM, VMEM],
+    )(coefs, back, own_hidden, *letters, *[got[d] for d in reversed(others)], *[theirs[d] for d in reversed(others)])
     projection_output, written = call(
         output_kernel,
         "output",

time: 34.2 us -> 34 us (level)
  waiting for transfers between devices: 3.97 us -> 3.3 us
    pallas_call x1, Pallas kernels: 1.05 us -> 1.72 us  [on_device(): call(functools.partial(down_kernel, groups, length), 'down', 1.0, [jax.Sh...]
    ppermute x3, waiting for transfers between devices: 1.43 us -> 1.04 us  [swap_pair(): lax.ppermute(array, ('group', 'fsdp'), [(g * size + f, (g ^ partner[f % 2...]
  transfers between devices with their start and end apart: 19 -> 19, of which waited for: 5 -> 4; matrix products, arithmetic and copies ran while one was open for 0% -> 0% of each run, Pallas kernels for 16% -> 18%
where the time goes in v7:
time: 34 us; the launch traced here: 33.8 us
  starting transfers between devices  21.3 us (63%)
  Pallas kernels  8.47 us (25%)
  waiting for transfers between devices  3.3 us (10%)
  between operations  0.75 us (2%)
    ppermute x15, starting transfers between devices, swap(): return lax.ppermute(array, axis, [(i, i ^ distance) for i in range(size)])  15.3 us
    ppermute x3, starting transfers between devices, swap_pair(): lax.ppermute(array, ('group', 'fsdp'), [(g * size + f, (g ^ partner[f % 2...  4.02 us
    ppermute x15, waiting for transfers between devices, swap(): return lax.ppermute(array, axis, [(i, i ^ distance) for i in range(size)])  2.26 us
    ppermute x1, starting transfers between devices, swap_cores(): lax.ppermute(array, axis, [(i, i ^ partner[i % 2]) for i in range(size)])  1.98 us
    pallas_call x1, Pallas kernels, on_device(): call(functools.partial(pack_kernel, groups, depth), 'pack', 1.8, [pltpu.V...  1.85 us
    pallas_call x1, Pallas kernels, on_device(): call(functools.partial(down_kernel, groups, length), 'down', 1.0, [jax.Sh...  1.72 us
    pallas_call x1, Pallas kernels, on_device(): call(functools.partial(second_kernel, groups), 'second', 1.5, [pltpu.VMEM...  1.47 us
    pallas_call x1, Pallas kernels, on_device(): call(first_kernel, 'first', 1.5, [pltpu.VMEM((units, groups * tokens), F3...  1.29 us
  transfers between devices with their start and end apart: 19, of which 4 were waited for; matrix products, arithmetic and copies ran while one was open for 0% of the time, Pallas kernels for 18%

profile of v7, /device:TPU:0, one launch (start us, length us, event | category | flops | bytes accessed | tf_op | source)
XLA Modules:
  0.0 33.8 jit_solution(6919641772564763924)
XLA Ops:
  0.6 1.8 %pack.1 = (bf16[64,1024]{1,0:T(8,128)(2,1)S(1)}, bf16[64,1024]{1,0:T(8,128)(2,1)S(1)}, bf16[64,1024]{1,0:T(8,128)(2,1)S(1)}, f32[16,128]{1,0:T(8,128)S(1)}, bf16...) custom-call(bf16[64,8192]{1,0:T(8,128)(2,1)} %hidden_ref.1, ...), custom_call_target="tpu_custom_call" | custom-call | flops 2070000000 | bytes 6480000 | tf_op jit(solution)/shard_map/pack/pallas_call | solution.py:336
  2.5 4.0 %collective-permute-start = (bf16[64,1024]{1,0:T(8,128)(2,1)S(1)}, bf16[64,1024]{1,0:T(8,128)(2,1)S(1)}, u32[]{:S(2)}, u32[]{:S(2)}) collective-permute-start(bf16[64,1024]{1,0:T(8,128)(2,1)S(1)} %get-tuple-element.40), channel_id=1, source_target_pairs={{0,24},{8,16},{16,8},{24,0},{1,25},{9,17},{17,9},{25,1},{2,26},{10... | collective-permute-start | bytes 393224 | tf_op jit(solution)/shard_map/ppermute | solution.py:31
  6.5 0.5 %collective-permute-start.1 = (bf16[64,1024]{1,0:T(8,128)(2,1)S(1)}, bf16[64,1024]{1,0:T(8,128)(2,1)S(1)}, u32[]{:S(2)}, u32[]{:S(2)}) collective-permute-start(bf16[64,1024]{1,0:T(8,128)(2,1)S(1)} %get-tuple-element.41), channel_id=1, source_target_pairs={{0,16},{8,24},{16,0},{24,8},{1,17},{9,25},{17,1},{25,9},{2,18},{10... | collective-permute-start | bytes 393224 | tf_op jit(solution)/shard_map/ppermute | solution.py:31
  7.1 1.2 %collective-permute-done.6 = f32[64,64]{1,0:T(8,128)S(1)} collective-permute-done((f32[64,64]{1,0:T(8,128)S(1)}, f32[64,64]{1,0:T(8,128)S(1)}, u32[]{:S(2)}, u32[]{:S(2)}) %collective-permute-start.6) | collective-permute-done | bytes 16416 | tf_op jit(solution)/shard_map/ppermute | solution.py:31
  8.3 2.0 %collective-permute-start.8 = (f32[64,64]{1,0:T(8,128)S(1)}, f32[64,64]{1,0:T(8,128)S(1)}, u32[]{:S(2)}, u32[]{:S(2)}) collective-permute-start(f32[64,64]{1,0:T(8,128)S(1)} %add.13), channel_id=1, source_target_pairs={{0,2},{1,5},{2,0},{3,7},{4,6},{5,1},{6,4},{7,3},{8,10},{9,13},{10,... | collective-permute-start | bytes 49160 | tf_op jit(solution)/shard_map/ppermute | solution.py:36
  10.3 2.5 %collective-permute-start.7 = (f32[64,64]{1,0:T(8,128)S(1)}, f32[64,64]{1,0:T(8,128)S(1)}, u32[]{:S(2)}, u32[]{:S(2)}) collective-permute-start(f32[64,64]{1,0:T(8,128)S(1)} %add.13), channel_id=1, source_target_pairs={{0,6},{1,7},{2,4},{3,5},{4,2},{5,3},{6,0},{7,1},{8,14},{9,15},{10,... | collective-permute-start | bytes 49160 | tf_op jit(solution)/shard_map/ppermute | solution.py:31
  12.8 0.5 %collective-permute-start.4 = (bf16[64,1024]{1,0:T(8,128)(2,1)S(1)}, bf16[64,1024]{1,0:T(8,128)(2,1)S(1)}, u32[]{:S(2)}, u32[]{:S(2)}) collective-permute-start(bf16[64,1024]{1,0:T(8,128)(2,1)S(1)} %collective-permute-done.1.refs_1_.rest_4_), channel_id=1, source_target_pairs={{0,1},{1,0},{2,3},{3,2},{4,5},{5,4},{6,7},{7,6},{8,9},{9,8},{10,11... | collective-permute-start | bytes 393224 | tf_op jit(solution)/shard_map/ppermute | solution.py:31
  13.4 1.3 %first.1 = (f32[1848,256]{1,0:T(8,128)S(1)}, f32[256,64]{1,0:T(8,128)S(1)}) custom-call(bf16[1848,2048]{1,0:T(8,128)(2,1)S(1)} %bitcast.4, bf16[64,2048]{1,0:T(8,128)(2,1)S(1)} %get-tuple-element.38.at_ref, bf16[64,2048]{1,0:T(8,128)(2,1)S(1)} %get-tuple-element.39.own_hidden, bf16[64,1024]{1,0:T(8,128)(2,1)S(1)} %collective-permute-done.refs_0_.rest_3_, ...), custom_call_target="tpu_custom_call" | custom-call | flops 1724999936 | bytes 5400000 | tf_op jit(solution)/shard_map/first/pallas_call | solution.py:378
  14.7 0.5 %collective-permute-start.9 = (f32[64,64]{1,0:T(8,128)S(1)}, f32[64,64]{1,0:T(8,128)S(1)}, u32[]{:S(2)}, u32[]{:S(2)}) collective-permute-start(f32[64,64]{1,0:T(8,128)S(1)} %collective-permute-done.8), channel_id=1, source_target_pairs={{0,1},{1,0},{2,3},{3,2},{4,5},{5,4},{6,7},{7,6},{8,9},{9,8},{10,11... | collective-permute-start | bytes 49160 | tf_op jit(solution)/shard_map/ppermute | solution.py:31
  15.2 1.5 %second.1 = (bf16[64,1848]{1,0:T(8,128)(2,1)S(1)}, bf16[64,1848]{1,0:T(8,128)(2,1)S(1)}, f32[64,1848]{1,0:T(8,128)S(1)}, f32[64,1848]{1,0:T(8,128)S(1)}, f32[64,...) custom-call(bf16[1848,2048]{1,0:T(8,128)(2,1)S(1)} %bitcast.5, ...), custom_call_target="tpu_custom_call" | custom-call | flops 1724999936 | bytes 5400000 | tf_op jit(solution)/shard_map/second/pallas_call | solution.py:386
  16.7 1.6 %collective-permute-start.14 = (bf16[64,1848]{1,0:T(8,128)(2,1)S(1)}, bf16[64,1848]{1,0:T(8,128)(2,1)S(1)}, u32[]{:S(2)}, u32[]{:S(2)}) collective-permute-start(bf16[64,1848]{1,0:T(8,128)(2,1)S(1)} %get-tuple-element.62), channel_id=1, source_target_pairs={{0,8},{1,17},{2,10},{3,19},{4,12},{5,21},{6,14},{7,23},{8,0},{9,25... | collective-permute-start | bytes 709640 | tf_op jit(solution)/shard_map/ppermute | solution.py:41
  18.3 1.6 %collective-permute-start.10 = (f32[80,128]{1,0:T(8,128)S(1)}, f32[80,128]{1,0:T(8,128)S(1)}, u32[]{:S(2)}, u32[]{:S(2)}) collective-permute-start(f32[80,128]{1,0:T(8,128)S(1)} %get-tuple-element.55), channel_id=1, source_target_pairs={{0,24},{8,16},{16,8},{24,0},{1,25},{9,17},{17,9},{25,1},{2,26},{10... | collective-permute-start | bytes 122888 | tf_op jit(solution)/shard_map/ppermute | solution.py:31
  19.9 0.5 %collective-permute-start.11 = (f32[80,128]{1,0:T(8,128)S(1)}, f32[80,128]{1,0:T(8,128)S(1)}, u32[]{:S(2)}, u32[]{:S(2)}) collective-permute-start(f32[80,128]{1,0:T(8,128)S(1)} %get-tuple-element.56), channel_id=1, source_target_pairs={{0,16},{8,24},{16,0},{24,8},{1,17},{9,25},{17,1},{25,9},{2,18},{10... | collective-permute-start | bytes 122888 | tf_op jit(solution)/shard_map/ppermute | solution.py:31
  20.4 1.5 %collective-permute-start.12 = (f32[80,128]{1,0:T(8,128)S(1)}, f32[80,128]{1,0:T(8,128)S(1)}, u32[]{:S(2)}, u32[]{:S(2)}) collective-permute-start(f32[80,128]{1,0:T(8,128)S(1)} %get-tuple-element.57), channel_id=1, source_target_pairs={{0,8},{8,0},{16,24},{24,16},{1,9},{9,1},{17,25},{25,17},{2,10},{10... | collective-permute-start | bytes 122888 | tf_op jit(solution)/shard_map/ppermute | solution.py:31
  21.9 0.5 %collective-permute-start.13 = (bf16[64,1848]{1,0:T(8,128)(2,1)S(1)}, bf16[64,1848]{1,0:T(8,128)(2,1)S(1)}, u32[]{:S(2)}, u32[]{:S(2)}) collective-permute-start(bf16[64,1848]{1,0:T(8,128)(2,1)S(1)} %get-tuple-element.60), channel_id=1, source_target_pairs={{0,8},{1,17},{2,10},{3,19},{4,12},{5,21},{6,14},{7,23},{8,0},{9,25... | collective-permute-start | bytes 709640 | tf_op jit(solution)/shard_map/ppermute | solution.py:41
  22.4 1.0 %collective-permute-done.14.came = bf16[64,1848]{1,0:T(8,128)(2,1)S(1)} collective-permute-done((bf16[64,1848]{1,0:T(8,128)(2,1)S(1)}, bf16[64,1848]{1,0:T(8,128)(2,1)S(1)}, u32[]{:S(2)}, u32[]{:S(2)}) %collective-permute-start.14) | collective-permute-done | bytes 236576 | tf_op jit(solution)/shard_map/ppermute | solution.py:41
  23.5 1.9 %collective-permute-start.15 = (bf16[64,1848]{1,0:T(8,128)(2,1)S(1)}, bf16[64,1848]{1,0:T(8,128)(2,1)S(1)}, u32[]{:S(2)}, u32[]{:S(2)}) collective-permute-start(bf16[64,1848]{1,0:T(8,128)(2,1)S(1)} %add.20), channel_id=1, source_target_pairs={{0,16},{1,9},{2,18},{3,11},{4,20},{5,13},{6,22},{7,15},{8,24},{9,1... | collective-permute-start | bytes 709640 | tf_op jit(solution)/shard_map/ppermute | solution.py:41
  25.9 1.7 %collective-permute-start.16 = (bf16[16,1848]{1,0:T(8,128)(2,1)S(1)}, bf16[16,1848]{1,0:T(8,128)(2,1)S(1)}, u32[]{:S(2)}, u32[]{:S(2)}) collective-permute-start(bf16[16,1848]{1,0:T(8,128)(2,1)S(1)} %get-tuple-element.68), channel_id=1, source_target_pairs={{0,24},{8,16},{16,8},{24,0},{1,25},{9,17},{17,9},{25,1},{2,26},{10... | collective-permute-start | bytes 177416 | tf_op jit(solution)/shard_map/ppermute | solution.py:31
  27.6 1.3 %collective-permute-start.17 = (bf16[16,1848]{1,0:T(8,128)(2,1)S(1)}, bf16[16,1848]{1,0:T(8,128)(2,1)S(1)}, u32[]{:S(2)}, u32[]{:S(2)}) collective-permute-start(bf16[16,1848]{1,0:T(8,128)(2,1)S(1)} %get-tuple-element.69), channel_id=1, source_target_pairs={{0,16},{8,24},{16,0},{24,8},{1,17},{9,25},{17,1},{25,9},{2,18},{10... | collective-permute-start | bytes 177416 | tf_op jit(solution)/shard_map/ppermute | solution.py:31
  28.9 0.5 %collective-permute-start.18 = (bf16[16,1848]{1,0:T(8,128)(2,1)S(1)}, bf16[16,1848]{1,0:T(8,128)(2,1)S(1)}, u32[]{:S(2)}, u32[]{:S(2)}) collective-permute-start(bf16[16,1848]{1,0:T(8,128)(2,1)S(1)} %get-tuple-element.70), channel_id=1, source_target_pairs={{0,8},{8,0},{16,24},{24,16},{1,9},{9,1},{17,25},{25,17},{2,10},{10... | collective-permute-start | bytes 177416 | tf_op jit(solution)/shard_map/ppermute | solution.py:31
  29.4 1.7 %down.1 = (f32[64,2048]{1,0:T(8,128)}, f32[1,1]{1,0:T(1,128)}) custom-call(f32[64,128]{1,0:T(8,128)S(1)} %get-tuple-element.64.coef_ref, f32[64,64]{1,0:T(8,128)S(1)} %add_add_fusion.back_ref.own_back, bf16[64,2048]{1,0:T(8,128)(2,1)S(1)} %get-tuple-element.39.own_hidden, f32[80,128]{1,0:T(8,128)S(1)} %collective-permute-done.10.refs_0_.rest_0_, ...), custom_call_target="tpu_custom_call" | custom-call | flops 1150000000 | bytes 3600000 | tf_op jit(solution)/shard_map/down/pallas_call | solution.py:433
  31.2 0.9 %output.1 = (bf16[64,1848]{1,0:T(8,128)(2,1)}, f32[8,128]{1,0:T(8,128)S(1)}) custom-call(f32[64,1848]{1,0:T(8,128)S(1)} %get-tuple-element.45.total_ref, bf16[64,64]{1,0:T(8,128)(2,1)S(1)} %get-tuple-element.58.low_ref, bf16[64,1848]{1,0:T(8,128)(2,1)S(1)} %get-tuple-element.59.up_ref, bf16[64,1848]{1,0:T(8,128)(2,1)S(1)} %collective-permute-done.13.rest_0_, ...), custom_call_target="tpu_custom_call" | custom-call | flops 1150000000 | bytes 3600000 | tf_op jit(solution)/shard_map/output/pallas_call | solution.py:442
  32.1 1.0 %collective-permute-done.16.rest_0_ = bf16[16,1848]{1,0:T(8,128)(2,1)S(1)} collective-permute-done((bf16[16,1848]{1,0:T(8,128)(2,1)S(1)}, bf16[16,1848]{1,0:T(8,128)(2,1)S(1)}, u32[]{:S(2)}, u32[]{:S(2)}) %collective-permute-start.16) | collective-permute-done | bytes 59168 | tf_op jit(solution)/shard_map/ppermute | solution.py:31
  33.1 0.7 %gradient.1 = f32[16,1848]{1,0:T(8,128)} custom-call(f32[8,128]{1,0:T(8,128)S(1)} %get-tuple-element.66.written, f32[16,1848]{1,0:T(8,128)S(1)} %get-tuple-element.67.own_term, bf16[16,1848]{1,0:T(8,128)(2,1)S(1)} %collective-permute-done.16.rest_0_, bf16[16,1848]{1,0:T(8,128)(2,1)S(1)} %collective-permute-done.17.rest_1_, ...), custom_call_target="tpu_custom_call" | custom-call | flops 2875000064 | bytes 9000000 | tf_op jit(solution)/shard_map/gradient/pallas_call | solution.py:449
  (27 shorter events, 0.8 us)
Async XLA Ops:
  0.6 12.7 %copy-start = (bf16[2048,1848]{0,1:T(8,128)(2,1)S(1)}, bf16[2048,1848]{0,1:T(8,128)(2,1)}, u32[]{:S(2)}) copy-start(bf16[2048,1848]{0,1:T(8,128)(2,1)} %param.11) | copy-start | bytes 22708228
  2.5 10.3 %collective-permute-start = (bf16[64,1024]{1,0:T(8,128)(2,1)S(1)}, bf16[64,1024]{1,0:T(8,128)(2,1)S(1)}, u32[]{:S(2)}, u32[]{:S(2)}) collective-permute-start(bf16[64,1024]{1,0:T(8,128)(2,1)S(1)} %get-tuple-element.40), channel_id=1, source_target_pairs={{0,24},{8,16},{16,8},{24,0},{1,25},{9,17},{17,9},{25,1},{2,26},{10... | collective-permute-start | bytes 393224 | tf_op jit(solution)/shard_map/ppermute | solution.py:31
  6.5 6.3 %collective-permute-start.1 = (bf16[64,1024]{1,0:T(8,128)(2,1)S(1)}, bf16[64,1024]{1,0:T(8,128)(2,1)S(1)}, u32[]{:S(2)}, u32[]{:S(2)}) collective-permute-start(bf16[64,1024]{1,0:T(8,128)(2,1)S(1)} %get-tuple-element.41), channel_id=1, source_target_pairs={{0,16},{8,24},{16,0},{24,8},{1,17},{9,25},{17,1},{25,9},{2,18},{10... | collective-permute-start | bytes 393224 | tf_op jit(solution)/shard_map/ppermute | solution.py:31
  7.0 6.3 %collective-permute-start.2 = (bf16[64,1024]{1,0:T(8,128)(2,1)S(1)}, bf16[64,1024]{1,0:T(8,128)(2,1)S(1)}, u32[]{:S(2)}, u32[]{:S(2)}) collective-permute-start(bf16[64,1024]{1,0:T(8,128)(2,1)S(1)} %get-tuple-element.42), channel_id=1, source_target_pairs={{0,8},{8,0},{16,24},{24,16},{1,9},{9,1},{17,25},{25,17},{2,10},{10... | collective-permute-start | bytes 393224 | tf_op jit(solution)/shard_map/ppermute | solution.py:31
  7.1 1.2 %collective-permute-start.6 = (f32[64,64]{1,0:T(8,128)S(1)}, f32[64,64]{1,0:T(8,128)S(1)}, u32[]{:S(2)}, u32[]{:S(2)}) collective-permute-start(f32[64,64]{1,0:T(8,128)S(1)} %get-tuple-element.49), channel_id=1, source_target_pairs={{0,1},{1,0},{2,3},{3,2},{4,5},{5,4},{6,7},{7,6},{8,9},{9,8},{10,11... | collective-permute-start | bytes 49160 | tf_op jit(solution)/shard_map/ppermute | solution.py:31
  8.3 6.3 %collective-permute-start.8 = (f32[64,64]{1,0:T(8,128)S(1)}, f32[64,64]{1,0:T(8,128)S(1)}, u32[]{:S(2)}, u32[]{:S(2)}) collective-permute-start(f32[64,64]{1,0:T(8,128)S(1)} %add.13), channel_id=1, source_target_pairs={{0,2},{1,5},{2,0},{3,7},{4,6},{5,1},{6,4},{7,3},{8,10},{9,13},{10,... | collective-permute-start | bytes 49160 | tf_op jit(solution)/shard_map/ppermute | solution.py:36
  10.3 7.9 %collective-permute-start.7 = (f32[64,64]{1,0:T(8,128)S(1)}, f32[64,64]{1,0:T(8,128)S(1)}, u32[]{:S(2)}, u32[]{:S(2)}) collective-permute-start(f32[64,64]{1,0:T(8,128)S(1)} %add.13), channel_id=1, source_target_pairs={{0,6},{1,7},{2,4},{3,5},{4,2},{5,3},{6,0},{7,1},{8,14},{9,15},{10,... | collective-permute-start | bytes 49160 | tf_op jit(solution)/shard_map/ppermute | solution.py:31
  12.8 2.4 %collective-permute-start.3 = (bf16[64,1024]{1,0:T(8,128)(2,1)S(1)}, bf16[64,1024]{1,0:T(8,128)(2,1)S(1)}, u32[]{:S(2)}, u32[]{:S(2)}) collective-permute-start(bf16[64,1024]{1,0:T(8,128)(2,1)S(1)} %collective-permute-done.refs_0_.rest_3_), channel_id=1, source_target_pairs={{0,1},{1,0},{2,3},{3,2},{4,5},{5,4},{6,7},{7,6},{8,9},{9,8},{10,11... | collective-permute-start | bytes 393224 | tf_op jit(solution)/shard_map/ppermute | solution.py:31
  12.8 2.4 %collective-permute-start.4 = (bf16[64,1024]{1,0:T(8,128)(2,1)S(1)}, bf16[64,1024]{1,0:T(8,128)(2,1)S(1)}, u32[]{:S(2)}, u32[]{:S(2)}) collective-permute-start(bf16[64,1024]{1,0:T(8,128)(2,1)S(1)} %collective-permute-done.1.refs_1_.rest_4_), channel_id=1, source_target_pairs={{0,1},{1,0},{2,3},{3,2},{4,5},{5,4},{6,7},{7,6},{8,9},{9,8},{10,11... | collective-permute-start | bytes 393224 | tf_op jit(solution)/shard_map/ppermute | solution.py:31
  13.3 1.9 %collective-permute-start.5 = (bf16[64,1024]{1,0:T(8,128)(2,1)S(1)}, bf16[64,1024]{1,0:T(8,128)(2,1)S(1)}, u32[]{:S(2)}, u32[]{:S(2)}) collective-permute-start(bf16[64,1024]{1,0:T(8,128)(2,1)S(1)} %collective-permute-done.2.refs_2_.rest_5_), channel_id=1, source_target_pairs={{0,1},{1,0},{2,3},{3,2},{4,5},{5,4},{6,7},{7,6},{8,9},{9,8},{10,11... | collective-permute-start | bytes 393224 | tf_op jit(solution)/shard_map/ppermute | solution.py:31
  14.7 3.6 %collective-permute-start.9 = (f32[64,64]{1,0:T(8,128)S(1)}, f32[64,64]{1,0:T(8,128)S(1)}, u32[]{:S(2)}, u32[]{:S(2)}) collective-permute-start(f32[64,64]{1,0:T(8,128)S(1)} %collective-permute-done.8), channel_id=1, source_target_pairs={{0,1},{1,0},{2,3},{3,2},{4,5},{5,4},{6,7},{7,6},{8,9},{9,8},{10,11... | collective-permute-start | bytes 49160 | tf_op jit(solution)/shard_map/ppermute | solution.py:31
  16.7 6.8 %collective-permute-start.14 = (bf16[64,1848]{1,0:T(8,128)(2,1)S(1)}, bf16[64,1848]{1,0:T(8,128)(2,1)S(1)}, u32[]{:S(2)}, u32[]{:S(2)}) collective-permute-start(bf16[64,1848]{1,0:T(8,128)(2,1)S(1)} %get-tuple-element.62), channel_id=1, source_target_pairs={{0,8},{1,17},{2,10},{3,19},{4,12},{5,21},{6,14},{7,23},{8,0},{9,25... | collective-permute-start | bytes 709640 | tf_op jit(solution)/shard_map/ppermute | solution.py:41
  18.3 7.1 %collective-permute-start.10 = (f32[80,128]{1,0:T(8,128)S(1)}, f32[80,128]{1,0:T(8,128)S(1)}, u32[]{:S(2)}, u32[]{:S(2)}) collective-permute-start(f32[80,128]{1,0:T(8,128)S(1)} %get-tuple-element.55), channel_id=1, source_target_pairs={{0,24},{8,16},{16,8},{24,0},{1,25},{9,17},{17,9},{25,1},{2,26},{10... | collective-permute-start | bytes 122888 | tf_op jit(solution)/shard_map/ppermute | solution.py:31
  19.9 5.6 %collective-permute-start.11 = (f32[80,128]{1,0:T(8,128)S(1)}, f32[80,128]{1,0:T(8,128)S(1)}, u32[]{:S(2)}, u32[]{:S(2)}) collective-permute-start(f32[80,128]{1,0:T(8,128)S(1)} %get-tuple-element.56), channel_id=1, source_target_pairs={{0,16},{8,24},{16,0},{24,8},{1,17},{9,25},{17,1},{25,9},{2,18},{10... | collective-permute-start | bytes 122888 | tf_op jit(solution)/shard_map/ppermute | solution.py:31
  20.4 5.1 %collective-permute-start.12 = (f32[80,128]{1,0:T(8,128)S(1)}, f32[80,128]{1,0:T(8,128)S(1)}, u32[]{:S(2)}, u32[]{:S(2)}) collective-permute-start(f32[80,128]{1,0:T(8,128)S(1)} %get-tuple-element.57), channel_id=1, source_target_pairs={{0,8},{8,0},{16,24},{24,16},{1,9},{9,1},{17,25},{25,17},{2,10},{10... | collective-permute-start | bytes 122888 | tf_op jit(solution)/shard_map/ppermute | solution.py:31
  21.9 9.2 %collective-permute-start.13 = (bf16[64,1848]{1,0:T(8,128)(2,1)S(1)}, bf16[64,1848]{1,0:T(8,128)(2,1)S(1)}, u32[]{:S(2)}, u32[]{:S(2)}) collective-permute-start(bf16[64,1848]{1,0:T(8,128)(2,1)S(1)} %get-tuple-element.60), channel_id=1, source_target_pairs={{0,8},{1,17},{2,10},{3,19},{4,12},{5,21},{6,14},{7,23},{8,0},{9,25... | collective-permute-start | bytes 709640 | tf_op jit(solution)/shard_map/ppermute | solution.py:41
  23.5 7.6 %collective-permute-start.15 = (bf16[64,1848]{1,0:T(8,128)(2,1)S(1)}, bf16[64,1848]{1,0:T(8,128)(2,1)S(1)}, u32[]{:S(2)}, u32[]{:S(2)}) collective-permute-start(bf16[64,1848]{1,0:T(8,128)(2,1)S(1)} %add.20), channel_id=1, source_target_pairs={{0,16},{1,9},{2,18},{3,11},{4,20},{5,13},{6,22},{7,15},{8,24},{9,1... | collective-permute-start | bytes 709640 | tf_op jit(solution)/shard_map/ppermute | solution.py:41
  25.9 7.2 %collective-permute-start.16 = (bf16[16,1848]{1,0:T(8,128)(2,1)S(1)}, bf16[16,1848]{1,0:T(8,128)(2,1)S(1)}, u32[]{:S(2)}, u32[]{:S(2)}) collective-permute-start(bf16[16,1848]{1,0:T(8,128)(2,1)S(1)} %get-tuple-element.68), channel_id=1, source_target_pairs={{0,24},{8,16},{16,8},{24,0},{1,25},{9,17},{17,9},{25,1},{2,26},{10... | collective-permute-start | bytes 177416 | tf_op jit(solution)/shard_map/ppermute | solution.py:31
  27.6 5.5 %collective-permute-start.17 = (bf16[16,1848]{1,0:T(8,128)(2,1)S(1)}, bf16[16,1848]{1,0:T(8,128)(2,1)S(1)}, u32[]{:S(2)}, u32[]{:S(2)}) collective-permute-start(bf16[16,1848]{1,0:T(8,128)(2,1)S(1)} %get-tuple-element.69), channel_id=1, source_target_pairs={{0,16},{8,24},{16,0},{24,8},{1,17},{9,25},{17,1},{25,9},{2,18},{10... | collective-permute-start | bytes 177416 | tf_op jit(solution)/shard_map/ppermute | solution.py:31
  28.9 4.3 %collective-permute-start.18 = (bf16[16,1848]{1,0:T(8,128)(2,1)S(1)}, bf16[16,1848]{1,0:T(8,128)(2,1)S(1)}, u32[]{:S(2)}, u32[]{:S(2)}) collective-permute-start(bf16[16,1848]{1,0:T(8,128)(2,1)S(1)} %get-tuple-element.70), channel_id=1, source_target_pairs={{0,8},{8,0},{16,24},{24,16},{1,9},{9,1},{17,25},{25,17},{2,10},{10... | collective-permute-start | bytes 177416 | tf_op jit(solution)/shard_map/ppermute | solution.py:31

commit v8 on v7

--- a/solution.py
+++ b/solution.py
@@ -45,11 +45,11 @@
     )
 
 
-def sum_over_fsdp(partial, earlier, later):
+def sum_over_fsdp(partial, loaded, earlier, later):
     size = lax.axis_size("fsdp")
     if size & (size - 1):
         return lax.psum(partial, "fsdp")
-    chip = partial + swap(partial, "fsdp", 1)
+    chip = after(partial + swap(partial, "fsdp", 1), loaded)
     if size == 8:
         one = swap_cores(chip, "fsdp", (2, 4))
         chip = after(chip, earlier) + swap(chip, "fsdp", 6)
@@ -95,21 +95,20 @@
     return copies
 
 
-def pack_kernel(groups, depth, hidden_ref, old_hbm, reward_hbm, length_hbm, dest_hbm, new_hbm, at_hbm, upstream_hbm, up_hbm, *rest):
-    messages, tail_ref, own_hidden = rest[: groups - 1], rest[groups - 1], rest[groups]
-    at_ref, upstream_ref, up_ref, back_ref = rest[groups + 1 : groups + 5]
-    old_ref, new_ref, reward_ref, length_ref, dest_ref, sems, small_sems = rest[groups + 5 :]
+def pack_kernel(groups, depth, hidden_ref, old_hbm, reward_hbm, length_hbm, dest_hbm, new_hbm, upstream_hbm, up_hbm, *rest):
+    messages, tail_ref = rest[: groups - 1], rest[groups - 1]
+    upstream_ref, up_ref, back_ref = rest[groups : groups + 3]
+    old_ref, new_ref, reward_ref, length_ref, dest_ref, sems, small_sems = rest[groups + 3 :]
     own, _, core = positions()
     half = depth // 2
     small = [(old_hbm, old_ref), (reward_hbm, reward_ref), (length_hbm, length_ref), (dest_hbm, dest_ref)]
-    small += [(new_hbm, new_ref), (upstream_hbm, upstream_ref), (up_hbm, up_ref)]
-    small = start_all(small, small_sems)
+    small = start_all(small + [(new_hbm, new_ref)], small_sems)
+    factors = start_all([(upstream_hbm, upstream_ref), (up_hbm, up_ref)], small_sems, 5)
     pairs = []
     for d in reversed(range(1, groups)):
         start = pl.multiple_of((own ^ d) * depth + core * half, LANES)
         pairs.append((hidden_ref.at[:, pl.ds(start, half)], messages[d - 1]))
-    pairs.append((hidden_ref.at[:, pl.ds(pl.multiple_of(own * depth, LANES), depth)], own_hidden))
-    copies = start_all(pairs + [(at_hbm, at_ref)], sems)
+    copies = start_all(pairs, sems)
     for copy in small:
         copy.wait()
     total, squares = jnp.float32(0), jnp.float32(0)
@@ -137,8 +136,17 @@
     rows = value.shape[0]
     for i in range(lanes // LANES):
         tail_ref[i * rows : (i + 1) * rows] = value[:, i * LANES : (i + 1) * LANES]
+    for copy in factors:
+        copy.wait()
     back_ref[...] = lax.dot_general(upstream_ref[...], up_ref[...], NT, preferred_element_type=F32)
     for copy in copies:
+        copy.wait()
+
+
+def load_kernel(hidden_ref, at_hbm, own_hidden, at_ref, sems):
+    depth = own_hidden.shape[1]
+    mine = hidden_ref.at[:, pl.ds(pl.multiple_of(positions()[0] * depth, LANES), depth)]
+    for copy in start_all([(mine, own_hidden), (at_hbm, at_ref)], sems):
         copy.wait()
 
 
@@ -333,27 +341,25 @@
     length = logp_new.shape[2]
     chunks = -(-groups * length // LANES)
     tail_rows = chunks * (BLOCK + -(-groups // BLOCK) * BLOCK)
-    *messages, tail, own_hidden, at, upstream, up, back = call(
+    *messages, tail, upstream, up, back = call(
         functools.partial(pack_kernel, groups, depth),
         "pack",
         1.8,
         [pltpu.VMEM((tokens, half), BF16)] * (groups - 1)
         + [
             pltpu.VMEM((tail_rows, LANES), F32),
-            pltpu.VMEM((tokens, depth), BF16),
-            pltpu.VMEM((rank, depth), BF16),
             pltpu.VMEM((tokens, units), BF16),
             pltpu.VMEM((rank, units), BF16),
             pltpu.VMEM((tokens, rank), F32),
         ],
-        [HBM] * 9,
+        [HBM] * 8,
         scratch=[
             pltpu.VMEM(logp_old.shape, F32),
             pltpu.VMEM(logp_new.shape, F32),
             pltpu.SMEM(rewards.shape, F32),
             pltpu.SMEM(comp_lengths.shape, jnp.int32),
             pltpu.SMEM(assignment.shape, jnp.int32),
-            pltpu.SemaphoreType.DMA((groups + 1,)),
+            pltpu.SemaphoreType.DMA((groups - 1,)),
             pltpu.SemaphoreType.DMA((7,)),
         ],
     )(
@@ -366,13 +372,20 @@
                 comp_lengths,
                 assignment,
                 logp_new,
-                at,
                 upstream,
                 adapter_up_matrix,
             ),
         )
     )
     got = {d: swap(messages[d - 1], "group", d) for d in reversed(others)}
+    own_hidden, at = call(
+        load_kernel,
+        "load",
+        1.0,
+        [pltpu.VMEM((tokens, depth), BF16), pltpu.VMEM((rank, depth), BF16)],
+        [HBM] * 2,
+        scratch=[pltpu.SemaphoreType.DMA((2,))],
+    )(in_hbm(hidden_input_slots), in_hbm(at))
     held = pltpu.with_memory_space_constraint(weight, pltpu.VMEM)
     far, near = groups - 1, list(range(1, groups - 1))
     held_sums, held_lows = call(
@@ -398,7 +411,7 @@
         [VMEM] * (4 + groups),
     )(held, at, own_hidden, held_sums, held_lows, *[theirs[d] for d in reversed(others)])
     own_low, *lows = terms[groups - 4 :]
-    back = sum_over_fsdp(back, held_lows, own_low)
+    back = sum_over_fsdp(back, at, held_lows, own_low)
     came = [swap(term, "group", d) for d, term in enumerate(terms[: groups - 4], 2)]
     ways = (1, far ^ 1)
     far_term = swap_pair(far_term, ways)

time: 34 us -> 33.8 us (level)
  waiting for transfers between devices: 3.3 us -> 2.26 us
  Pallas kernels: 8.47 us -> 9.36 us
    ppermute x15, waiting for transfers between devices: 2.26 us -> 1.21 us  [swap(): return lax.ppermute(array, axis, [(i, i ^ distance) for i in range(size)])]
    pallas_call x0 -> x1, Pallas kernels: none -> 1.05 us  [on_device(): call(load_kernel, 'load', 1.0, [pltpu.VMEM((tokens, depth), BF16), pltpu....]
  transfers between devices with their start and end apart: 19 -> 19, of which waited for: 4 -> 4; matrix products, arithmetic and copies ran while one was open for 0% -> 0% of each run, Pallas kernels for 18% -> 21%
where the time goes in v8:
time: 33.8 us; the launch traced here: 33.6 us
  starting transfers between devices  21.3 us (63%)
  Pallas kernels  9.36 us (28%)
  waiting for transfers between devices  2.26 us (7%)
  between operations  0.75 us (2%)
    ppermute x15, starting transfers between devices, swap(): return lax.ppermute(array, axis, [(i, i ^ distance) for i in range(size)])  15.3 us
    ppermute x3, starting transfers between devices, swap_pair(): lax.ppermute(array, ('group', 'fsdp'), [(g * size + f, (g ^ partner[f % 2...  4.02 us
    ppermute x1, starting transfers between devices, swap_cores(): lax.ppermute(array, axis, [(i, i ^ partner[i % 2]) for i in range(size)])  1.97 us
    pallas_call x1, Pallas kernels, on_device(): call(functools.partial(down_kernel, groups, length), 'down', 1.0, [jax.Sh...  1.72 us
    pallas_call x1, Pallas kernels, on_device(): call(functools.partial(pack_kernel, groups, depth), 'pack', 1.8, [pltpu.V...  1.68 us
    pallas_call x1, Pallas kernels, on_device(): call(functools.partial(second_kernel, groups), 'second', 1.5, [pltpu.VMEM...  1.48 us
    pallas_call x1, Pallas kernels, on_device(): call(first_kernel, 'first', 1.5, [pltpu.VMEM((units, groups * tokens), F3...  1.29 us
    ppermute x15, waiting for transfers between devices, swap(): return lax.ppermute(array, axis, [(i, i ^ distance) for i in range(size)])  1.21 us
  transfers between devices with their start and end apart: 19, of which 4 were waited for; matrix products, arithmetic and copies ran while one was open for 0% of the time, Pallas kernels for 21%

profile of v8, /device:TPU:0, one launch (start us, length us, event | category | flops | bytes accessed | tf_op | source)
XLA Modules:
  0.0 33.6 jit_solution(1737350434546263596)
XLA Ops:
  0.6 1.7 %pack.1 = (bf16[64,1024]{1,0:T(8,128)(2,1)S(1)}, bf16[64,1024]{1,0:T(8,128)(2,1)S(1)}, bf16[64,1024]{1,0:T(8,128)(2,1)S(1)}, f32[16,128]{1,0:T(8,128)S(1)}, bf16...) custom-call(bf16[64,8192]{1,0:T(8,128)(2,1)} %hidden_ref.3, f32[1,4,16]{2,1,0:T(4,128)} %old_hbm.1, ...), custom_call_target="tpu_custom_call" | custom-call | flops 2070000000 | bytes 6480000 | tf_op jit(solution)/shard_map/pack/pallas_call | solution.py:344
  2.3 4.0 %collective-permute-start = (bf16[64,1024]{1,0:T(8,128)(2,1)S(1)}, bf16[64,1024]{1,0:T(8,128)(2,1)S(1)}, u32[]{:S(2)}, u32[]{:S(2)}) collective-permute-start(bf16[64,1024]{1,0:T(8,128)(2,1)S(1)} %get-tuple-element.41), channel_id=1, source_target_pairs={{0,24},{8,16},{16,8},{24,0},{1,25},{9,17},{17,9},{25,1},{2,26},{10... | collective-permute-start | bytes 393224 | tf_op jit(solution)/shard_map/ppermute | solution.py:31
  6.3 0.5 %collective-permute-start.1 = (bf16[64,1024]{1,0:T(8,128)(2,1)S(1)}, bf16[64,1024]{1,0:T(8,128)(2,1)S(1)}, u32[]{:S(2)}, u32[]{:S(2)}) collective-permute-start(bf16[64,1024]{1,0:T(8,128)(2,1)S(1)} %get-tuple-element.42), channel_id=1, source_target_pairs={{0,16},{8,24},{16,0},{24,8},{1,17},{9,25},{17,1},{25,9},{2,18},{10... | collective-permute-start | bytes 393224 | tf_op jit(solution)/shard_map/ppermute | solution.py:31
  6.9 1.0 %load.1 = (bf16[64,2048]{1,0:T(8,128)(2,1)S(1)}, bf16[64,2048]{1,0:T(8,128)(2,1)S(1)}) custom-call(bf16[64,8192]{1,0:T(8,128)(2,1)} %hidden_ref.3, bf16[64,2048]{1,0:T(8,128)(2,1)} %bitcast.6), custom_call_target="tpu_custom_call" | custom-call | flops 1150000000 | bytes 3600000 | tf_op jit(solution)/shard_map/load/pallas_call | solution.py:381
  8.2 2.0 %collective-permute-start.8 = (f32[64,64]{1,0:T(8,128)S(1)}, f32[64,64]{1,0:T(8,128)S(1)}, u32[]{:S(2)}, u32[]{:S(2)}) collective-permute-start(f32[64,64]{1,0:T(8,128)S(1)} %add.13), channel_id=1, source_target_pairs={{0,2},{1,5},{2,0},{3,7},{4,6},{5,1},{6,4},{7,3},{8,10},{9,13},{10,... | collective-permute-start | bytes 49160 | tf_op jit(solution)/shard_map/ppermute | solution.py:36
  10.1 2.5 %collective-permute-start.7 = (f32[64,64]{1,0:T(8,128)S(1)}, f32[64,64]{1,0:T(8,128)S(1)}, u32[]{:S(2)}, u32[]{:S(2)}) collective-permute-start(f32[64,64]{1,0:T(8,128)S(1)} %add.13), channel_id=1, source_target_pairs={{0,6},{1,7},{2,4},{3,5},{4,2},{5,3},{6,0},{7,1},{8,14},{9,15},{10,... | collective-permute-start | bytes 49160 | tf_op jit(solution)/shard_map/ppermute | solution.py:31
  12.6 0.5 %collective-permute-start.4 = (bf16[64,1024]{1,0:T(8,128)(2,1)S(1)}, bf16[64,1024]{1,0:T(8,128)(2,1)S(1)}, u32[]{:S(2)}, u32[]{:S(2)}) collective-permute-start(bf16[64,1024]{1,0:T(8,128)(2,1)S(1)} %collective-permute-done.1.refs_1_.rest_4_), channel_id=1, source_target_pairs={{0,1},{1,0},{2,3},{3,2},{4,5},{5,4},{6,7},{7,6},{8,9},{9,8},{10,11... | collective-permute-start | bytes 393224 | tf_op jit(solution)/shard_map/ppermute | solution.py:31
  13.2 1.3 %first.1 = (f32[1848,256]{1,0:T(8,128)S(1)}, f32[256,64]{1,0:T(8,128)S(1)}) custom-call(bf16[1848,2048]{1,0:T(8,128)(2,1)S(1)} %bitcast.4, bf16[64,2048]{1,0:T(8,128)(2,1)S(1)} %get-tuple-element.39.at_ref, bf16[64,2048]{1,0:T(8,128)(2,1)S(1)} %get-tuple-element.40.own_hidden, bf16[64,1024]{1,0:T(8,128)(2,1)S(1)} %collective-permute-done.refs_0_.rest_3_, ...), custom_call_target="tpu_custom_call" | custom-call | flops 1724999936 | bytes 5400000 | tf_op jit(solution)/shard_map/first/pallas_call | solution.py:391
  14.5 0.5 %collective-permute-start.9 = (f32[64,64]{1,0:T(8,128)S(1)}, f32[64,64]{1,0:T(8,128)S(1)}, u32[]{:S(2)}, u32[]{:S(2)}) collective-permute-start(f32[64,64]{1,0:T(8,128)S(1)} %collective-permute-done.8), channel_id=1, source_target_pairs={{0,1},{1,0},{2,3},{3,2},{4,5},{5,4},{6,7},{7,6},{8,9},{9,8},{10,11... | collective-permute-start | bytes 49160 | tf_op jit(solution)/shard_map/ppermute | solution.py:31
  15.0 1.5 %second.1 = (bf16[64,1848]{1,0:T(8,128)(2,1)S(1)}, bf16[64,1848]{1,0:T(8,128)(2,1)S(1)}, f32[64,1848]{1,0:T(8,128)S(1)}, f32[64,1848]{1,0:T(8,128)S(1)}, f32[64,...) custom-call(bf16[1848,2048]{1,0:T(8,128)(2,1)S(1)} %bitcast.5, ...), custom_call_target="tpu_custom_call" | custom-call | flops 1724999936 | bytes 5400000 | tf_op jit(solution)/shard_map/second/pallas_call | solution.py:399
  16.5 1.6 %collective-permute-start.14 = (bf16[64,1848]{1,0:T(8,128)(2,1)S(1)}, bf16[64,1848]{1,0:T(8,128)(2,1)S(1)}, u32[]{:S(2)}, u32[]{:S(2)}) collective-permute-start(bf16[64,1848]{1,0:T(8,128)(2,1)S(1)} %get-tuple-element.64), channel_id=1, source_target_pairs={{0,8},{1,17},{2,10},{3,19},{4,12},{5,21},{6,14},{7,23},{8,0},{9,25... | collective-permute-start | bytes 709640 | tf_op jit(solution)/shard_map/ppermute | solution.py:41
  18.2 1.6 %collective-permute-start.10 = (f32[80,128]{1,0:T(8,128)S(1)}, f32[80,128]{1,0:T(8,128)S(1)}, u32[]{:S(2)}, u32[]{:S(2)}) collective-permute-start(f32[80,128]{1,0:T(8,128)S(1)} %get-tuple-element.57), channel_id=1, source_target_pairs={{0,24},{8,16},{16,8},{24,0},{1,25},{9,17},{17,9},{25,1},{2,26},{10... | collective-permute-start | bytes 122888 | tf_op jit(solution)/shard_map/ppermute | solution.py:31
  19.7 0.5 %collective-permute-start.11 = (f32[80,128]{1,0:T(8,128)S(1)}, f32[80,128]{1,0:T(8,128)S(1)}, u32[]{:S(2)}, u32[]{:S(2)}) collective-permute-start(f32[80,128]{1,0:T(8,128)S(1)} %get-tuple-element.58), channel_id=1, source_target_pairs={{0,16},{8,24},{16,0},{24,8},{1,17},{9,25},{17,1},{25,9},{2,18},{10... | collective-permute-start | bytes 122888 | tf_op jit(solution)/shard_map/ppermute | solution.py:31
  20.2 1.5 %collective-permute-start.12 = (f32[80,128]{1,0:T(8,128)S(1)}, f32[80,128]{1,0:T(8,128)S(1)}, u32[]{:S(2)}, u32[]{:S(2)}) collective-permute-start(f32[80,128]{1,0:T(8,128)S(1)} %get-tuple-element.59), channel_id=1, source_target_pairs={{0,8},{8,0},{16,24},{24,16},{1,9},{9,1},{17,25},{25,17},{2,10},{10... | collective-permute-start | bytes 122888 | tf_op jit(solution)/shard_map/ppermute | solution.py:31
  21.7 0.5 %collective-permute-start.13 = (bf16[64,1848]{1,0:T(8,128)(2,1)S(1)}, bf16[64,1848]{1,0:T(8,128)(2,1)S(1)}, u32[]{:S(2)}, u32[]{:S(2)}) collective-permute-start(bf16[64,1848]{1,0:T(8,128)(2,1)S(1)} %get-tuple-element.62), channel_id=1, source_target_pairs={{0,8},{1,17},{2,10},{3,19},{4,12},{5,21},{6,14},{7,23},{8,0},{9,25... | collective-permute-start | bytes 709640 | tf_op jit(solution)/shard_map/ppermute | solution.py:41
  22.3 1.0 %collective-permute-done.14.came = bf16[64,1848]{1,0:T(8,128)(2,1)S(1)} collective-permute-done((bf16[64,1848]{1,0:T(8,128)(2,1)S(1)}, bf16[64,1848]{1,0:T(8,128)(2,1)S(1)}, u32[]{:S(2)}, u32[]{:S(2)}) %collective-permute-start.14) | collective-permute-done | bytes 236576 | tf_op jit(solution)/shard_map/ppermute | solution.py:41
  23.4 1.9 %collective-permute-start.15 = (bf16[64,1848]{1,0:T(8,128)(2,1)S(1)}, bf16[64,1848]{1,0:T(8,128)(2,1)S(1)}, u32[]{:S(2)}, u32[]{:S(2)}) collective-permute-start(bf16[64,1848]{1,0:T(8,128)(2,1)S(1)} %add.20), channel_id=1, source_target_pairs={{0,16},{1,9},{2,18},{3,11},{4,20},{5,13},{6,22},{7,15},{8,24},{9,1... | collective-permute-start | bytes 709640 | tf_op jit(solution)/shard_map/ppermute | solution.py:41
  25.7 1.7 %collective-permute-start.16 = (bf16[16,1848]{1,0:T(8,128)(2,1)S(1)}, bf16[16,1848]{1,0:T(8,128)(2,1)S(1)}, u32[]{:S(2)}, u32[]{:S(2)}) collective-permute-start(bf16[16,1848]{1,0:T(8,128)(2,1)S(1)} %get-tuple-element.70), channel_id=1, source_target_pairs={{0,24},{8,16},{16,8},{24,0},{1,25},{9,17},{17,9},{25,1},{2,26},{10... | collective-permute-start | bytes 177416 | tf_op jit(solution)/shard_map/ppermute | solution.py:31
  27.4 1.3 %collective-permute-start.17 = (bf16[16,1848]{1,0:T(8,128)(2,1)S(1)}, bf16[16,1848]{1,0:T(8,128)(2,1)S(1)}, u32[]{:S(2)}, u32[]{:S(2)}) collective-permute-start(bf16[16,1848]{1,0:T(8,128)(2,1)S(1)} %get-tuple-element.71), channel_id=1, source_target_pairs={{0,16},{8,24},{16,0},{24,8},{1,17},{9,25},{17,1},{25,9},{2,18},{10... | collective-permute-start | bytes 177416 | tf_op jit(solution)/shard_map/ppermute | solution.py:31
  28.7 0.5 %collective-permute-start.18 = (bf16[16,1848]{1,0:T(8,128)(2,1)S(1)}, bf16[16,1848]{1,0:T(8,128)(2,1)S(1)}, u32[]{:S(2)}, u32[]{:S(2)}) collective-permute-start(bf16[16,1848]{1,0:T(8,128)(2,1)S(1)} %get-tuple-element.72), channel_id=1, source_target_pairs={{0,8},{8,0},{16,24},{24,16},{1,9},{9,1},{17,25},{25,17},{2,10},{10... | collective-permute-start | bytes 177416 | tf_op jit(solution)/shard_map/ppermute | solution.py:31
  29.2 1.7 %down.1 = (f32[64,2048]{1,0:T(8,128)}, f32[1,1]{1,0:T(1,128)}) custom-call(f32[64,128]{1,0:T(8,128)S(1)} %get-tuple-element.66.coef_ref, f32[64,64]{1,0:T(8,128)S(1)} %add_add_fusion.back_ref.own_back, bf16[64,2048]{1,0:T(8,128)(2,1)S(1)} %get-tuple-element.40.own_hidden, f32[80,128]{1,0:T(8,128)S(1)} %collective-permute-done.10.refs_0_.rest_0_, ...), custom_call_target="tpu_custom_call" | custom-call | flops 1150000000 | bytes 3600000 | tf_op jit(solution)/shard_map/down/pallas_call | solution.py:446
  31.0 0.9 %output.1 = (bf16[64,1848]{1,0:T(8,128)(2,1)}, f32[8,128]{1,0:T(8,128)S(1)}) custom-call(f32[64,1848]{1,0:T(8,128)S(1)} %get-tuple-element.46.total_ref, bf16[64,64]{1,0:T(8,128)(2,1)S(1)} %get-tuple-element.60.low_ref, bf16[64,1848]{1,0:T(8,128)(2,1)S(1)} %get-tuple-element.61.up_ref, bf16[64,1848]{1,0:T(8,128)(2,1)S(1)} %collective-permute-done.13.rest_0_, ...), custom_call_target="tpu_custom_call" | custom-call | flops 1150000000 | bytes 3600000 | tf_op jit(solution)/shard_map/output/pallas_call | solution.py:455
  31.9 1.0 %collective-permute-done.16.rest_0_ = bf16[16,1848]{1,0:T(8,128)(2,1)S(1)} collective-permute-done((bf16[16,1848]{1,0:T(8,128)(2,1)S(1)}, bf16[16,1848]{1,0:T(8,128)(2,1)S(1)}, u32[]{:S(2)}, u32[]{:S(2)}) %collective-permute-start.16) | collective-permute-done | bytes 59168 | tf_op jit(solution)/shard_map/ppermute | solution.py:31
  33.0 0.7 %gradient.1 = f32[16,1848]{1,0:T(8,128)} custom-call(f32[8,128]{1,0:T(8,128)S(1)} %get-tuple-element.68.written, f32[16,1848]{1,0:T(8,128)S(1)} %get-tuple-element.69.own_term, bf16[16,1848]{1,0:T(8,128)(2,1)S(1)} %collective-permute-done.16.rest_0_, bf16[16,1848]{1,0:T(8,128)(2,1)S(1)} %collective-permute-done.17.rest_1_, ...), custom_call_target="tpu_custom_call" | custom-call | flops 2875000064 | bytes 9000000 | tf_op jit(solution)/shard_map/gradient/pallas_call | solution.py:462
  (28 shorter events, 1.0 us)
Async XLA Ops:
  0.6 12.6 %copy-start = (bf16[2048,1848]{0,1:T(8,128)(2,1)S(1)}, bf16[2048,1848]{0,1:T(8,128)(2,1)}, u32[]{:S(2)}) copy-start(bf16[2048,1848]{0,1:T(8,128)(2,1)} %param.11) | copy-start | bytes 22708228
  2.3 10.3 %collective-permute-start = (bf16[64,1024]{1,0:T(8,128)(2,1)S(1)}, bf16[64,1024]{1,0:T(8,128)(2,1)S(1)}, u32[]{:S(2)}, u32[]{:S(2)}) collective-permute-start(bf16[64,1024]{1,0:T(8,128)(2,1)S(1)} %get-tuple-element.41), channel_id=1, source_target_pairs={{0,24},{8,16},{16,8},{24,0},{1,25},{9,17},{17,9},{25,1},{2,26},{10... | collective-permute-start | bytes 393224 | tf_op jit(solution)/shard_map/ppermute | solution.py:31
  6.3 6.3 %collective-permute-start.1 = (bf16[64,1024]{1,0:T(8,128)(2,1)S(1)}, bf16[64,1024]{1,0:T(8,128)(2,1)S(1)}, u32[]{:S(2)}, u32[]{:S(2)}) collective-permute-start(bf16[64,1024]{1,0:T(8,128)(2,1)S(1)} %get-tuple-element.42), channel_id=1, source_target_pairs={{0,16},{8,24},{16,0},{24,8},{1,17},{9,25},{17,1},{25,9},{2,18},{10... | collective-permute-start | bytes 393224 | tf_op jit(solution)/shard_map/ppermute | solution.py:31
  6.8 6.3 %collective-permute-start.2 = (bf16[64,1024]{1,0:T(8,128)(2,1)S(1)}, bf16[64,1024]{1,0:T(8,128)(2,1)S(1)}, u32[]{:S(2)}, u32[]{:S(2)}) collective-permute-start(bf16[64,1024]{1,0:T(8,128)(2,1)S(1)} %get-tuple-element.43), channel_id=1, source_target_pairs={{0,8},{8,0},{16,24},{24,16},{1,9},{9,1},{17,25},{25,17},{2,10},{10... | collective-permute-start | bytes 393224 | tf_op jit(solution)/shard_map/ppermute | solution.py:31
  6.9 1.2 %collective-permute-start.6 = (f32[64,64]{1,0:T(8,128)S(1)}, f32[64,64]{1,0:T(8,128)S(1)}, u32[]{:S(2)}, u32[]{:S(2)}) collective-permute-start(f32[64,64]{1,0:T(8,128)S(1)} %get-tuple-element.50), channel_id=1, source_target_pairs={{0,1},{1,0},{2,3},{3,2},{4,5},{5,4},{6,7},{7,6},{8,9},{9,8},{10,11... | collective-permute-start | bytes 49160 | tf_op jit(solution)/shard_map/ppermute | solution.py:31
  8.2 6.3 %collective-permute-start.8 = (f32[64,64]{1,0:T(8,128)S(1)}, f32[64,64]{1,0:T(8,128)S(1)}, u32[]{:S(2)}, u32[]{:S(2)}) collective-permute-start(f32[64,64]{1,0:T(8,128)S(1)} %add.13), channel_id=1, source_target_pairs={{0,2},{1,5},{2,0},{3,7},{4,6},{5,1},{6,4},{7,3},{8,10},{9,13},{10,... | collective-permute-start | bytes 49160 | tf_op jit(solution)/shard_map/ppermute | solution.py:36
  10.1 7.9 %collective-permute-start.7 = (f32[64,64]{1,0:T(8,128)S(1)}, f32[64,64]{1,0:T(8,128)S(1)}, u32[]{:S(2)}, u32[]{:S(2)}) collective-permute-start(f32[64,64]{1,0:T(8,128)S(1)} %add.13), channel_id=1, source_target_pairs={{0,6},{1,7},{2,4},{3,5},{4,2},{5,3},{6,0},{7,1},{8,14},{9,15},{10,... | collective-permute-start | bytes 49160 | tf_op jit(solution)/shard_map/ppermute | solution.py:31
  12.6 2.4 %collective-permute-start.3 = (bf16[64,1024]{1,0:T(8,128)(2,1)S(1)}, bf16[64,1024]{1,0:T(8,128)(2,1)S(1)}, u32[]{:S(2)}, u32[]{:S(2)}) collective-permute-start(bf16[64,1024]{1,0:T(8,128)(2,1)S(1)} %collective-permute-done.refs_0_.rest_3_), channel_id=1, source_target_pairs={{0,1},{1,0},{2,3},{3,2},{4,5},{5,4},{6,7},{7,6},{8,9},{9,8},{10,11... | collective-permute-start | bytes 393224 | tf_op jit(solution)/shard_map/ppermute | solution.py:31
  12.6 2.4 %collective-permute-start.4 = (bf16[64,1024]{1,0:T(8,128)(2,1)S(1)}, bf16[64,1024]{1,0:T(8,128)(2,1)S(1)}, u32[]{:S(2)}, u32[]{:S(2)}) collective-permute-start(bf16[64,1024]{1,0:T(8,128)(2,1)S(1)} %collective-permute-done.1.refs_1_.rest_4_), channel_id=1, source_target_pairs={{0,1},{1,0},{2,3},{3,2},{4,5},{5,4},{6,7},{7,6},{8,9},{9,8},{10,11... | collective-permute-start | bytes 393224 | tf_op jit(solution)/shard_map/ppermute | solution.py:31
  13.1 1.9 %collective-permute-start.5 = (bf16[64,1024]{1,0:T(8,128)(2,1)S(1)}, bf16[64,1024]{1,0:T(8,128)(2,1)S(1)}, u32[]{:S(2)}, u32[]{:S(2)}) collective-permute-start(bf16[64,1024]{1,0:T(8,128)(2,1)S(1)} %collective-permute-done.2.refs_2_.rest_5_), channel_id=1, source_target_pairs={{0,1},{1,0},{2,3},{3,2},{4,5},{5,4},{6,7},{7,6},{8,9},{9,8},{10,11... | collective-permute-start | bytes 393224 | tf_op jit(solution)/shard_map/ppermute | solution.py:31
  14.5 3.6 %collective-permute-start.9 = (f32[64,64]{1,0:T(8,128)S(1)}, f32[64,64]{1,0:T(8,128)S(1)}, u32[]{:S(2)}, u32[]{:S(2)}) collective-permute-start(f32[64,64]{1,0:T(8,128)S(1)} %collective-permute-done.8), channel_id=1, source_target_pairs={{0,1},{1,0},{2,3},{3,2},{4,5},{5,4},{6,7},{7,6},{8,9},{9,8},{10,11... | collective-permute-start | bytes 49160 | tf_op jit(solution)/shard_map/ppermute | solution.py:31
  16.5 6.8 %collective-permute-start.14 = (bf16[64,1848]{1,0:T(8,128)(2,1)S(1)}, bf16[64,1848]{1,0:T(8,128)(2,1)S(1)}, u32[]{:S(2)}, u32[]{:S(2)}) collective-permute-start(bf16[64,1848]{1,0:T(8,128)(2,1)S(1)} %get-tuple-element.64), channel_id=1, source_target_pairs={{0,8},{1,17},{2,10},{3,19},{4,12},{5,21},{6,14},{7,23},{8,0},{9,25... | collective-permute-start | bytes 709640 | tf_op jit(solution)/shard_map/ppermute | solution.py:41
  18.2 7.1 %collective-permute-start.10 = (f32[80,128]{1,0:T(8,128)S(1)}, f32[80,128]{1,0:T(8,128)S(1)}, u32[]{:S(2)}, u32[]{:S(2)}) collective-permute-start(f32[80,128]{1,0:T(8,128)S(1)} %get-tuple-element.57), channel_id=1, source_target_pairs={{0,24},{8,16},{16,8},{24,0},{1,25},{9,17},{17,9},{25,1},{2,26},{10... | collective-permute-start | bytes 122888 | tf_op jit(solution)/shard_map/ppermute | solution.py:31
  19.7 5.6 %collective-permute-start.11 = (f32[80,128]{1,0:T(8,128)S(1)}, f32[80,128]{1,0:T(8,128)S(1)}, u32[]{:S(2)}, u32[]{:S(2)}) collective-permute-start(f32[80,128]{1,0:T(8,128)S(1)} %get-tuple-element.58), channel_id=1, source_target_pairs={{0,16},{8,24},{16,0},{24,8},{1,17},{9,25},{17,1},{25,9},{2,18},{10... | collective-permute-start | bytes 122888 | tf_op jit(solution)/shard_map/ppermute | solution.py:31
  20.2 5.1 %collective-permute-start.12 = (f32[80,128]{1,0:T(8,128)S(1)}, f32[80,128]{1,0:T(8,128)S(1)}, u32[]{:S(2)}, u32[]{:S(2)}) collective-permute-start(f32[80,128]{1,0:T(8,128)S(1)} %get-tuple-element.59), channel_id=1, source_target_pairs={{0,8},{8,0},{16,24},{24,16},{1,9},{9,1},{17,25},{25,17},{2,10},{10... | collective-permute-start | bytes 122888 | tf_op jit(solution)/shard_map/ppermute | solution.py:31
  21.7 9.2 %collective-permute-start.13 = (bf16[64,1848]{1,0:T(8,128)(2,1)S(1)}, bf16[64,1848]{1,0:T(8,128)(2,1)S(1)}, u32[]{:S(2)}, u32[]{:S(2)}) collective-permute-start(bf16[64,1848]{1,0:T(8,128)(2,1)S(1)} %get-tuple-element.62), channel_id=1, source_target_pairs={{0,8},{1,17},{2,10},{3,19},{4,12},{5,21},{6,14},{7,23},{8,0},{9,25... | collective-permute-start | bytes 709640 | tf_op jit(solution)/shard_map/ppermute | solution.py:41
  23.4 7.6 %collective-permute-start.15 = (bf16[64,1848]{1,0:T(8,128)(2,1)S(1)}, bf16[64,1848]{1,0:T(8,128)(2,1)S(1)}, u32[]{:S(2)}, u32[]{:S(2)}) collective-permute-start(bf16[64,1848]{1,0:T(8,128)(2,1)S(1)} %add.20), channel_id=1, source_target_pairs={{0,16},{1,9},{2,18},{3,11},{4,20},{5,13},{6,22},{7,15},{8,24},{9,1... | collective-permute-start | bytes 709640 | tf_op jit(solution)/shard_map/ppermute | solution.py:41
  25.7 7.2 %collective-permute-start.16 = (bf16[16,1848]{1,0:T(8,128)(2,1)S(1)}, bf16[16,1848]{1,0:T(8,128)(2,1)S(1)}, u32[]{:S(2)}, u32[]{:S(2)}) collective-permute-start(bf16[16,1848]{1,0:T(8,128)(2,1)S(1)} %get-tuple-element.70), channel_id=1, source_target_pairs={{0,24},{8,16},{16,8},{24,0},{1,25},{9,17},{17,9},{25,1},{2,26},{10... | collective-permute-start | bytes 177416 | tf_op jit(solution)/shard_map/ppermute | solution.py:31
  27.4 5.5 %collective-permute-start.17 = (bf16[16,1848]{1,0:T(8,128)(2,1)S(1)}, bf16[16,1848]{1,0:T(8,128)(2,1)S(1)}, u32[]{:S(2)}, u32[]{:S(2)}) collective-permute-start(bf16[16,1848]{1,0:T(8,128)(2,1)S(1)} %get-tuple-element.71), channel_id=1, source_target_pairs={{0,16},{8,24},{16,0},{24,8},{1,17},{9,25},{17,1},{25,9},{2,18},{10... | collective-permute-start | bytes 177416 | tf_op jit(solution)/shard_map/ppermute | solution.py:31
  28.7 4.3 %collective-permute-start.18 = (bf16[16,1848]{1,0:T(8,128)(2,1)S(1)}, bf16[16,1848]{1,0:T(8,128)(2,1)S(1)}, u32[]{:S(2)}, u32[]{:S(2)}) collective-permute-start(bf16[16,1848]{1,0:T(8,128)(2,1)S(1)} %get-tuple-element.72), channel_id=1, source_target_pairs={{0,8},{8,0},{16,24},{24,16},{1,9},{9,1},{17,25},{25,17},{2,10},{10... | collective-permute-start | bytes 177416 | tf_op jit(solution)/shard_map/ppermute | solution.py:31

commit v9 on v8

--- a/solution.py
+++ b/solution.py
@@ -191,8 +191,8 @@
         parts = [result[i * tokens : (i + 1) * tokens] for i in range(groups)]
         kept[:, start:end] = parts[0]
         far[:, start:end] = parts[-1].astype(BF16)
-        early[:, start:end] = jnp.where(core == 0, parts[1], parts[-2]).astype(BF16)
-        late[:, start:end] = jnp.where(core == 0, parts[-2], parts[1])
+        early[:, start:end] = jnp.where(core == 0, parts[-2], parts[1]).astype(BF16)
+        late[:, start:end] = jnp.where(core == 0, parts[1], parts[-2])
         for ref, part in zip(nears, parts[2:-2]):
             ref[:, start:end] = part.astype(BF16)
 
@@ -413,7 +413,7 @@
     own_low, *lows = terms[groups - 4 :]
     back = sum_over_fsdp(back, at, held_lows, own_low)
     came = [swap(term, "group", d) for d, term in enumerate(terms[: groups - 4], 2)]
-    ways = (1, far ^ 1)
+    ways = (far ^ 1, 1)
     far_term = swap_pair(far_term, ways)
     letters = call(
         letter_kernel,

time: 33.8 us -> 33.5 us (level)
  starting transfers between devices: 21.3 us -> 20.9 us
    ppermute x3, waiting for transfers between devices: 1.04 us -> 1.83 us  [swap_pair(): lax.ppermute(array, ('group', 'fsdp'), [(g * size + f, (g ^ partner[f % 2...]
    ppermute x15, waiting for transfers between devices: 1.21 us -> 0.53 us  [swap(): return lax.ppermute(array, axis, [(i, i ^ distance) for i in range(size)])]
    ppermute x3, starting transfers between devices: 4.02 us -> 3.64 us  [swap_pair(): lax.ppermute(array, ('group', 'fsdp'), [(g * size + f, (g ^ partner[f % 2...]
  transfers between devices with their start and end apart: 19 -> 19, of which waited for: 4 -> 3; matrix products, arithmetic and copies ran while one was open for 0% -> 0% of each run, Pallas kernels for 21% -> 21%
where the time goes in v9:
time: 33.5 us; the launch traced here: 33.4 us
  starting transfers between devices  20.9 us (62%)
  Pallas kernels  9.36 us (28%)
  waiting for transfers between devices  2.36 us (7%)
  between operations  0.75 us (2%)
    ppermute x15, starting transfers between devices, swap(): return lax.ppermute(array, axis, [(i, i ^ distance) for i in range(size)])  15.3 us
    ppermute x3, starting transfers between devices, swap_pair(): lax.ppermute(array, ('group', 'fsdp'), [(g * size + f, (g ^ partner[f % 2...  3.64 us
    ppermute x1, starting transfers between devices, swap_cores(): lax.ppermute(array, axis, [(i, i ^ partner[i % 2]) for i in range(size)])  1.97 us
    ppermute x3, waiting for transfers between devices, swap_pair(): lax.ppermute(array, ('group', 'fsdp'), [(g * size + f, (g ^ partner[f % 2...  1.83 us
    pallas_call x1, Pallas kernels, on_device(): call(functools.partial(down_kernel, groups, length), 'down', 1.0, [jax.Sh...  1.72 us
    pallas_call x1, Pallas kernels, on_device(): call(functools.partial(pack_kernel, groups, depth), 'pack', 1.8, [pltpu.V...  1.68 us
    pallas_call x1, Pallas kernels, on_device(): call(functools.partial(second_kernel, groups), 'second', 1.5, [pltpu.VMEM...  1.48 us
    pallas_call x1, Pallas kernels, on_device(): call(first_kernel, 'first', 1.5, [pltpu.VMEM((units, groups * tokens), F3...  1.29 us
  transfers between devices with their start and end apart: 19, of which 3 were waited for; matrix products, arithmetic and copies ran while one was open for 0% of the time, Pallas kernels for 21%

profile of v9, /device:TPU:0, one launch (start us, length us, event | category | flops | bytes accessed | tf_op | source)
XLA Modules:
  0.0 33.4 jit_solution(9144473925470816527)
XLA Ops:
  0.6 1.7 %pack.1 = (bf16[64,1024]{1,0:T(8,128)(2,1)S(1)}, bf16[64,1024]{1,0:T(8,128)(2,1)S(1)}, bf16[64,1024]{1,0:T(8,128)(2,1)S(1)}, f32[16,128]{1,0:T(8,128)S(1)}, bf16...) custom-call(bf16[64,8192]{1,0:T(8,128)(2,1)} %hidden_ref.3, f32[1,4,16]{2,1,0:T(4,128)} %old_hbm.1, ...), custom_call_target="tpu_custom_call" | custom-call | flops 2070000000 | bytes 6480000 | tf_op jit(solution)/shard_map/pack/pallas_call | solution.py:344
  2.3 4.0 %collective-permute-start = (bf16[64,1024]{1,0:T(8,128)(2,1)S(1)}, bf16[64,1024]{1,0:T(8,128)(2,1)S(1)}, u32[]{:S(2)}, u32[]{:S(2)}) collective-permute-start(bf16[64,1024]{1,0:T(8,128)(2,1)S(1)} %get-tuple-element.41), channel_id=1, source_target_pairs={{0,24},{8,16},{16,8},{24,0},{1,25},{9,17},{17,9},{25,1},{2,26},{10... | collective-permute-start | bytes 393224 | tf_op jit(solution)/shard_map/ppermute | solution.py:31
  6.3 0.5 %collective-permute-start.1 = (bf16[64,1024]{1,0:T(8,128)(2,1)S(1)}, bf16[64,1024]{1,0:T(8,128)(2,1)S(1)}, u32[]{:S(2)}, u32[]{:S(2)}) collective-permute-start(bf16[64,1024]{1,0:T(8,128)(2,1)S(1)} %get-tuple-element.42), channel_id=1, source_target_pairs={{0,16},{8,24},{16,0},{24,8},{1,17},{9,25},{17,1},{25,9},{2,18},{10... | collective-permute-start | bytes 393224 | tf_op jit(solution)/shard_map/ppermute | solution.py:31
  6.9 1.0 %load.1 = (bf16[64,2048]{1,0:T(8,128)(2,1)S(1)}, bf16[64,2048]{1,0:T(8,128)(2,1)S(1)}) custom-call(bf16[64,8192]{1,0:T(8,128)(2,1)} %hidden_ref.3, bf16[64,2048]{1,0:T(8,128)(2,1)} %bitcast.6), custom_call_target="tpu_custom_call" | custom-call | flops 1150000000 | bytes 3600000 | tf_op jit(solution)/shard_map/load/pallas_call | solution.py:381
  8.2 2.0 %collective-permute-start.8 = (f32[64,64]{1,0:T(8,128)S(1)}, f32[64,64]{1,0:T(8,128)S(1)}, u32[]{:S(2)}, u32[]{:S(2)}) collective-permute-start(f32[64,64]{1,0:T(8,128)S(1)} %add.13), channel_id=1, source_target_pairs={{0,2},{1,5},{2,0},{3,7},{4,6},{5,1},{6,4},{7,3},{8,10},{9,13},{10,... | collective-permute-start | bytes 49160 | tf_op jit(solution)/shard_map/ppermute | solution.py:36
  10.1 2.5 %collective-permute-start.7 = (f32[64,64]{1,0:T(8,128)S(1)}, f32[64,64]{1,0:T(8,128)S(1)}, u32[]{:S(2)}, u32[]{:S(2)}) collective-permute-start(f32[64,64]{1,0:T(8,128)S(1)} %add.13), channel_id=1, source_target_pairs={{0,6},{1,7},{2,4},{3,5},{4,2},{5,3},{6,0},{7,1},{8,14},{9,15},{10,... | collective-permute-start | bytes 49160 | tf_op jit(solution)/shard_map/ppermute | solution.py:31
  12.6 0.5 %collective-permute-start.4 = (bf16[64,1024]{1,0:T(8,128)(2,1)S(1)}, bf16[64,1024]{1,0:T(8,128)(2,1)S(1)}, u32[]{:S(2)}, u32[]{:S(2)}) collective-permute-start(bf16[64,1024]{1,0:T(8,128)(2,1)S(1)} %collective-permute-done.1.refs_1_.rest_4_), channel_id=1, source_target_pairs={{0,1},{1,0},{2,3},{3,2},{4,5},{5,4},{6,7},{7,6},{8,9},{9,8},{10,11... | collective-permute-start | bytes 393224 | tf_op jit(solution)/shard_map/ppermute | solution.py:31
  13.2 1.3 %first.1 = (f32[1848,256]{1,0:T(8,128)S(1)}, f32[256,64]{1,0:T(8,128)S(1)}) custom-call(bf16[1848,2048]{1,0:T(8,128)(2,1)S(1)} %bitcast.4, bf16[64,2048]{1,0:T(8,128)(2,1)S(1)} %get-tuple-element.39.at_ref, bf16[64,2048]{1,0:T(8,128)(2,1)S(1)} %get-tuple-element.40.own_hidden, bf16[64,1024]{1,0:T(8,128)(2,1)S(1)} %collective-permute-done.refs_0_.rest_3_, ...), custom_call_target="tpu_custom_call" | custom-call | flops 1724999936 | bytes 5400000 | tf_op jit(solution)/shard_map/first/pallas_call | solution.py:391
  14.5 0.5 %collective-permute-start.9 = (f32[64,64]{1,0:T(8,128)S(1)}, f32[64,64]{1,0:T(8,128)S(1)}, u32[]{:S(2)}, u32[]{:S(2)}) collective-permute-start(f32[64,64]{1,0:T(8,128)S(1)} %collective-permute-done.8), channel_id=1, source_target_pairs={{0,1},{1,0},{2,3},{3,2},{4,5},{5,4},{6,7},{7,6},{8,9},{9,8},{10,11... | collective-permute-start | bytes 49160 | tf_op jit(solution)/shard_map/ppermute | solution.py:31
  15.0 1.5 %second.1 = (bf16[64,1848]{1,0:T(8,128)(2,1)S(1)}, bf16[64,1848]{1,0:T(8,128)(2,1)S(1)}, f32[64,1848]{1,0:T(8,128)S(1)}, f32[64,1848]{1,0:T(8,128)S(1)}, f32[64,...) custom-call(bf16[1848,2048]{1,0:T(8,128)(2,1)S(1)} %bitcast.5, ...), custom_call_target="tpu_custom_call" | custom-call | flops 1724999936 | bytes 5400000 | tf_op jit(solution)/shard_map/second/pallas_call | solution.py:399
  16.5 1.6 %collective-permute-start.14 = (bf16[64,1848]{1,0:T(8,128)(2,1)S(1)}, bf16[64,1848]{1,0:T(8,128)(2,1)S(1)}, u32[]{:S(2)}, u32[]{:S(2)}) collective-permute-start(bf16[64,1848]{1,0:T(8,128)(2,1)S(1)} %get-tuple-element.64), channel_id=1, source_target_pairs={{0,16},{1,9},{2,18},{3,11},{4,20},{5,13},{6,22},{7,15},{8,24},{9,1... | collective-permute-start | bytes 709640 | tf_op jit(solution)/shard_map/ppermute | solution.py:41
  18.2 1.5 %collective-permute-start.10 = (f32[80,128]{1,0:T(8,128)S(1)}, f32[80,128]{1,0:T(8,128)S(1)}, u32[]{:S(2)}, u32[]{:S(2)}) collective-permute-start(f32[80,128]{1,0:T(8,128)S(1)} %get-tuple-element.57), channel_id=1, source_target_pairs={{0,24},{8,16},{16,8},{24,0},{1,25},{9,17},{17,9},{25,1},{2,26},{10... | collective-permute-start | bytes 122888 | tf_op jit(solution)/shard_map/ppermute | solution.py:31
  19.7 1.5 %collective-permute-start.11 = (f32[80,128]{1,0:T(8,128)S(1)}, f32[80,128]{1,0:T(8,128)S(1)}, u32[]{:S(2)}, u32[]{:S(2)}) collective-permute-start(f32[80,128]{1,0:T(8,128)S(1)} %get-tuple-element.58), channel_id=1, source_target_pairs={{0,16},{8,24},{16,0},{24,8},{1,17},{9,25},{17,1},{25,9},{2,18},{10... | collective-permute-start | bytes 122888 | tf_op jit(solution)/shard_map/ppermute | solution.py:31
  21.2 0.5 %collective-permute-start.12 = (f32[80,128]{1,0:T(8,128)S(1)}, f32[80,128]{1,0:T(8,128)S(1)}, u32[]{:S(2)}, u32[]{:S(2)}) collective-permute-start(f32[80,128]{1,0:T(8,128)S(1)} %get-tuple-element.59), channel_id=1, source_target_pairs={{0,8},{8,0},{16,24},{24,16},{1,9},{9,1},{17,25},{25,17},{2,10},{10... | collective-permute-start | bytes 122888 | tf_op jit(solution)/shard_map/ppermute | solution.py:31
  21.8 0.5 %collective-permute-start.13 = (bf16[64,1848]{1,0:T(8,128)(2,1)S(1)}, bf16[64,1848]{1,0:T(8,128)(2,1)S(1)}, u32[]{:S(2)}, u32[]{:S(2)}) collective-permute-start(bf16[64,1848]{1,0:T(8,128)(2,1)S(1)} %get-tuple-element.62), channel_id=1, source_target_pairs={{0,16},{1,9},{2,18},{3,11},{4,20},{5,13},{6,22},{7,15},{8,24},{9,1... | collective-permute-start | bytes 709640 | tf_op jit(solution)/shard_map/ppermute | solution.py:41
  22.3 1.8 %collective-permute-done.14.came = bf16[64,1848]{1,0:T(8,128)(2,1)S(1)} collective-permute-done((bf16[64,1848]{1,0:T(8,128)(2,1)S(1)}, bf16[64,1848]{1,0:T(8,128)(2,1)S(1)}, u32[]{:S(2)}, u32[]{:S(2)}) %collective-permute-start.14) | collective-permute-done | bytes 236576 | tf_op jit(solution)/shard_map/ppermute | solution.py:41
  24.2 1.6 %collective-permute-start.15 = (bf16[64,1848]{1,0:T(8,128)(2,1)S(1)}, bf16[64,1848]{1,0:T(8,128)(2,1)S(1)}, u32[]{:S(2)}, u32[]{:S(2)}) collective-permute-start(bf16[64,1848]{1,0:T(8,128)(2,1)S(1)} %add.20), channel_id=1, source_target_pairs={{0,8},{1,17},{2,10},{3,19},{4,12},{5,21},{6,14},{7,23},{8,0},{9,25... | collective-permute-start | bytes 709640 | tf_op jit(solution)/shard_map/ppermute | solution.py:41
  25.7 0.4 %adapter.1 = (bf16[16,1848]{1,0:T(8,128)(2,1)S(1)}, bf16[16,1848]{1,0:T(8,128)(2,1)S(1)}, bf16[16,1848]{1,0:T(8,128)(2,1)S(1)}, f32[16,1848]{1,0:T(8,128)S(1)}, ...) custom-call(f32[64,64]{1,0:T(8,128)S(1)} %get-tuple-element.47.own_low, ...), custom_call_target="tpu_custom_call" | custom-call | flops 1150000000 | bytes 3600000 | tf_op jit(solution)/shard_map/adapter/pallas_call | solution.py:432
  26.1 1.6 %collective-permute-start.16 = (bf16[16,1848]{1,0:T(8,128)(2,1)S(1)}, bf16[16,1848]{1,0:T(8,128)(2,1)S(1)}, u32[]{:S(2)}, u32[]{:S(2)}) collective-permute-start(bf16[16,1848]{1,0:T(8,128)(2,1)S(1)} %get-tuple-element.70), channel_id=1, source_target_pairs={{0,24},{8,16},{16,8},{24,0},{1,25},{9,17},{17,9},{25,1},{2,26},{10... | collective-permute-start | bytes 177416 | tf_op jit(solution)/shard_map/ppermute | solution.py:31
  27.7 0.5 %collective-permute-start.17 = (bf16[16,1848]{1,0:T(8,128)(2,1)S(1)}, bf16[16,1848]{1,0:T(8,128)(2,1)S(1)}, u32[]{:S(2)}, u32[]{:S(2)}) collective-permute-start(bf16[16,1848]{1,0:T(8,128)(2,1)S(1)} %get-tuple-element.71), channel_id=1, source_target_pairs={{0,16},{8,24},{16,0},{24,8},{1,17},{9,25},{17,1},{25,9},{2,18},{10... | collective-permute-start | bytes 177416 | tf_op jit(solution)/shard_map/ppermute | solution.py:31
  28.2 1.5 %collective-permute-start.18 = (bf16[16,1848]{1,0:T(8,128)(2,1)S(1)}, bf16[16,1848]{1,0:T(8,128)(2,1)S(1)}, u32[]{:S(2)}, u32[]{:S(2)}) collective-permute-start(bf16[16,1848]{1,0:T(8,128)(2,1)S(1)} %get-tuple-element.72), channel_id=1, source_target_pairs={{0,8},{8,0},{16,24},{24,16},{1,9},{9,1},{17,25},{25,17},{2,10},{10... | collective-permute-start | bytes 177416 | tf_op jit(solution)/shard_map/ppermute | solution.py:31
  29.6 1.7 %down.1 = (f32[64,2048]{1,0:T(8,128)}, f32[1,1]{1,0:T(1,128)}) custom-call(f32[64,128]{1,0:T(8,128)S(1)} %get-tuple-element.66.coef_ref, f32[64,64]{1,0:T(8,128)S(1)} %add_add_fusion.back_ref.own_back, bf16[64,2048]{1,0:T(8,128)(2,1)S(1)} %get-tuple-element.40.own_hidden, f32[80,128]{1,0:T(8,128)S(1)} %collective-permute-done.10.refs_0_.rest_0_, ...), custom_call_target="tpu_custom_call" | custom-call | flops 1150000000 | bytes 3600000 | tf_op jit(solution)/shard_map/down/pallas_call | solution.py:446
  31.4 0.9 %output.1 = (bf16[64,1848]{1,0:T(8,128)(2,1)}, f32[8,128]{1,0:T(8,128)S(1)}) custom-call(f32[64,1848]{1,0:T(8,128)S(1)} %get-tuple-element.46.total_ref, bf16[64,64]{1,0:T(8,128)(2,1)S(1)} %get-tuple-element.60.low_ref, bf16[64,1848]{1,0:T(8,128)(2,1)S(1)} %get-tuple-element.61.up_ref, bf16[64,1848]{1,0:T(8,128)(2,1)S(1)} %collective-permute-done.13.rest_0_, ...), custom_call_target="tpu_custom_call" | custom-call | flops 1150000000 | bytes 3600000 | tf_op jit(solution)/shard_map/output/pallas_call | solution.py:455
  32.7 0.7 %gradient.1 = f32[16,1848]{1,0:T(8,128)} custom-call(f32[8,128]{1,0:T(8,128)S(1)} %get-tuple-element.68.written, f32[16,1848]{1,0:T(8,128)S(1)} %get-tuple-element.69.own_term, bf16[16,1848]{1,0:T(8,128)(2,1)S(1)} %collective-permute-done.16.rest_0_, bf16[16,1848]{1,0:T(8,128)(2,1)S(1)} %collective-permute-done.17.rest_1_, ...), custom_call_target="tpu_custom_call" | custom-call | flops 2875000064 | bytes 9000000 | tf_op jit(solution)/shard_map/gradient/pallas_call | solution.py:462
  (28 shorter events, 0.9 us)
Async XLA Ops:
  0.6 12.6 %copy-start = (bf16[2048,1848]{0,1:T(8,128)(2,1)S(1)}, bf16[2048,1848]{0,1:T(8,128)(2,1)}, u32[]{:S(2)}) copy-start(bf16[2048,1848]{0,1:T(8,128)(2,1)} %param.11) | copy-start | bytes 22708228
  2.3 10.3 %collective-permute-start = (bf16[64,1024]{1,0:T(8,128)(2,1)S(1)}, bf16[64,1024]{1,0:T(8,128)(2,1)S(1)}, u32[]{:S(2)}, u32[]{:S(2)}) collective-permute-start(bf16[64,1024]{1,0:T(8,128)(2,1)S(1)} %get-tuple-element.41), channel_id=1, source_target_pairs={{0,24},{8,16},{16,8},{24,0},{1,25},{9,17},{17,9},{25,1},{2,26},{10... | collective-permute-start | bytes 393224 | tf_op jit(solution)/shard_map/ppermute | solution.py:31
  6.3 6.3 %collective-permute-start.1 = (bf16[64,1024]{1,0:T(8,128)(2,1)S(1)}, bf16[64,1024]{1,0:T(8,128)(2,1)S(1)}, u32[]{:S(2)}, u32[]{:S(2)}) collective-permute-start(bf16[64,1024]{1,0:T(8,128)(2,1)S(1)} %get-tuple-element.42), channel_id=1, source_target_pairs={{0,16},{8,24},{16,0},{24,8},{1,17},{9,25},{17,1},{25,9},{2,18},{10... | collective-permute-start | bytes 393224 | tf_op jit(solution)/shard_map/ppermute | solution.py:31
  6.8 6.3 %collective-permute-start.2 = (bf16[64,1024]{1,0:T(8,128)(2,1)S(1)}, bf16[64,1024]{1,0:T(8,128)(2,1)S(1)}, u32[]{:S(2)}, u32[]{:S(2)}) collective-permute-start(bf16[64,1024]{1,0:T(8,128)(2,1)S(1)} %get-tuple-element.43), channel_id=1, source_target_pairs={{0,8},{8,0},{16,24},{24,16},{1,9},{9,1},{17,25},{25,17},{2,10},{10... | collective-permute-start | bytes 393224 | tf_op jit(solution)/shard_map/ppermute | solution.py:31
  6.9 1.2 %collective-permute-start.6 = (f32[64,64]{1,0:T(8,128)S(1)}, f32[64,64]{1,0:T(8,128)S(1)}, u32[]{:S(2)}, u32[]{:S(2)}) collective-permute-start(f32[64,64]{1,0:T(8,128)S(1)} %get-tuple-element.50), channel_id=1, source_target_pairs={{0,1},{1,0},{2,3},{3,2},{4,5},{5,4},{6,7},{7,6},{8,9},{9,8},{10,11... | collective-permute-start | bytes 49160 | tf_op jit(solution)/shard_map/ppermute | solution.py:31
  8.2 6.3 %collective-permute-start.8 = (f32[64,64]{1,0:T(8,128)S(1)}, f32[64,64]{1,0:T(8,128)S(1)}, u32[]{:S(2)}, u32[]{:S(2)}) collective-permute-start(f32[64,64]{1,0:T(8,128)S(1)} %add.13), channel_id=1, source_target_pairs={{0,2},{1,5},{2,0},{3,7},{4,6},{5,1},{6,4},{7,3},{8,10},{9,13},{10,... | collective-permute-start | bytes 49160 | tf_op jit(solution)/shard_map/ppermute | solution.py:36
  10.1 8.0 %collective-permute-start.7 = (f32[64,64]{1,0:T(8,128)S(1)}, f32[64,64]{1,0:T(8,128)S(1)}, u32[]{:S(2)}, u32[]{:S(2)}) collective-permute-start(f32[64,64]{1,0:T(8,128)S(1)} %add.13), channel_id=1, source_target_pairs={{0,6},{1,7},{2,4},{3,5},{4,2},{5,3},{6,0},{7,1},{8,14},{9,15},{10,... | collective-permute-start | bytes 49160 | tf_op jit(solution)/shard_map/ppermute | solution.py:31
  12.6 2.4 %collective-permute-start.3 = (bf16[64,1024]{1,0:T(8,128)(2,1)S(1)}, bf16[64,1024]{1,0:T(8,128)(2,1)S(1)}, u32[]{:S(2)}, u32[]{:S(2)}) collective-permute-start(bf16[64,1024]{1,0:T(8,128)(2,1)S(1)} %collective-permute-done.refs_0_.rest_3_), channel_id=1, source_target_pairs={{0,1},{1,0},{2,3},{3,2},{4,5},{5,4},{6,7},{7,6},{8,9},{9,8},{10,11... | collective-permute-start | bytes 393224 | tf_op jit(solution)/shard_map/ppermute | solution.py:31
  12.6 2.4 %collective-permute-start.4 = (bf16[64,1024]{1,0:T(8,128)(2,1)S(1)}, bf16[64,1024]{1,0:T(8,128)(2,1)S(1)}, u32[]{:S(2)}, u32[]{:S(2)}) collective-permute-start(bf16[64,1024]{1,0:T(8,128)(2,1)S(1)} %collective-permute-done.1.refs_1_.rest_4_), channel_id=1, source_target_pairs={{0,1},{1,0},{2,3},{3,2},{4,5},{5,4},{6,7},{7,6},{8,9},{9,8},{10,11... | collective-permute-start | bytes 393224 | tf_op jit(solution)/shard_map/ppermute | solution.py:31
  13.1 1.9 %collective-permute-start.5 = (bf16[64,1024]{1,0:T(8,128)(2,1)S(1)}, bf16[64,1024]{1,0:T(8,128)(2,1)S(1)}, u32[]{:S(2)}, u32[]{:S(2)}) collective-permute-start(bf16[64,1024]{1,0:T(8,128)(2,1)S(1)} %collective-permute-done.2.refs_2_.rest_5_), channel_id=1, source_target_pairs={{0,1},{1,0},{2,3},{3,2},{4,5},{5,4},{6,7},{7,6},{8,9},{9,8},{10,11... | collective-permute-start | bytes 393224 | tf_op jit(solution)/shard_map/ppermute | solution.py:31
  14.5 3.6 %collective-permute-start.9 = (f32[64,64]{1,0:T(8,128)S(1)}, f32[64,64]{1,0:T(8,128)S(1)}, u32[]{:S(2)}, u32[]{:S(2)}) collective-permute-start(f32[64,64]{1,0:T(8,128)S(1)} %collective-permute-done.8), channel_id=1, source_target_pairs={{0,1},{1,0},{2,3},{3,2},{4,5},{5,4},{6,7},{7,6},{8,9},{9,8},{10,11... | collective-permute-start | bytes 49160 | tf_op jit(solution)/shard_map/ppermute | solution.py:31
  16.5 7.6 %collective-permute-start.14 = (bf16[64,1848]{1,0:T(8,128)(2,1)S(1)}, bf16[64,1848]{1,0:T(8,128)(2,1)S(1)}, u32[]{:S(2)}, u32[]{:S(2)}) collective-permute-start(bf16[64,1848]{1,0:T(8,128)(2,1)S(1)} %get-tuple-element.64), channel_id=1, source_target_pairs={{0,16},{1,9},{2,18},{3,11},{4,20},{5,13},{6,22},{7,15},{8,24},{9,1... | collective-permute-start | bytes 709640 | tf_op jit(solution)/shard_map/ppermute | solution.py:41
  18.2 7.5 %collective-permute-start.10 = (f32[80,128]{1,0:T(8,128)S(1)}, f32[80,128]{1,0:T(8,128)S(1)}, u32[]{:S(2)}, u32[]{:S(2)}) collective-permute-start(f32[80,128]{1,0:T(8,128)S(1)} %get-tuple-element.57), channel_id=1, source_target_pairs={{0,24},{8,16},{16,8},{24,0},{1,25},{9,17},{17,9},{25,1},{2,26},{10... | collective-permute-start | bytes 122888 | tf_op jit(solution)/shard_map/ppermute | solution.py:31
  19.7 6.0 %collective-permute-start.11 = (f32[80,128]{1,0:T(8,128)S(1)}, f32[80,128]{1,0:T(8,128)S(1)}, u32[]{:S(2)}, u32[]{:S(2)}) collective-permute-start(f32[80,128]{1,0:T(8,128)S(1)} %get-tuple-element.58), channel_id=1, source_target_pairs={{0,16},{8,24},{16,0},{24,8},{1,17},{9,25},{17,1},{25,9},{2,18},{10... | collective-permute-start | bytes 122888 | tf_op jit(solution)/shard_map/ppermute | solution.py:31
  21.2 4.5 %collective-permute-start.12 = (f32[80,128]{1,0:T(8,128)S(1)}, f32[80,128]{1,0:T(8,128)S(1)}, u32[]{:S(2)}, u32[]{:S(2)}) collective-permute-start(f32[80,128]{1,0:T(8,128)S(1)} %get-tuple-element.59), channel_id=1, source_target_pairs={{0,8},{8,0},{16,24},{24,16},{1,9},{9,1},{17,25},{25,17},{2,10},{10... | collective-permute-start | bytes 122888 | tf_op jit(solution)/shard_map/ppermute | solution.py:31
  21.8 9.6 %collective-permute-start.13 = (bf16[64,1848]{1,0:T(8,128)(2,1)S(1)}, bf16[64,1848]{1,0:T(8,128)(2,1)S(1)}, u32[]{:S(2)}, u32[]{:S(2)}) collective-permute-start(bf16[64,1848]{1,0:T(8,128)(2,1)S(1)} %get-tuple-element.62), channel_id=1, source_target_pairs={{0,16},{1,9},{2,18},{3,11},{4,20},{5,13},{6,22},{7,15},{8,24},{9,1... | collective-permute-start | bytes 709640 | tf_op jit(solution)/shard_map/ppermute | solution.py:41
  24.2 7.2 %collective-permute-start.15 = (bf16[64,1848]{1,0:T(8,128)(2,1)S(1)}, bf16[64,1848]{1,0:T(8,128)(2,1)S(1)}, u32[]{:S(2)}, u32[]{:S(2)}) collective-permute-start(bf16[64,1848]{1,0:T(8,128)(2,1)S(1)} %add.20), channel_id=1, source_target_pairs={{0,8},{1,17},{2,10},{3,19},{4,12},{5,21},{6,14},{7,23},{8,0},{9,25... | collective-permute-start | bytes 709640 | tf_op jit(solution)/shard_map/ppermute | solution.py:41
  26.1 6.6 %collective-permute-start.16 = (bf16[16,1848]{1,0:T(8,128)(2,1)S(1)}, bf16[16,1848]{1,0:T(8,128)(2,1)S(1)}, u32[]{:S(2)}, u32[]{:S(2)}) collective-permute-start(bf16[16,1848]{1,0:T(8,128)(2,1)S(1)} %get-tuple-element.70), channel_id=1, source_target_pairs={{0,24},{8,16},{16,8},{24,0},{1,25},{9,17},{17,9},{25,1},{2,26},{10... | collective-permute-start | bytes 177416 | tf_op jit(solution)/shard_map/ppermute | solution.py:31
  27.7 5.0 %collective-permute-start.17 = (bf16[16,1848]{1,0:T(8,128)(2,1)S(1)}, bf16[16,1848]{1,0:T(8,128)(2,1)S(1)}, u32[]{:S(2)}, u32[]{:S(2)}) collective-permute-start(bf16[16,1848]{1,0:T(8,128)(2,1)S(1)} %get-tuple-element.71), channel_id=1, source_target_pairs={{0,16},{8,24},{16,0},{24,8},{1,17},{9,25},{17,1},{25,9},{2,18},{10... | collective-permute-start | bytes 177416 | tf_op jit(solution)/shard_map/ppermute | solution.py:31
  28.2 4.5 %collective-permute-start.18 = (bf16[16,1848]{1,0:T(8,128)(2,1)S(1)}, bf16[16,1848]{1,0:T(8,128)(2,1)S(1)}, u32[]{:S(2)}, u32[]{:S(2)}) collective-permute-start(bf16[16,1848]{1,0:T(8,128)(2,1)S(1)} %get-tuple-element.72), channel_id=1, source_target_pairs={{0,8},{8,0},{16,24},{24,16},{1,9},{9,1},{17,25},{25,17},{2,10},{10... | collective-permute-start | bytes 177416 | tf_op jit(solution)/shard_map/ppermute | solution.py:31
